TPU v7x, 512 devices: a whole 4x4x16 slice. The times are simulated.
512 devices in a mesh: lat: 16 (over z_hi, x), lon: 32 (over z_lo, y, core).
Axes of the slice: x: 4, y: 4, z: 16 (z_hi: 4, z_lo: 4; z = z_hi * 4 + z_lo), core: 2. Of those that a mesh axis runs over, the one named last changes fastest.
Arguments:
- state_field: bfloat16 [128, 1024, 256], P('lat', 'lon'), may hold values from -6 to 6
- support_offsets: int32 [128, 5, 8], replicated, may hold values from -8 to 8, as said below
- kernel_values: bfloat16 [3, 128, 5, 8], replicated, may hold values from -1 to 1
- basis_weight: bfloat16 [3, 256, 256], replicated, may hold values from -0.21875 to 0.21875
- weight_in: bfloat16 [256, 1024], replicated, may hold values from -0.375 to 0.375
- weight_out: bfloat16 [1024, 256], replicated, may hold values from -0.1875 to 0.1875
- cotangent: bfloat16 [128, 1024, 256], P('lat', 'lon'), may hold values from -6 to 6
Outputs:
- block_out: bfloat16 [128, 1024, 256], P('lat', 'lon')
- grad_field: bfloat16 [128, 1024, 256], P('lat', 'lon')
- grad_basis_weight: bfloat16 [3, 256, 256], replicated
- grad_weight_in: bfloat16 [256, 1024], replicated
- grad_weight_out: bfloat16 [1024, 256], replicated
Inputs may be any that keep to these rules, and one draw needn't show every extreme that they name: `support_offsets`: with p = min(i, 127 - i) and w(i) = max(1, 8 // (1 + p // 8)), every offset of cycle i lies within -w(i)..w(i); slot 0 holds w(i) and slot 1 holds -w(i) for every cycle and latitude offset.
All inputs are finite; a program needn't handle non-finite values.
Results may differ from a plain program's by a relative error of at most 0.017.
Values may be sent and summed in bfloat16 or wider, within the bound.
No kernel may reach another device: no remote copies, remote signals or barrier semaphores. Data moves between devices by JAX's collectives and lax.ppermute only.
A program may use at most 64 MiB of HBM per device.

v0:
```python
import math

import jax
import jax.numpy as jnp
from jax import lax
from jax.sharding import PartitionSpec as P

RAD = 2
WIDE = 8


def with_halo(cells, sides, width, closed):
    for axis, dim in sides:
        count = lax.axis_size(axis)
        ends = count if closed else count - 1
        head = lax.slice_in_dim(cells, 0, width, axis=dim)
        tail = lax.slice_in_dim(cells, cells.shape[dim] - width, cells.shape[dim], axis=dim)
        cells = jnp.concatenate(
            [
                lax.ppermute(tail, axis, [(i, (i + 1) % count) for i in range(ends)]),
                cells,
                lax.ppermute(head, axis, [((i + 1) % count, i) for i in range(ends)]),
            ],
            axis=dim,
        )
    return cells


def banded(values, shifts, out_cols, sign):
    in_cols = out_cols + 2 * WIDE
    source_ids = jnp.arange(in_cols, dtype=jnp.int32)[None, None, :, None]
    target_ids = jnp.arange(out_cols, dtype=jnp.int32)[None, None, None, :]
    aimed = target_ids + WIDE + sign * shifts[:, :, None, None]
    onehot = (source_ids == aimed).astype(jnp.float32)
    matrix = jnp.einsum(
        "kis,ismj->kimj", values.astype(jnp.float32), onehot, precision=lax.Precision.HIGHEST
    )
    high_part = matrix.astype(jnp.bfloat16)
    low_part = (matrix - high_part.astype(jnp.float32)).astype(jnp.bfloat16)
    return (high_part, low_part)


def local(
    state_field, support_offsets, kernel_values, basis_weight, weight_in, weight_out, cotangent
):
    band_rows, band_cols, channels = state_field.shape
    lag_count = 2 * RAD + 1
    band_start = lax.axis_index("lat") * band_rows
    local_offsets = lax.dynamic_slice_in_dim(support_offsets, band_start, band_rows, 0)
    local_values = lax.dynamic_slice_in_dim(kernel_values, band_start, band_rows, 1)
    widened = with_halo(state_field, (("lon", 1),), WIDE, True)
    extended = with_halo(widened, (("lat", 0),), RAD, False)
    basis_sum = jnp.zeros((basis_weight.shape[0], band_rows, band_cols, channels), jnp.float32)
    for offset_row in range(lag_count):
        high_part, low_part = banded(
            local_values[:, :, offset_row, :], local_offsets[:, offset_row, :], band_cols, 1
        )
        window = extended[offset_row : offset_row + band_rows]
        basis_sum = basis_sum + jnp.einsum(
            "kimj,imc->kijc", high_part, window, preferred_element_type=jnp.float32
        )
        basis_sum = basis_sum + jnp.einsum(
            "kimj,imc->kijc", low_part, window, preferred_element_type=jnp.float32
        )
    basis_out = basis_sum.astype(jnp.bfloat16)
    mixed_grid = jnp.einsum(
        "kijc,kcd->ijd", basis_out, basis_weight, preferred_element_type=jnp.float32
    ).astype(jnp.bfloat16)
    mixed_rows = mixed_grid.reshape(-1, channels)
    preactivation = jnp.dot(mixed_rows, weight_in, preferred_element_type=jnp.float32)
    hidden = jax.nn.gelu(preactivation).astype(jnp.bfloat16)
    branch_out = jnp.dot(hidden, weight_out, preferred_element_type=jnp.float32).reshape(
        state_field.shape
    )
    block_out = (state_field.astype(jnp.float32) + branch_out).astype(jnp.bfloat16)
    cot_flat = cotangent.reshape(-1, channels)
    upstream = jnp.dot(cot_flat, weight_out.T, preferred_element_type=jnp.float32)
    grad_pre = jax.vjp(jax.nn.gelu, preactivation)[1](upstream)[0].astype(jnp.bfloat16)
    grad_mixed = jnp.dot(grad_pre, weight_in.T, preferred_element_type=jnp.float32).astype(
        jnp.bfloat16
    )
    grad_grid = grad_mixed.reshape(state_field.shape)
    kernel_term = jnp.einsum(
        "kijc,ijd->kcd", basis_out, grad_grid, preferred_element_type=jnp.float32
    )
    inner_term = jnp.dot(mixed_rows.T, grad_pre, preferred_element_type=jnp.float32)
    outer_term = jnp.dot(hidden.T, cot_flat, preferred_element_type=jnp.float32)
    grad_basis = jnp.einsum(
        "ijd,kcd->kijc", grad_grid, basis_weight, preferred_element_type=jnp.float32
    ).astype(jnp.bfloat16)
    landing = jnp.zeros((band_rows + 2 * RAD, band_cols + 2 * WIDE, channels), jnp.float32)
    for offset_row in range(lag_count):
        high_part, low_part = banded(
            local_values[:, :, offset_row, :], local_offsets[:, offset_row, :], band_cols, 1
        )
        spread = jnp.einsum(
            "kimj,kijc->imc", high_part, grad_basis, preferred_element_type=jnp.float32
        )
        spread = spread + jnp.einsum(
            "kimj,kijc->imc", low_part, grad_basis, preferred_element_type=jnp.float32
        )
        landing = landing + jnp.pad(spread, ((offset_row, 2 * RAD - offset_row), (0, 0), (0, 0)))
    rim_cells = jnp.concatenate([landing[:, :WIDE], landing[:, band_cols + WIDE :]], axis=1)
    arrived = with_halo(rim_cells.astype(jnp.bfloat16), (("lon", 1),), WIDE, True).astype(
        rim_cells.dtype
    )
    middle = landing[:, WIDE : WIDE + band_cols]
    middle = middle.at[:, :WIDE].add(arrived[:, :WIDE])
    middle = middle.at[:, band_cols - WIDE :].add(arrived[:, 3 * WIDE :])
    edge_rows = jnp.concatenate([middle[:RAD], middle[band_rows + RAD :]], axis=0)
    arrived_rows = with_halo(edge_rows.astype(jnp.bfloat16), (("lat", 0),), RAD, False).astype(
        edge_rows.dtype
    )
    core_rows = middle[RAD : RAD + band_rows]
    core_rows = core_rows.at[:RAD].add(arrived_rows[:RAD])
    adjoint = core_rows.at[band_rows - RAD :].add(arrived_rows[3 * RAD :])
    grad_field = (cotangent.astype(jnp.float32) + adjoint).astype(jnp.bfloat16)
    grad_scale = 1.0 / math.sqrt(
        band_rows * lax.axis_size("lat") * band_cols * lax.axis_size("lon")
    )
    summed = lax.psum((kernel_term, inner_term, outer_term), ("lat", "lon"))
    finished = tuple(((total * grad_scale).astype(jnp.bfloat16) for total in summed))
    return (block_out, grad_field, finished[0], finished[1], finished[2])


def solution(mesh):
    return jax.shard_map(
        local,
        mesh=mesh,
        in_specs=(P("lat", "lon", None), P(), P(), P(), P(), P(), P("lat", "lon", None)),
        out_specs=(P("lat", "lon", None), P("lat", "lon", None), P(), P(), P()),
        check_vma=False,
    )
```

profile of v0, /device:TPU:1, one launch (start us, length us, event | category | flops | bytes accessed | tf_op | source)
XLA Modules:
  0.0 558.0 jit_solution(2841381405902397656)
XLA Ops:
  7.2 0.8 fusion.103
  8.1 8.9 %collective-permute-start.1 = (bf16[8,8,256]{2,1,0:T(8,128)(2,1)S(1)}, bf16[8,8,256]{2,1,0:T(8,128)(2,1)S(1)}, u32[]{:S(2)}, u32[]{:S(2)}) collective-permute-start(bf16[8,8,256]{2,1,0:T(8,128)(2,1)S(1)} %get-tuple-element.74), channel_id=1, source_target_pairs={{1,0},{2,1},{3,2},{4,3},{5,4},{6,5},{7,6},{8,7},{9,8},{10,9},{11,1... | collective-permute-start | bytes 98312 | tf_op jit(solution)/shard_map/ppermute | solution.py:22
  17.0 1.9 collective-permute-start
  23.1 0.6 copy-done.5
  24.1 0.8 copy-done.4
  24.9 1.3 collective-permute-start.2
  26.2 1.3 collective-permute-start.3
  28.0 3.1 collective-permute-done.3
  33.1 0.7 copy-done.1
  34.1 0.9 fusion.20
  35.5 1.6 fusion.97
  39.0 1.3 fusion.105
  41.8 1.9 collective-permute-start.4
  43.7 7.5 %collective-permute-start.5 = (bf16[12,8,256]{2,1,0:T(8,128)(2,1)S(1)}, bf16[12,8,256]{2,1,0:T(8,128)(2,1)S(1)}, u32[]{:S(2)}, u32[]{:S(2)}) collective-permute-start(bf16[12,8,256]{2,1,0:T(8,128)(2,1)S(1)} %get-tuple-element.69), channel_id=1, source_target_pairs={{1,0},{2,1},{3,2},{4,3},{5,4},{6,5},{7,6},{8,7},{9,8},{10,9},{11,1... | collective-permute-start | bytes 147464 | tf_op jit(solution)/shard_map/ppermute | solution.py:22
  51.3 1.2 convolution_bitcast_fusion
  52.7 3.1 collective-permute-start.6
  55.8 1.3 collective-permute-start.7
  57.1 0.7 add_convert_fusion.1
  57.8 7.2 %collective-permute-done.7 = bf16[2,32,256]{2,1,0:T(8,128)(2,1)S(1)} collective-permute-done((bf16[2,32,256]{2,1,0:T(8,128)(2,1)S(1)}, bf16[2,32,256]{2,1,0:T(8,128)(2,1)S(1)}, u32[]{:S(2)}, u32[]{:S(2)}) %collective-permute-start.7) | collective-permute-done | bytes 32800 | tf_op jit(solution)/shard_map/ppermute | solution.py:22
  65.1 0.7 add_convert_fusion
  65.8 481.1 %all-reduce.8.cloned.1.call-done = (f32[3,256,256]{2,1,0:T(8,128)}, f32[256,1024]{1,0:T(8,128)}, f32[1024,256]{1,0:T(8,128)}) async-done(((f32[3,256,256]{2,1,0:T(8,128)}, f32[256,1024]{1,0:T(8,128)}, f32[1024,256]{1,0:T(8,128)}), (f32[3,256,256]{2,1,0:T(8,128)}, f32[256,1024]{1,0:T(8,128)}, f32[1024,256]{1,0:T(8,128)})) %all-reduce.8.cloned.1.call-update) | async-done | bytes 2883600 | tf_op jit(solution)/shard_map/psum | solution.py:121
  546.9 2.0 multiply_convert_fusion.3
  548.9 0.9 multiply_convert_fusion.1
  550.3 0.9 multiply_convert_fusion
  (86 shorter events, 11.8 us)
Async XLA Ops:
  7.2 27.0 %copy-start = (bf16[256,1024]{1,0:T(8,128)(2,1)S(1)}, bf16[256,1024]{1,0:T(8,128)(2,1)}, u32[]{:S(2)}) copy-start(bf16[256,1024]{1,0:T(8,128)(2,1)} %param.19) | copy-start | bytes 1572868
  7.2 539.7 %all-reduce.8.cloned.1.call-start = ((), (), s32[]{:S(2)}) async-start(), calls=%async_computation | async-start | bytes 5767168 | tf_op jit(solution)/shard_map/psum | solution.py:121
  8.1 10.9 %copy-start.8 = (s32[128,5,8]{0,2,1:T(8,128)S(1)}, s32[128,5,8]{0,2,1:T(8,128)}, u32[]{:S(2)}) copy-start(s32[128,5,8]{0,2,1:T(8,128)} %param.16) | copy-start | bytes 61444
  8.1 16.8 %collective-permute-start.1 = (bf16[8,8,256]{2,1,0:T(8,128)(2,1)S(1)}, bf16[8,8,256]{2,1,0:T(8,128)(2,1)S(1)}, u32[]{:S(2)}, u32[]{:S(2)}) collective-permute-start(bf16[8,8,256]{2,1,0:T(8,128)(2,1)S(1)} %get-tuple-element.74), channel_id=1, source_target_pairs={{1,0},{2,1},{3,2},{4,3},{5,4},{6,5},{7,6},{8,7},{9,8},{10,9},{11,1... | collective-permute-start | bytes 98312 | tf_op jit(solution)/shard_map/ppermute | solution.py:22
  17.0 7.1 %collective-permute-start = (bf16[8,8,256]{2,1,0:T(8,128)(2,1)S(1)}, bf16[8,8,256]{2,1,0:T(8,128)(2,1)S(1)}, u32[]{:S(2)}, u32[]{:S(2)}) collective-permute-start(bf16[8,8,256]{2,1,0:T(8,128)(2,1)S(1)} %get-tuple-element.75), channel_id=1, source_target_pairs={{0,1},{1,2},{2,3},{3,4},{4,5},{5,6},{6,7},{7,8},{8,9},{9,10},{10,1... | collective-permute-start | bytes 98312 | tf_op jit(solution)/shard_map/ppermute | solution.py:20
  19.0 0.8 copy-start.7
  22.6 1.0 copy-start.5
  22.6 1.1 copy-start.6
  24.0 0.9 copy-start.4
  24.9 6.6 %collective-permute-start.2 = (bf16[2,48,256]{2,1,0:T(8,128)(2,1)S(1)}, bf16[2,48,256]{2,1,0:T(8,128)(2,1)S(1)}, u32[]{:S(2)}, u32[]{:S(2)}) collective-permute-start(bf16[2,48,256]{2,1,0:T(8,128)(2,1)S(1)} %get-tuple-element.72), channel_id=1, source_target_pairs={{0,32},{32,64},{64,96},{96,128},{128,160},{160,192},{192,224},{224... | collective-permute-start | bytes 147464 | tf_op jit(solution)/shard_map/ppermute | solution.py:20
  26.2 4.8 collective-permute-start.3
  32.8 1.0 copy-start.1
  41.8 10.8 %collective-permute-start.4 = (bf16[12,8,256]{2,1,0:T(8,128)(2,1)S(1)}, bf16[12,8,256]{2,1,0:T(8,128)(2,1)S(1)}, u32[]{:S(2)}, u32[]{:S(2)}) collective-permute-start(bf16[12,8,256]{2,1,0:T(8,128)(2,1)S(1)} %get-tuple-element.68), channel_id=1, source_target_pairs={{0,1},{1,2},{2,3},{3,4},{4,5},{5,6},{6,7},{7,8},{8,9},{9,10},{10,1... | collective-permute-start | bytes 147464 | tf_op jit(solution)/shard_map/ppermute | solution.py:20
  43.7 8.8 %collective-permute-start.5 = (bf16[12,8,256]{2,1,0:T(8,128)(2,1)S(1)}, bf16[12,8,256]{2,1,0:T(8,128)(2,1)S(1)}, u32[]{:S(2)}, u32[]{:S(2)}) collective-permute-start(bf16[12,8,256]{2,1,0:T(8,128)(2,1)S(1)} %get-tuple-element.69), channel_id=1, source_target_pairs={{1,0},{2,1},{3,2},{4,3},{5,4},{6,5},{7,6},{8,7},{9,8},{10,9},{11,1... | collective-permute-start | bytes 147464 | tf_op jit(solution)/shard_map/ppermute | solution.py:22
  52.7 5.1 collective-permute-start.6
  55.8 9.2 %collective-permute-start.7 = (bf16[2,32,256]{2,1,0:T(8,128)(2,1)S(1)}, bf16[2,32,256]{2,1,0:T(8,128)(2,1)S(1)}, u32[]{:S(2)}, u32[]{:S(2)}) collective-permute-start(bf16[2,32,256]{2,1,0:T(8,128)(2,1)S(1)} %get-tuple-element.71), channel_id=1, source_target_pairs={{32,0},{64,32},{96,64},{128,96},{160,128},{192,160},{224,192},{256... | collective-permute-start | bytes 98312 | tf_op jit(solution)/shard_map/ppermute | solution.py:22
  546.9 2.0 copy-start.3
  548.9 1.4 copy-start.2
Sparse Core Ops, SparseCore 0:
  52.7 494.1 all-reduce.7
where the time goes:
time: 559 us; the launch traced here: 558 us
  waiting for transfers between devices  491 us (88%)
  starting transfers between devices  27.3 us (5%)
  between operations  14.5 us (3%)
  matrix products  13.9 us (2%)
  other arithmetic  5.91 us (1%)
    psum x1, waiting for transfers between devices, local(): summed = lax.psum((kernel_term, inner_term, outer_term), ('lat', 'lon'))  481 us
    ppermute x4, starting transfers between devices, with_halo(): lax.ppermute(head, axis, [((i + 1) % count, i) for i in range(ends)])  19 us
  transfers between devices with their start and end apart: 9, of which 3 were waited for; matrix products, arithmetic and copies ran while one was open for 1% of the time, Pallas kernels for 0%

commit v1 on v0

--- a/solution.py
+++ b/solution.py
@@ -3,10 +3,46 @@
 import jax
 import jax.numpy as jnp
 from jax import lax
+from jax.sharding import Mesh
 from jax.sharding import PartitionSpec as P
 
 RAD = 2
 WIDE = 8
+
+FINE = (("z_hi", 4), ("x", 4), ("z_mid", 2), ("z_low", 2), ("y", 4), ("core", 2))
+LAT = ("z_hi", "x")
+LON = ("z_mid", "z_low", "y", "core")
+NEAR = ("x", "z_low", "y", "core")
+FAR = ("z_hi", "z_mid")
+LANES = 128
+
+
+def columns_first(matrix):
+    rows, cols = matrix.shape
+    return [matrix[:, c : c + LANES] for c in range(0, cols, LANES)]
+
+
+def total_over_devices(terms, scale):
+    near, far = lax.axis_size(NEAR), lax.axis_size(FAR)
+    flat = [term.reshape(-1, term.shape[-1]) for term in terms]
+    blocks = [block.astype(jnp.bfloat16) for term in flat for block in columns_first(term)]
+    packed = jnp.concatenate(blocks, axis=0).reshape(near, -1, LANES)
+    shares = lax.all_to_all(packed, NEAR, 0, 0)
+    share = jnp.sum(shares.astype(jnp.float32), axis=0).astype(jnp.bfloat16)
+    spread = jnp.broadcast_to(share[None], (far,) + share.shape)
+    planes = lax.all_to_all(spread, FAR, 0, 0)
+    done = (jnp.sum(planes.astype(jnp.float32), axis=0) * scale).astype(jnp.bfloat16)
+    copies = jnp.broadcast_to(done[None], (near,) + done.shape)
+    whole = lax.all_to_all(copies, NEAR, 0, 0).reshape(-1, LANES)
+    outs, start = [], 0
+    for term, matrix in zip(terms, flat):
+        rows, cols = matrix.shape
+        pieces = []
+        for _ in range(0, cols, LANES):
+            pieces.append(whole[start : start + rows])
+            start += rows
+        outs.append(jnp.concatenate(pieces, axis=1).reshape(term.shape))
+    return tuple(outs)
 
 
 def with_halo(cells, sides, width, closed):
@@ -45,11 +81,11 @@
 ):
     band_rows, band_cols, channels = state_field.shape
     lag_count = 2 * RAD + 1
-    band_start = lax.axis_index("lat") * band_rows
+    band_start = lax.axis_index(LAT) * band_rows
     local_offsets = lax.dynamic_slice_in_dim(support_offsets, band_start, band_rows, 0)
     local_values = lax.dynamic_slice_in_dim(kernel_values, band_start, band_rows, 1)
-    widened = with_halo(state_field, (("lon", 1),), WIDE, True)
-    extended = with_halo(widened, (("lat", 0),), RAD, False)
+    widened = with_halo(state_field, ((LON, 1),), WIDE, True)
+    extended = with_halo(widened, ((LAT, 0),), RAD, False)
     basis_sum = jnp.zeros((basis_weight.shape[0], band_rows, band_cols, channels), jnp.float32)
     for offset_row in range(lag_count):
         high_part, low_part = banded(
@@ -101,14 +137,14 @@
         )
         landing = landing + jnp.pad(spread, ((offset_row, 2 * RAD - offset_row), (0, 0), (0, 0)))
     rim_cells = jnp.concatenate([landing[:, :WIDE], landing[:, band_cols + WIDE :]], axis=1)
-    arrived = with_halo(rim_cells.astype(jnp.bfloat16), (("lon", 1),), WIDE, True).astype(
+    arrived = with_halo(rim_cells.astype(jnp.bfloat16), ((LON, 1),), WIDE, True).astype(
         rim_cells.dtype
     )
     middle = landing[:, WIDE : WIDE + band_cols]
     middle = middle.at[:, :WIDE].add(arrived[:, :WIDE])
     middle = middle.at[:, band_cols - WIDE :].add(arrived[:, 3 * WIDE :])
     edge_rows = jnp.concatenate([middle[:RAD], middle[band_rows + RAD :]], axis=0)
-    arrived_rows = with_halo(edge_rows.astype(jnp.bfloat16), (("lat", 0),), RAD, False).astype(
+    arrived_rows = with_halo(edge_rows.astype(jnp.bfloat16), ((LAT, 0),), RAD, False).astype(
         edge_rows.dtype
     )
     core_rows = middle[RAD : RAD + band_rows]
@@ -116,18 +152,19 @@
     adjoint = core_rows.at[band_rows - RAD :].add(arrived_rows[3 * RAD :])
     grad_field = (cotangent.astype(jnp.float32) + adjoint).astype(jnp.bfloat16)
     grad_scale = 1.0 / math.sqrt(
-        band_rows * lax.axis_size("lat") * band_cols * lax.axis_size("lon")
+        band_rows * lax.axis_size(LAT) * band_cols * lax.axis_size(LON)
     )
-    summed = lax.psum((kernel_term, inner_term, outer_term), ("lat", "lon"))
-    finished = tuple(((total * grad_scale).astype(jnp.bfloat16) for total in summed))
+    finished = total_over_devices((kernel_term, inner_term, outer_term), grad_scale)
     return (block_out, grad_field, finished[0], finished[1], finished[2])
 
 
 def solution(mesh):
+    names, sizes = zip(*FINE)
+    mesh = Mesh(mesh.devices.reshape(sizes), names)
     return jax.shard_map(
         local,
         mesh=mesh,
-        in_specs=(P("lat", "lon", None), P(), P(), P(), P(), P(), P("lat", "lon", None)),
-        out_specs=(P("lat", "lon", None), P("lat", "lon", None), P(), P(), P()),
+        in_specs=(P(LAT, LON, None), P(), P(), P(), P(), P(), P(LAT, LON, None)),
+        out_specs=(P(LAT, LON, None), P(LAT, LON, None), P(), P(), P()),
         check_vma=False,
     )

time: 559 us -> 147 us (0.26)
  the two profiles are of different devices: /device:TPU:1 before, /device:TPU:6 now
where the time goes in v1:
time: 147 us
  blocking collectives  52.1 us (35%)
  starting transfers between devices  43.7 us (30%)
  waiting for transfers between devices  24.7 us (17%)
  matrix products  12.1 us (8%)
  local copies, waits for them, and re-layouts  7.9 us (5%)
  other arithmetic  4.65 us (3%)
    all_to_all x1, blocking collectives, total_over_devices(): planes = lax.all_to_all(spread, FAR, 0, 0)  27 us
    all_to_all x1, blocking collectives, total_over_devices(): shares = lax.all_to_all(packed, NEAR, 0, 0)  25.1 us
    ppermute x4, starting transfers between devices, with_halo(): lax.ppermute(head, axis, [((i + 1) % count, i) for i in range(ends)])  21.7 us
    ppermute x4, waiting for transfers between devices, with_halo(): lax.ppermute(head, axis, [((i + 1) % count, i) for i in range(ends)])  17.5 us
    ppermute x4, starting transfers between devices, with_halo(): lax.ppermute(tail, axis, [(i, (i + 1) % count) for i in range(ends)])  15 us
    ppermute x4, waiting for transfers between devices, with_halo(): lax.ppermute(tail, axis, [(i, (i + 1) % count) for i in range(ends)])  7.2 us
    all_to_all x1, starting transfers between devices, total_over_devices(): whole = lax.all_to_all(copies, NEAR, 0, 0).reshape(-1, LANES)  6.98 us
    unnamed x62, local copies, waits for them, and re-layouts  3.1 us
  transfers between devices with their start and end apart: 9, of which 3 were waited for; matrix products, arithmetic and copies ran while one was open for 9% of the time, Pallas kernels for 0%

profile of v1, /device:TPU:6, one launch (start us, length us, event | category | flops | bytes accessed | tf_op | source)
XLA Modules:
  0.0 146.5 jit_solution(14557699503580636876)
XLA Ops:
  0.6 0.8 fusion.105
  1.5 1.9 %collective-permute-start = (bf16[8,8,256]{2,1,0:T(8,128)(2,1)S(1)}, bf16[8,8,256]{2,1,0:T(8,128)(2,1)S(1)}, u32[]{:S(2)}, u32[]{:S(2)}) collective-permute-start(bf16[8,8,256]{2,1,0:T(8,128)(2,1)S(1)} %get-tuple-element.76), channel_id=1, source_target_pairs={{0,1},{1,2},{2,3},{3,4},{4,5},{5,6},{6,7},{7,8},{8,9},{9,10},{10,1... | collective-permute-start | bytes 98312 | tf_op jit(solution)/shard_map/ppermute | solution.py:56
  3.4 8.4 %collective-permute-start.1 = (bf16[8,8,256]{2,1,0:T(8,128)(2,1)S(1)}, bf16[8,8,256]{2,1,0:T(8,128)(2,1)S(1)}, u32[]{:S(2)}, u32[]{:S(2)}) collective-permute-start(bf16[8,8,256]{2,1,0:T(8,128)(2,1)S(1)} %get-tuple-element.75), channel_id=1, source_target_pairs={{1,0},{2,1},{3,2},{4,3},{5,4},{6,5},{7,6},{8,7},{9,8},{10,9},{11,1... | collective-permute-start | bytes 98312 | tf_op jit(solution)/shard_map/ppermute | solution.py:58
  11.9 0.8 constant_dynamic-slice_fusion.7
  13.0 0.8 constant_dynamic-slice_fusion.6
  18.1 9.0 %collective-permute-start.2 = (bf16[2,48,256]{2,1,0:T(8,128)(2,1)S(1)}, bf16[2,48,256]{2,1,0:T(8,128)(2,1)S(1)}, u32[]{:S(2)}, u32[]{:S(2)}) collective-permute-start(bf16[2,48,256]{2,1,0:T(8,128)(2,1)S(1)} %get-tuple-element.73), channel_id=1, source_target_pairs={{0,32},{32,64},{64,96},{96,128},{128,160},{160,192},{192,224},{224... | collective-permute-start | bytes 147464 | tf_op jit(solution)/shard_map/ppermute | solution.py:56
  27.1 1.9 %collective-permute-start.3 = (bf16[2,48,256]{2,1,0:T(8,128)(2,1)S(1)}, bf16[2,48,256]{2,1,0:T(8,128)(2,1)S(1)}, u32[]{:S(2)}, u32[]{:S(2)}) collective-permute-start(bf16[2,48,256]{2,1,0:T(8,128)(2,1)S(1)} %get-tuple-element.74), channel_id=1, source_target_pairs={{32,0},{64,32},{96,64},{128,96},{160,128},{192,160},{224,192},{256... | collective-permute-start | bytes 147464 | tf_op jit(solution)/shard_map/ppermute | solution.py:58
  30.0 9.6 %collective-permute-done.3 = bf16[2,48,256]{2,1,0:T(8,128)(2,1)S(1)} collective-permute-done((bf16[2,48,256]{2,1,0:T(8,128)(2,1)S(1)}, bf16[2,48,256]{2,1,0:T(8,128)(2,1)S(1)}, u32[]{:S(2)}, u32[]{:S(2)}) %collective-permute-start.3) | collective-permute-done | bytes 49184 | tf_op jit(solution)/shard_map/ppermute | solution.py:58
  42.2 0.9 fusion.20
  45.4 25.1 %all_to_all.15 = bf16[64,88,128]{2,1,0:T(8,128)(2,1)S(1)} all-to-all(bf16[64,88,128]{2,1,0:T(8,128)(2,1)S(1)} %bitcast.193), channel_id=1, replica_groups=mesh['z_hi'=4,'x'=4,'z_mid'=2,'z_low'=2,'y'=4,'core'=2] {'x','z_low','y'..., dimensions={0} | all-to-all | bytes 2883584 | tf_op jit(solution)/shard_map/all_to_all | solution.py:30
  70.6 0.8 reduce_sum.21
  71.4 0.8 broadcast_in_dim.4
  72.1 27.0 %all_to_all.16 = bf16[8,88,128]{2,1,0:T(8,128)(2,1)S(1)} all-to-all(bf16[8,88,128]{2,1,0:T(8,128)(2,1)S(1)} %broadcast_in_dim.4), channel_id=1, replica_groups=mesh['z_hi'=4,'x'=4,'z_mid'=2,'z_low'=2,'y'=4,'core'=2] {'z_hi','z_mid'}, dimensions={0} | all-to-all | bytes 360448 | tf_op jit(solution)/shard_map/all_to_all | solution.py:33
  99.2 1.3 broadcast_in_dim.5
  100.5 7.0 %all-to-all-start.2 = ((bf16[64,88,128]{2,1,0:T(8,128)(2,1)}), bf16[64,88,128]{2,1,0:T(8,128)(2,1)S(1)}, u32[]{:S(2)}, u32[]{:S(2)}) async-start(bf16[64,88,128]{2,1,0:T(8,128)(2,1)} %broadcast_in_dim.5), calls=%async_computation.2 | async-start | bytes 2883584 | tf_op jit(solution)/shard_map/all_to_all | solution.py:36
  107.5 1.4 fusion.7
  111.9 2.2 %collective-permute-start.4 = (bf16[12,8,256]{2,1,0:T(8,128)(2,1)S(1)}, bf16[12,8,256]{2,1,0:T(8,128)(2,1)S(1)}, u32[]{:S(2)}, u32[]{:S(2)}) collective-permute-start(bf16[12,8,256]{2,1,0:T(8,128)(2,1)S(1)} %get-tuple-element.69), channel_id=1, source_target_pairs={{0,1},{1,2},{2,3},{3,4},{4,5},{5,6},{6,7},{7,8},{8,9},{9,10},{10,1... | collective-permute-start | bytes 147464 | tf_op jit(solution)/shard_map/ppermute | solution.py:56
  114.1 7.4 %collective-permute-start.5 = (bf16[12,8,256]{2,1,0:T(8,128)(2,1)S(1)}, bf16[12,8,256]{2,1,0:T(8,128)(2,1)S(1)}, u32[]{:S(2)}, u32[]{:S(2)}) collective-permute-start(bf16[12,8,256]{2,1,0:T(8,128)(2,1)S(1)} %get-tuple-element.70), channel_id=1, source_target_pairs={{1,0},{2,1},{3,2},{4,3},{5,4},{6,5},{7,6},{8,7},{9,8},{10,9},{11,1... | collective-permute-start | bytes 147464 | tf_op jit(solution)/shard_map/ppermute | solution.py:58
  122.0 7.2 %collective-permute-done.4 = bf16[12,8,256]{2,1,0:T(8,128)(2,1)S(1)} collective-permute-done((bf16[12,8,256]{2,1,0:T(8,128)(2,1)S(1)}, bf16[12,8,256]{2,1,0:T(8,128)(2,1)S(1)}, u32[]{:S(2)}, u32[]{:S(2)}) %collective-permute-start.4) | collective-permute-done | bytes 49184 | tf_op jit(solution)/shard_map/ppermute | solution.py:56
  129.3 1.9 %collective-permute-start.6 = (bf16[2,32,256]{2,1,0:T(8,128)(2,1)S(1)}, bf16[2,32,256]{2,1,0:T(8,128)(2,1)S(1)}, u32[]{:S(2)}, u32[]{:S(2)}) collective-permute-start(bf16[2,32,256]{2,1,0:T(8,128)(2,1)S(1)} %get-tuple-element.71), channel_id=1, source_target_pairs={{0,32},{32,64},{64,96},{96,128},{128,160},{160,192},{192,224},{224... | collective-permute-start | bytes 98312 | tf_op jit(solution)/shard_map/ppermute | solution.py:56
  131.3 3.9 %collective-permute-start.7 = (bf16[2,32,256]{2,1,0:T(8,128)(2,1)S(1)}, bf16[2,32,256]{2,1,0:T(8,128)(2,1)S(1)}, u32[]{:S(2)}, u32[]{:S(2)}) collective-permute-start(bf16[2,32,256]{2,1,0:T(8,128)(2,1)S(1)} %get-tuple-element.72), channel_id=1, source_target_pairs={{32,0},{64,32},{96,64},{128,96},{160,128},{192,160},{224,192},{256... | collective-permute-start | bytes 98312 | tf_op jit(solution)/shard_map/ppermute | solution.py:58
  135.9 7.8 %collective-permute-done.7 = bf16[2,32,256]{2,1,0:T(8,128)(2,1)S(1)} collective-permute-done((bf16[2,32,256]{2,1,0:T(8,128)(2,1)S(1)}, bf16[2,32,256]{2,1,0:T(8,128)(2,1)S(1)}, u32[]{:S(2)}, u32[]{:S(2)}) %collective-permute-start.7) | collective-permute-done | bytes 32800 | tf_op jit(solution)/shard_map/ppermute | solution.py:58
  144.8 0.9 pad_maximum_fusion
  145.7 0.8 pad_maximum_fusion.1
  (128 shorter events, 15.3 us)
Async XLA Ops:
  0.6 41.6 %copy-start = (bf16[256,1024]{1,0:T(8,128)(2,1)S(1)}, bf16[256,1024]{1,0:T(8,128)(2,1)}, u32[]{:S(2)}) copy-start(bf16[256,1024]{1,0:T(8,128)(2,1)} %param.19) | copy-start | bytes 1572868
  1.5 16.4 %collective-permute-start = (bf16[8,8,256]{2,1,0:T(8,128)(2,1)S(1)}, bf16[8,8,256]{2,1,0:T(8,128)(2,1)S(1)}, u32[]{:S(2)}, u32[]{:S(2)}) collective-permute-start(bf16[8,8,256]{2,1,0:T(8,128)(2,1)S(1)} %get-tuple-element.76), channel_id=1, source_target_pairs={{0,1},{1,2},{2,3},{3,4},{4,5},{5,6},{6,7},{7,8},{8,9},{9,10},{10,1... | collective-permute-start | bytes 98312 | tf_op jit(solution)/shard_map/ppermute | solution.py:56
  3.4 14.7 %collective-permute-start.1 = (bf16[8,8,256]{2,1,0:T(8,128)(2,1)S(1)}, bf16[8,8,256]{2,1,0:T(8,128)(2,1)S(1)}, u32[]{:S(2)}, u32[]{:S(2)}) collective-permute-start(bf16[8,8,256]{2,1,0:T(8,128)(2,1)S(1)} %get-tuple-element.75), channel_id=1, source_target_pairs={{1,0},{2,1},{3,2},{4,3},{5,4},{6,5},{7,6},{8,7},{9,8},{10,9},{11,1... | collective-permute-start | bytes 98312 | tf_op jit(solution)/shard_map/ppermute | solution.py:58
  14.6 25.5 %copy-start.1 = (bf16[3,8,48,32]{2,3,1,0:T(8,128)(2,1)}, bf16[3,8,48,32]{2,3,1,0:T(8,128)(2,1)S(1)}, u32[]{:S(2)}) copy-start(bf16[3,8,48,32]{2,3,1,0:T(8,128)(2,1)S(1)} %get-tuple-element.58) | copy-start | bytes 221188
  15.3 25.4 %copy-start.3 = (bf16[3,8,48,32]{2,3,1,0:T(8,128)(2,1)}, bf16[3,8,48,32]{2,3,1,0:T(8,128)(2,1)S(1)}, u32[]{:S(2)}) copy-start(bf16[3,8,48,32]{2,3,1,0:T(8,128)(2,1)S(1)} %get-tuple-element.55) | copy-start | bytes 221188
  16.5 1.0 copy-start.9
  16.5 1.1 copy-start.11
  17.1 1.0 copy-start.6
  18.1 11.4 %collective-permute-start.2 = (bf16[2,48,256]{2,1,0:T(8,128)(2,1)S(1)}, bf16[2,48,256]{2,1,0:T(8,128)(2,1)S(1)}, u32[]{:S(2)}, u32[]{:S(2)}) collective-permute-start(bf16[2,48,256]{2,1,0:T(8,128)(2,1)S(1)} %get-tuple-element.73), channel_id=1, source_target_pairs={{0,32},{32,64},{64,96},{96,128},{128,160},{160,192},{192,224},{224... | collective-permute-start | bytes 147464 | tf_op jit(solution)/shard_map/ppermute | solution.py:56
  27.1 12.5 %collective-permute-start.3 = (bf16[2,48,256]{2,1,0:T(8,128)(2,1)S(1)}, bf16[2,48,256]{2,1,0:T(8,128)(2,1)S(1)}, u32[]{:S(2)}, u32[]{:S(2)}) collective-permute-start(bf16[2,48,256]{2,1,0:T(8,128)(2,1)S(1)} %get-tuple-element.74), channel_id=1, source_target_pairs={{32,0},{64,32},{96,64},{128,96},{160,128},{192,160},{224,192},{256... | collective-permute-start | bytes 147464 | tf_op jit(solution)/shard_map/ppermute | solution.py:58
  40.9 1.0 copy-start.5
  43.1 1.7 %copy-start.14 = (f32[256,1024]{1,0:T(8,128)}, f32[256,1024]{1,0:T(8,128)S(1)}, u32[]{:S(2)}) copy-start(f32[256,1024]{1,0:T(8,128)S(1)} %get-tuple-element.93) | copy-start | bytes 3145732
  100.5 44.0 %all-to-all-start.2 = ((bf16[64,88,128]{2,1,0:T(8,128)(2,1)}), bf16[64,88,128]{2,1,0:T(8,128)(2,1)S(1)}, u32[]{:S(2)}, u32[]{:S(2)}) async-start(bf16[64,88,128]{2,1,0:T(8,128)(2,1)} %broadcast_in_dim.5), calls=%async_computation.2 | async-start | bytes 2883584 | tf_op jit(solution)/shard_map/all_to_all | solution.py:36
  108.9 0.9 copy-start.4
  109.4 1.0 copy-start.2
  111.7 9.8 %copy-start.10 = (bf16[1024,256]{1,0:T(8,128)(2,1)S(1)}, bf16[1024,256]{1,0:T(8,128)(2,1)}, u32[]{:S(2)}) copy-start(bf16[1024,256]{1,0:T(8,128)(2,1)} %param.20) | copy-start | bytes 1572868
  111.7 9.8 %copy-start.15 = (f32[256,1024]{1,0:T(8,128)S(1)}, f32[256,1024]{1,0:T(8,128)}, u32[]{:S(2)}) copy-start(f32[256,1024]{1,0:T(8,128)} %copy-done.14) | copy-start | bytes 3145732
  111.9 17.4 %collective-permute-start.4 = (bf16[12,8,256]{2,1,0:T(8,128)(2,1)S(1)}, bf16[12,8,256]{2,1,0:T(8,128)(2,1)S(1)}, u32[]{:S(2)}, u32[]{:S(2)}) collective-permute-start(bf16[12,8,256]{2,1,0:T(8,128)(2,1)S(1)} %get-tuple-element.69), channel_id=1, source_target_pairs={{0,1},{1,2},{2,3},{3,4},{4,5},{5,6},{6,7},{7,8},{8,9},{9,10},{10,1... | collective-permute-start | bytes 147464 | tf_op jit(solution)/shard_map/ppermute | solution.py:56
  114.1 15.2 %collective-permute-start.5 = (bf16[12,8,256]{2,1,0:T(8,128)(2,1)S(1)}, bf16[12,8,256]{2,1,0:T(8,128)(2,1)S(1)}, u32[]{:S(2)}, u32[]{:S(2)}) collective-permute-start(bf16[12,8,256]{2,1,0:T(8,128)(2,1)S(1)} %get-tuple-element.70), channel_id=1, source_target_pairs={{1,0},{2,1},{3,2},{4,3},{5,4},{6,5},{7,6},{8,7},{9,8},{10,9},{11,1... | collective-permute-start | bytes 147464 | tf_op jit(solution)/shard_map/ppermute | solution.py:58
  122.0 13.2 %copy-start.7 = (bf16[8,32,256]{2,1,0:T(8,128)(2,1)S(1)}, bf16[8,32,256]{2,1,0:T(8,128)(2,1)}, u32[]{:S(2)}) copy-start(bf16[8,32,256]{2,1,0:T(8,128)(2,1)} %param.15) | copy-start | bytes 393220
  129.3 14.5 %copy-start.12 = (bf16[8,32,256]{2,1,0:T(8,128)(2,1)S(1)}, bf16[8,32,256]{2,1,0:T(8,128)(2,1)}, u32[]{:S(2)}) copy-start(bf16[8,32,256]{2,1,0:T(8,128)(2,1)} %param.21) | copy-start | bytes 393220
  129.3 6.6 %collective-permute-start.6 = (bf16[2,32,256]{2,1,0:T(8,128)(2,1)S(1)}, bf16[2,32,256]{2,1,0:T(8,128)(2,1)S(1)}, u32[]{:S(2)}, u32[]{:S(2)}) collective-permute-start(bf16[2,32,256]{2,1,0:T(8,128)(2,1)S(1)} %get-tuple-element.71), channel_id=1, source_target_pairs={{0,32},{32,64},{64,96},{96,128},{128,160},{160,192},{192,224},{224... | collective-permute-start | bytes 98312 | tf_op jit(solution)/shard_map/ppermute | solution.py:56
  131.3 12.5 %collective-permute-start.7 = (bf16[2,32,256]{2,1,0:T(8,128)(2,1)S(1)}, bf16[2,32,256]{2,1,0:T(8,128)(2,1)S(1)}, u32[]{:S(2)}, u32[]{:S(2)}) collective-permute-start(bf16[2,32,256]{2,1,0:T(8,128)(2,1)S(1)} %get-tuple-element.72), channel_id=1, source_target_pairs={{32,0},{64,32},{96,64},{128,96},{160,128},{192,160},{224,192},{256... | collective-permute-start | bytes 98312 | tf_op jit(solution)/shard_map/ppermute | solution.py:58
  144.8 1.7 %copy-start.13 = (bf16[256,1024]{1,0:T(8,128)(2,1)}, bf16[256,1024]{1,0:T(8,128)(2,1)S(1)}, u32[]{:S(2)}) copy-start(bf16[256,1024]{1,0:T(8,128)(2,1)S(1)} %slice_dynamic-update-slice_fusion.4) | copy-start | bytes 1572868
  (1 other events, 0.7 us)

commit v2 on v0

v2 whole, which is shorter than its diff:
```python
import functools
import math

import jax
import jax.numpy as jnp
from jax import lax
from jax.experimental import pallas as pl
from jax.experimental.pallas import tpu as pltpu
from jax.sharding import Mesh
from jax.sharding import PartitionSpec as P

RAD = 2
WIDE = 8
LAGS = 2 * RAD + 1

FINE = (("z_hi", 4), ("x", 4), ("z_mid", 2), ("z_low", 2), ("y", 4), ("core", 2))
LAT = ("z_hi", "x")
LON = ("z_mid", "z_low", "y", "core")
NEAR = ("x", "z_low", "y", "core")
FAR = ("z_hi", "z_mid")
LANES = 128
CHUNK = 256

ROWS, COLS = ((0,), (0,)), ((1,), (1,))
VMEM = pl.BlockSpec(memory_space=pltpu.VMEM)
SMEM = pl.BlockSpec(memory_space=pltpu.SMEM)


def dot(a, b, contract=((1,), (0,))):
    return lax.dot_general(a, b, (contract, ((), ())), preferred_element_type=jnp.float32)


def kernel_call(body, operands, specs, outs, scratch=(), flops=0, mib=24, name=None):
    moved = sum(x.size * x.dtype.itemsize for x in (*operands, *outs))
    return pl.pallas_call(
        body,
        out_shape=tuple(outs),
        in_specs=specs,
        out_specs=tuple(VMEM for _ in outs),
        scratch_shapes=scratch,
        compiler_params=pltpu.CompilerParams(vmem_limit_bytes=mib << 20),
        cost_estimate=pl.CostEstimate(flops=flops, bytes_accessed=moved, transcendentals=0),
        name=name,
    )(*operands)


def like(shape, dtype):
    return jax.ShapeDtypeStruct(shape, dtype)


def prepare_kernel(cols, offset_ref, value_ref, cot_ref, out_ref, high_ref, low_ref, up_ref):
    up_ref[...] = dot(cot_ref[...], out_ref[...], COLS)
    kinds, cycles, lags, slots = 3, high_ref.shape[0] // (3 * cols), LAGS, offset_ref.shape[0]
    slots = slots // (cycles * lags)
    span = cols + 2 * WIDE
    shape = (cols, LANES)
    ahead = lax.broadcasted_iota(jnp.int32, shape, 1) - lax.broadcasted_iota(jnp.int32, shape, 0)

    def cycle(i, carry):
        for start in range(0, high_ref.shape[1], LANES):
            sums = [jnp.zeros(shape, jnp.float32) for _ in range(kinds)]
            for q in range(lags):
                if q * span >= start + LANES or (q + 1) * span <= start:
                    continue
                for s in range(slots):
                    at = (i * lags + q) * slots + s
                    hit = ahead == offset_ref[at] + (q * span + WIDE - start)
                    for k in range(kinds):
                        value = value_ref[k * cycles * lags * slots + at]
                        sums[k] = sums[k] + jnp.where(hit, value, 0.0)
            for k in range(kinds):
                at = pl.ds(pl.multiple_of((i * kinds + k) * cols, cols), cols)
                high = sums[k].astype(jnp.bfloat16)
                high_ref[at, start : start + LANES] = high
                rest = sums[k] - high.astype(jnp.float32)
                low_ref[at, start : start + LANES] = rest.astype(jnp.bfloat16)
        return carry

    lax.fori_loop(0, cycles, cycle, 0)


def gelu_and_slope(x):
    c, a = math.sqrt(2.0 / math.pi), 0.044715
    square = x * x
    t = jnp.tanh(c * (x + a * (square * x)))
    cdf = 0.5 * (1.0 + t)
    slope = cdf + (0.5 * x) * (1.0 - t * t) * (c * (1.0 + (3.0 * a) * square))
    return x * cdf, slope


def main_kernel(
    high_ref, low_ref, top_ref, state_ref, bottom_ref, left_ref, right_ref, cot_ref, up_ref, mix_ref, in_ref,
    packed_ref, hidden_ref, grad_ref, cells_ref, basis_ref,
):
    rows, cols, channels = state_ref.shape
    span = cols + 2 * WIDE
    kinds = basis_ref.shape[0]
    for r in range(rows + 2 * RAD):
        if r < RAD:
            middle = top_ref[r]
        elif r < RAD + rows:
            middle = state_ref[r - RAD]
        else:
            middle = bottom_ref[r - RAD - rows]
        parts = [left_ref[r], middle, right_ref[r]]
        line = jnp.concatenate([part.astype(jnp.float32) for part in parts], axis=0)
        cells_ref[r * span : (r + 1) * span] = line.astype(jnp.bfloat16)
    used = (rows + 2 * RAD) * span
    cells_ref[used:] = jnp.zeros((cells_ref.shape[0] - used, channels), jnp.bfloat16)

    depth = high_ref.shape[1]
    for i in range(rows):
        window = cells_ref[i * span : i * span + depth]
        at = slice(i * kinds * cols, (i + 1) * kinds * cols)
        taken = dot(high_ref[at], window) + dot(low_ref[at], window)
        for k in range(kinds):
            piece = taken[k * cols : (k + 1) * cols].astype(jnp.bfloat16)
            basis_ref[k, i * cols : (i + 1) * cols] = piece
    mixed = sum(dot(basis_ref[k], mix_ref[k]) for k in range(kinds)).astype(jnp.bfloat16)

    cot = cot_ref[...]
    start = 0

    def pack(matrix, place, height):
        for c in range(0, matrix.shape[1], LANES):
            at = place + (c // LANES) * height
            packed_ref[at : at + matrix.shape[0]] = matrix[:, c : c + LANES].astype(jnp.bfloat16)

    units = in_ref.shape[1]
    outer_at, inner_at = 0, units * (channels // LANES)
    basis_at = inner_at + channels * (units // LANES)
    back = jnp.zeros((rows * cols, channels), jnp.float32)
    for c in range(0, units, CHUNK):
        weight = in_ref[:, c : c + CHUNK]
        hidden, slope = gelu_and_slope(dot(mixed, weight))
        hidden = hidden.astype(jnp.bfloat16)
        grad_pre = (up_ref[:, c : c + CHUNK] * slope).astype(jnp.bfloat16)
        hidden_ref[:, c : c + CHUNK] = hidden
        back = back + dot(grad_pre, weight, COLS)
        pack(dot(hidden, cot, ROWS), outer_at + c, units)
        pack(dot(mixed, grad_pre, ROWS), inner_at + (c // LANES) * channels, channels)
    grad_mixed = back.astype(jnp.bfloat16)
    grad_ref[...] = grad_mixed
    for k in range(kinds):
        pack(dot(basis_ref[k], grad_mixed, ROWS), basis_at + k * channels, kinds * channels)


def adjoint_kernel(
    grad_ref, mix_ref, high_ref, low_ref, hidden_ref, out_ref, state_ref,
    left_ref, right_ref, middle_ref, block_ref, back_ref, landing_ref,
):
    rows, cols, channels = state_ref.shape
    span = cols + 2 * WIDE
    kinds = mix_ref.shape[0]
    grad = grad_ref[...]
    for k in range(kinds):
        back_ref[k] = dot(grad, mix_ref[k], COLS).astype(jnp.bfloat16)
    landing_ref[...] = jnp.zeros_like(landing_ref)
    depth = high_ref.shape[1]
    for i in range(rows):
        pieces = [back_ref[k, i * cols : (i + 1) * cols] for k in range(kinds)]
        taken = jnp.concatenate(pieces, axis=0)
        at = slice(i * kinds * cols, (i + 1) * kinds * cols)
        spread = dot(high_ref[at], taken, ROWS) + dot(low_ref[at], taken, ROWS)
        landing_ref[i * span : i * span + depth] += spread
    for r in range(rows + 2 * RAD):
        line = landing_ref[r * span : (r + 1) * span]
        left_ref[r] = line[:WIDE].astype(jnp.bfloat16)
        middle_ref[r] = line[WIDE : WIDE + cols]
        right_ref[r] = line[WIDE + cols :].astype(jnp.bfloat16)
    branch = dot(hidden_ref[...], out_ref[...])
    for i in range(rows):
        line = state_ref[i].astype(jnp.float32) + branch[i * cols : (i + 1) * cols]
        block_ref[i] = line.astype(jnp.bfloat16)


def rims_kernel(middle_ref, left_ref, right_ref, top_ref, bottom_ref, core_ref):
    rows, cols = core_ref.shape[:2]
    for r in range(rows + 2 * RAD):
        line = middle_ref[r]
        head = line[:WIDE] + left_ref[r].astype(jnp.float32)
        tail = line[cols - WIDE :] + right_ref[r].astype(jnp.float32)
        line = jnp.concatenate([head, line[WIDE : cols - WIDE], tail], axis=0)
        if r < RAD:
            top_ref[r] = line.astype(jnp.bfloat16)
        elif r < RAD + rows:
            core_ref[r - RAD] = line
        else:
            bottom_ref[r - RAD - rows] = line.astype(jnp.bfloat16)


def field_kernel(cot_ref, core_ref, above_ref, below_ref, field_ref):
    rows = core_ref.shape[0]
    for r in range(rows):
        line = core_ref[r]
        if r < RAD:
            line = line + above_ref[r].astype(jnp.float32)
        if r >= rows - RAD:
            line = line + below_ref[r - rows + RAD].astype(jnp.float32)
        field_ref[r] = (cot_ref[r].astype(jnp.float32) + line).astype(jnp.bfloat16)


def sum_kernel(scale, parts_ref, *refs):
    out_ref = refs[-1]
    total = parts_ref[0].astype(jnp.float32)
    for i in range(1, parts_ref.shape[0]):
        total = total + parts_ref[i].astype(jnp.float32)
    total = (total * scale).astype(out_ref.dtype)
    for i in range(out_ref.shape[0]):
        out_ref[i] = total


def sum_and_copy(parts, scale, copies, *later_than):
    return kernel_call(
        functools.partial(sum_kernel, scale),
        (parts, *later_than),
        [VMEM] + [pl.BlockSpec(memory_space=pl.ANY)] * len(later_than),
        [like((copies,) + parts.shape[1:], jnp.bfloat16)],
        flops=parts.size,
        mib=16,
        name="sum_and_copy",
    )[0]


def unpack(whole, shapes):
    flat, outs, start = whole.reshape(-1, LANES), [], 0
    for rows, cols in shapes:
        pieces = []
        for _ in range(0, cols, LANES):
            pieces.append(flat[start : start + rows])
            start += rows
        outs.append(jnp.concatenate(pieces, axis=1))
    return outs


def shift(cells, axes, step, closed):
    count = lax.axis_size(axes)
    pairs = [(i, (i + step) % count) for i in range(count) if closed or 0 <= i + step < count]
    return lax.ppermute(cells, axes, pairs)


def local(
    state_field, support_offsets, kernel_values, basis_weight, weight_in, weight_out, cotangent
):
    rows, cols, channels = state_field.shape
    kinds, units = basis_weight.shape[0], weight_in.shape[1]
    cells, span = rows * cols, cols + 2 * WIDE
    tall = rows + 2 * RAD
    depth = -(-LAGS * span // LANES) * LANES
    near, far = lax.axis_size(NEAR), lax.axis_size(FAR)
    cot_flat = cotangent.reshape(cells, channels)
    f32, bf16 = jnp.float32, jnp.bfloat16

    top = shift(state_field[rows - RAD :], LAT, 1, False)
    bottom = shift(state_field[:RAD], LAT, -1, False)
    heads = jnp.concatenate([top[:, :WIDE], state_field[:, :WIDE], bottom[:, :WIDE]], axis=0)
    tails = jnp.concatenate(
        [top[:, cols - WIDE :], state_field[:, cols - WIDE :], bottom[:, cols - WIDE :]], axis=0
    )
    left = shift(tails, LON, 1, True)
    right = shift(heads, LON, -1, True)

    band_start = lax.axis_index(LAT) * rows
    offsets = lax.dynamic_slice_in_dim(support_offsets, band_start, rows, 0)
    values = lax.dynamic_slice_in_dim(kernel_values, band_start, rows, 1).astype(f32)
    band_shape = (rows * kinds * cols, depth)
    high, low, upstream = kernel_call(
        functools.partial(prepare_kernel, cols),
        (offsets.reshape(-1), values.reshape(-1), cot_flat, weight_out),
        [SMEM, SMEM, VMEM, VMEM],
        [like(band_shape, bf16), like(band_shape, bf16), like((cells, units), f32)],
        flops=8 * cells * channels * units,
        name="prepare",
    )
    packed_rows = channels * (2 * units + kinds * channels) // LANES
    packed, hidden, grad_mixed = kernel_call(
        main_kernel,
        (high, low, top, state_field, bottom, left, right, cot_flat, upstream, basis_weight, weight_in),
        [VMEM] * 11,
        [like((packed_rows, LANES), bf16), like((cells, units), bf16), like((cells, channels), bf16)],
        [
            pltpu.VMEM((rows * span + depth, channels), bf16),
            pltpu.VMEM((kinds, cells, channels), bf16),
        ],
        flops=8 * cells * channels * units,
        mib=32,
        name="main",
    )

    shares = lax.all_to_all(packed.reshape(near, -1, LANES), NEAR, 0, 0)

    to_left, to_right, middle, block_out = kernel_call(
        adjoint_kernel,
        (grad_mixed, basis_weight, high, low, hidden, weight_out, state_field),
        [VMEM] * 7,
        [
            like((tall, WIDE, channels), bf16),
            like((tall, WIDE, channels), bf16),
            like((tall, cols, channels), f32),
            like(state_field.shape, bf16),
        ],
        [
            pltpu.VMEM((kinds, cells, channels), bf16),
            pltpu.VMEM((rows * span + depth, channels), f32),
        ],
        flops=4 * cells * channels * units,
        mib=32,
        name="adjoint",
    )
    from_left = shift(to_right, LON, 1, True)
    from_right = shift(to_left, LON, -1, True)
    planes = sum_and_copy(shares, 1.0, far, from_left, from_right)
    planes = lax.all_to_all(planes, FAR, 0, 0)
    rim = like((RAD, cols, channels), bf16)
    to_above, to_below, core = kernel_call(
        rims_kernel,
        (middle, from_left, from_right),
        [VMEM] * 3,
        [rim, rim, like(state_field.shape, f32)],
        name="rims",
    )
    above = shift(to_below, LAT, 1, False)
    below = shift(to_above, LAT, -1, False)
    scale = 1.0 / math.sqrt(cells * lax.axis_size(LAT) * lax.axis_size(LON))
    copies = sum_and_copy(planes, scale, near, core)
    whole = lax.all_to_all(copies, NEAR, 0, 0)
    (grad_field,) = kernel_call(
        field_kernel,
        (cotangent, core, above, below),
        [VMEM] * 4,
        [like(state_field.shape, bf16)],
        name="field",
    )
    shapes = ((units, channels), (channels, units), (kinds * channels, channels))
    grad_out, grad_in, grad_basis = unpack(whole, shapes)
    return (block_out, grad_field, grad_basis.reshape(basis_weight.shape), grad_in, grad_out)


def solution(mesh):
    names, sizes = zip(*FINE)
    mesh = Mesh(mesh.devices.reshape(sizes), names)
    return jax.shard_map(
        local,
        mesh=mesh,
        in_specs=(P(LAT, LON, None), P(), P(), P(), P(), P(), P(LAT, LON, None)),
        out_specs=(P(LAT, LON, None), P(LAT, LON, None), P(), P(), P()),
        check_vma=False,
    )
```

time: 559 us -> 130 us (0.23)
  waiting for transfers between devices: 491 us -> 45.1 us
  starting transfers between devices: 27.3 us -> 62.7 us
  matrix products: 13.9 us -> 0 us
  between operations: 14.5 us -> 0.99 us
  Pallas kernels: 0 us -> 9.74 us
    psum x1 -> x0, waiting for transfers between devices: 481 us -> none  [local(): summed = lax.psum((kernel_term, inner_term, outer_term), ('lat', 'lon'))]
    all_to_all x0 -> x3, starting transfers between devices: none -> 36 us  [the longest x1 16.9 us: local(): planes = lax.all_to_all(planes, FAR, 0, 0)]
    all_to_all x0 -> x3, waiting for transfers between devices: none -> 25.4 us  [the longest x1 15.2 us: local(): planes = lax.all_to_all(planes, FAR, 0, 0)]
    dot_general x34 -> x0, matrix products: 13.9 us -> none  [the longest x5 2.28 us: banded(): jnp.einsum('kis,ismj->kimj', values.astype(jnp.float32), onehot, precisio...]
    pallas_call x0 -> x7, Pallas kernels: none -> 9.74 us  [kernel_call(): pl.pallas_call(body, out_shape=tuple(outs), in_specs=specs, out_specs=tup...]
    ppermute x8, waiting for transfers between devices: 10.3 us -> 19.7 us  [shift(): return lax.ppermute(cells, axes, pairs)]
  transfers between devices with their start and end apart: 9 -> 11, of which waited for: 3 -> 7; matrix products, arithmetic and copies ran while one was open for 1% -> 2% of each run, Pallas kernels for 0% -> 4%
where the time goes in v2:
time: 130 us; the launch traced here: 129 us
  starting transfers between devices  62.7 us (48%)
  waiting for transfers between devices  45.1 us (35%)
  Pallas kernels  9.74 us (7%)
  local copies, waits for them, and re-layouts  8.01 us (6%)
  other arithmetic  2.54 us (2%)
    ppermute x8, starting transfers between devices, shift(): return lax.ppermute(cells, axes, pairs)  26.7 us
    ppermute x8, waiting for transfers between devices, shift(): return lax.ppermute(cells, axes, pairs)  19.7 us
    all_to_all x1, starting transfers between devices, local(): planes = lax.all_to_all(planes, FAR, 0, 0)  16.9 us
    all_to_all x1, waiting for transfers between devices, local(): planes = lax.all_to_all(planes, FAR, 0, 0)  15.2 us
    all_to_all x1, starting transfers between devices, local(): shares = lax.all_to_all(packed.reshape(near, -1, LANES), NEAR, 0, 0)  11.3 us
    pallas_call x7, Pallas kernels, kernel_call(): pl.pallas_call(body, out_shape=tuple(outs), in_specs=specs, out_specs=tup...  9.74 us
    all_to_all x1, starting transfers between devices, local(): whole = lax.all_to_all(copies, NEAR, 0, 0)  7.72 us
    all_to_all x1, waiting for transfers between devices, local(): shares = lax.all_to_all(packed.reshape(near, -1, LANES), NEAR, 0, 0)  6.27 us
  transfers between devices with their start and end apart: 11, of which 7 were waited for; matrix products, arithmetic and copies ran while one was open for 2% of the time, Pallas kernels for 4%

profile of v2, /device:TPU:1, one launch (start us, length us, event | category | flops | bytes accessed | tf_op | source)
XLA Modules:
  0.0 129.1 jit_solution(12336166129996801418)
XLA Ops:
  1.4 1.3 collective-permute-start.1
  2.7 4.6 %collective-permute-start = (bf16[2,32,256]{2,1,0:T(8,128)(2,1)S(1)}, bf16[2,32,256]{2,1,0:T(8,128)(2,1)S(1)}, u32[]{:S(2)}, u32[]{:S(2)}) collective-permute-start(bf16[2,32,256]{2,1,0:T(8,128)(2,1)S(1)} %get-tuple-element.38), channel_id=1, source_target_pairs={{0,32},{32,64},{64,96},{96,128},{128,160},{160,192},{192,224},{224... | collective-permute-start | bytes 98312 | tf_op jit(solution)/shard_map/ppermute | solution.py:239
  9.6 4.6 %collective-permute-start.2 = (bf16[12,8,256]{2,1,0:T(8,128)(2,1)S(1)}, bf16[12,8,256]{2,1,0:T(8,128)(2,1)S(1)}, u32[]{:S(2)}, u32[]{:S(2)}) collective-permute-start(bf16[12,8,256]{2,1,0:T(8,128)(2,1)S(1)} %pad_maximum_fusion.2), channel_id=1, source_target_pairs={{0,1},{1,2},{2,3},{3,4},{4,5},{5,6},{6,7},{7,8},{8,9},{9,10},{10,1... | collective-permute-start | bytes 147464 | tf_op jit(solution)/shard_map/ppermute | solution.py:239
  14.1 6.1 %collective-permute-start.3 = (bf16[12,8,256]{2,1,0:T(8,128)(2,1)S(1)}, bf16[12,8,256]{2,1,0:T(8,128)(2,1)S(1)}, u32[]{:S(2)}, u32[]{:S(2)}) collective-permute-start(bf16[12,8,256]{2,1,0:T(8,128)(2,1)S(1)} %pad_maximum_fusion.3), channel_id=1, source_target_pairs={{0,31},{1,0},{2,1},{3,2},{4,3},{5,4},{6,5},{7,6},{8,7},{9,8},{10,9... | collective-permute-start | bytes 147464 | tf_op jit(solution)/shard_map/ppermute | solution.py:239
  20.3 1.0 copy-done.5
  22.2 2.9 %prepare.1 = (bf16[768,256]{1,0:T(8,128)(2,1)S(1)}, bf16[768,256]{1,0:T(8,128)(2,1)S(1)}, f32[256,1024]{1,0:T(8,128)S(1)}) custom-call(s32[320]{0:T(512)S(1)} %reshape.30.offset_ref, f32[960]{0:T(1024)S(1)} %reshape.38.value_ref, bf16[256,256]{1,0:T(8,128)(2,1)S(1)} %bitcast.5, bf16[1024,256]{1,0:T(8,128)(2,1)S(1)} %copy-done.5), custom_call_target="tpu_custom_call" | custom-call | flops 536870912 | bytes 2495488 | tf_op jit(solution)/shard_map/prepare/pallas_call | solution.py:35
  25.1 2.3 %main.1 = (bf16[5632,128]{1,0:T(8,128)(2,1)S(1)}, bf16[256,1024]{1,0:T(8,128)(2,1)S(1)}, bf16[256,256]{1,0:T(8,128)(2,1)S(1)}) custom-call(bf16[768,256]{1,0:T(8,128)(2,1)S(1)} %get-tuple-element.18.high_ref, bf16[768,256]{1,0:T(8,128)(2,1)S(1)} %get-tuple-element.19.low_ref, bf16[2,32,256]{2,1,0:T(8,128)(2,1)S(1)} %collective-permute-done.top_ref, ...), custom_call_target="tpu_custom_call" | custom-call | flops 536870912 | bytes 5275648 | tf_op jit(solution)/shard_map/main/pallas_call | solution.py:35
  27.5 1.1 copy-done.2
  29.4 11.3 %all-to-all-start = ((bf16[64,88,128]{2,1,0:T(8,128)(2,1)}), bf16[64,88,128]{2,1,0:T(8,128)(2,1)S(1)}, u32[]{:S(2)}, u32[]{:S(2)}) async-start(bf16[64,88,128]{2,1,0:T(8,128)(2,1)} %bitcast.4), calls=%async_computation | async-start | bytes 2883584 | tf_op jit(solution)/shard_map/all_to_all | solution.py:290
  41.8 1.7 %adjoint.1 = (bf16[12,8,256]{2,1,0:T(8,128)(2,1)S(1)}, bf16[12,8,256]{2,1,0:T(8,128)(2,1)S(1)}, f32[12,32,256]{2,1,0:T(8,128)S(1)}, bf16[8,32,256]{2,1,0:T(8,128)(2,1)}) custom-call(bf16[256,256]{1,0:T(8,128)(2,1)S(1)} %get-tuple-element.21.grad_ref, bf16[3,256,256]{2,1,0:T(8,128)(2,1)S(1)} %copy-done.1, bf16[768,256]{1,0:T(8,128)(2,1)S(1)} %get-tuple-element.18.high_ref, ...), custom_call_target="tpu_custom_call" | custom-call | flops 268435456 | bytes 3112960 | tf_op jit(solution)/shard_map/adjoint/pallas_call | solution.py:35
  44.2 3.7 %collective-permute-start.4 = (bf16[12,8,256]{2,1,0:T(8,128)(2,1)S(1)}, bf16[12,8,256]{2,1,0:T(8,128)(2,1)S(1)}, u32[]{:S(2)}, u32[]{:S(2)}) collective-permute-start(bf16[12,8,256]{2,1,0:T(8,128)(2,1)S(1)} %get-tuple-element.25), channel_id=1, source_target_pairs={{0,1},{1,2},{2,3},{3,4},{4,5},{5,6},{6,7},{7,8},{8,9},{9,10},{10,1... | collective-permute-start | bytes 147464 | tf_op jit(solution)/shard_map/ppermute | solution.py:239
  47.9 1.9 %collective-permute-start.5 = (bf16[12,8,256]{2,1,0:T(8,128)(2,1)S(1)}, bf16[12,8,256]{2,1,0:T(8,128)(2,1)S(1)}, u32[]{:S(2)}, u32[]{:S(2)}) collective-permute-start(bf16[12,8,256]{2,1,0:T(8,128)(2,1)S(1)} %get-tuple-element.26), channel_id=1, source_target_pairs={{0,31},{1,0},{2,1},{3,2},{4,3},{5,4},{6,5},{7,6},{8,7},{9,8},{10,9... | collective-permute-start | bytes 147464 | tf_op jit(solution)/shard_map/ppermute | solution.py:239
  49.8 1.6 %collective-permute-done.4.left_ref.refs_0_ = bf16[12,8,256]{2,1,0:T(8,128)(2,1)S(1)} collective-permute-done((bf16[12,8,256]{2,1,0:T(8,128)(2,1)S(1)}, bf16[12,8,256]{2,1,0:T(8,128)(2,1)S(1)}, u32[]{:S(2)}, u32[]{:S(2)}) %collective-permute-start.4) | collective-permute-done | bytes 49184 | tf_op jit(solution)/shard_map/ppermute | solution.py:239
  51.4 5.3 %collective-permute-done.5.right_ref.refs_1_ = bf16[12,8,256]{2,1,0:T(8,128)(2,1)S(1)} collective-permute-done((bf16[12,8,256]{2,1,0:T(8,128)(2,1)S(1)}, bf16[12,8,256]{2,1,0:T(8,128)(2,1)S(1)}, u32[]{:S(2)}, u32[]{:S(2)}) %collective-permute-start.5) | collective-permute-done | bytes 49184 | tf_op jit(solution)/shard_map/ppermute | solution.py:239
  56.7 6.3 %all-to-all-done.parts_ref = bf16[64,88,128]{2,1,0:T(8,128)(2,1)S(1)} async-done(((bf16[64,88,128]{2,1,0:T(8,128)(2,1)}), bf16[64,88,128]{2,1,0:T(8,128)(2,1)S(1)}, u32[]{:S(2)}, u32[]{:S(2)}) %all-to-all-start) | async-done | bytes 1441824 | tf_op jit(solution)/shard_map/all_to_all | solution.py:290
  63.9 16.9 %all-to-all-start.1 = ((bf16[8,88,128]{2,1,0:T(8,128)(2,1)}), bf16[8,88,128]{2,1,0:T(8,128)(2,1)S(1)}, u32[]{:S(2)}, u32[]{:S(2)}) async-start(bf16[8,88,128]{2,1,0:T(8,128)(2,1)} %sum_and_copy.2), calls=%async_computation.1 | async-start | bytes 360448 | tf_op jit(solution)/shard_map/all_to_all | solution.py:313
  80.8 15.2 %all-to-all-done.1.parts_ref = bf16[8,88,128]{2,1,0:T(8,128)(2,1)S(1)} async-done(((bf16[8,88,128]{2,1,0:T(8,128)(2,1)}), bf16[8,88,128]{2,1,0:T(8,128)(2,1)S(1)}, u32[]{:S(2)}, u32[]{:S(2)}) %all-to-all-start.1) | async-done | bytes 180256 | tf_op jit(solution)/shard_map/all_to_all | solution.py:313
  96.0 1.3 sum_and_copy.3
  97.3 7.7 %all-to-all-start.2 = ((bf16[64,88,128]{2,1,0:T(8,128)(2,1)}), bf16[64,88,128]{2,1,0:T(8,128)(2,1)S(1)}, u32[]{:S(2)}, u32[]{:S(2)}) async-start(bf16[64,88,128]{2,1,0:T(8,128)(2,1)} %sum_and_copy.3), calls=%async_computation.2 | async-start | bytes 2883584 | tf_op jit(solution)/shard_map/all_to_all | solution.py:326
  105.0 3.3 %collective-permute-start.6 = (bf16[2,32,256]{2,1,0:T(8,128)(2,1)S(1)}, bf16[2,32,256]{2,1,0:T(8,128)(2,1)S(1)}, u32[]{:S(2)}, u32[]{:S(2)}) collective-permute-start(bf16[2,32,256]{2,1,0:T(8,128)(2,1)S(1)} %get-tuple-element.28), channel_id=1, source_target_pairs={{0,32},{32,64},{64,96},{96,128},{128,160},{160,192},{192,224},{224... | collective-permute-start | bytes 98312 | tf_op jit(solution)/shard_map/ppermute | solution.py:239
  108.3 1.3 %collective-permute-start.7 = (bf16[2,32,256]{2,1,0:T(8,128)(2,1)S(1)}, bf16[2,32,256]{2,1,0:T(8,128)(2,1)S(1)}, u32[]{:S(2)}, u32[]{:S(2)}) collective-permute-start(bf16[2,32,256]{2,1,0:T(8,128)(2,1)S(1)} %get-tuple-element.29), channel_id=1, source_target_pairs={{32,0},{64,32},{96,64},{128,96},{160,128},{192,160},{224,192},{256... | collective-permute-start | bytes 98312 | tf_op jit(solution)/shard_map/ppermute | solution.py:239
  109.6 10.9 %collective-permute-done.6.above_ref = bf16[2,32,256]{2,1,0:T(8,128)(2,1)S(1)} collective-permute-done((bf16[2,32,256]{2,1,0:T(8,128)(2,1)S(1)}, bf16[2,32,256]{2,1,0:T(8,128)(2,1)S(1)}, u32[]{:S(2)}, u32[]{:S(2)}) %collective-permute-start.6) | collective-permute-done | bytes 32800 | tf_op jit(solution)/shard_map/ppermute | solution.py:239
  120.4 2.0 %collective-permute-done.7.below_ref = bf16[2,32,256]{2,1,0:T(8,128)(2,1)S(1)} collective-permute-done((bf16[2,32,256]{2,1,0:T(8,128)(2,1)S(1)}, bf16[2,32,256]{2,1,0:T(8,128)(2,1)S(1)}, u32[]{:S(2)}, u32[]{:S(2)}) %collective-permute-start.7) | collective-permute-done | bytes 32800 | tf_op jit(solution)/shard_map/ppermute | solution.py:239
  123.1 4.0 %all-to-all-done.2 = bf16[64,88,128]{2,1,0:T(8,128)(2,1)S(1)} async-done(((bf16[64,88,128]{2,1,0:T(8,128)(2,1)}), bf16[64,88,128]{2,1,0:T(8,128)(2,1)S(1)}, u32[]{:S(2)}, u32[]{:S(2)}) %all-to-all-start.2) | async-done | bytes 1441824 | tf_op jit(solution)/shard_map/all_to_all | solution.py:326
  (57 shorter events, 10.0 us)
Async XLA Ops:
  0.6 8.4 %copy-start = (s32[128,5,8]{0,2,1:T(8,128)S(1)}, s32[128,5,8]{0,2,1:T(8,128)}, u32[]{:S(2)}) copy-start(s32[128,5,8]{0,2,1:T(8,128)} %param.8) | copy-start | bytes 61444
  1.4 8.1 %collective-permute-start.1 = (bf16[2,32,256]{2,1,0:T(8,128)(2,1)S(1)}, bf16[2,32,256]{2,1,0:T(8,128)(2,1)S(1)}, u32[]{:S(2)}, u32[]{:S(2)}) collective-permute-start(bf16[2,32,256]{2,1,0:T(8,128)(2,1)S(1)} %get-tuple-element.37), channel_id=1, source_target_pairs={{32,0},{64,32},{96,64},{128,96},{160,128},{192,160},{224,192},{256... | collective-permute-start | bytes 98312 | tf_op jit(solution)/shard_map/ppermute | solution.py:239
  2.7 6.8 %collective-permute-start = (bf16[2,32,256]{2,1,0:T(8,128)(2,1)S(1)}, bf16[2,32,256]{2,1,0:T(8,128)(2,1)S(1)}, u32[]{:S(2)}, u32[]{:S(2)}) collective-permute-start(bf16[2,32,256]{2,1,0:T(8,128)(2,1)S(1)} %get-tuple-element.38), channel_id=1, source_target_pairs={{0,32},{32,64},{64,96},{96,128},{128,160},{160,192},{192,224},{224... | collective-permute-start | bytes 98312 | tf_op jit(solution)/shard_map/ppermute | solution.py:239
  7.3 17.8 %copy-start.1 = (bf16[3,256,256]{2,1,0:T(8,128)(2,1)S(1)}, bf16[3,256,256]{2,1,0:T(8,128)(2,1)}, u32[]{:S(2)}) copy-start(bf16[3,256,256]{2,1,0:T(8,128)(2,1)} %mix_ref.3) | copy-start | bytes 1179652
  7.3 17.8 %copy-start.3 = (bf16[8,32,256]{2,1,0:T(8,128)(2,1)S(1)}, bf16[8,32,256]{2,1,0:T(8,128)(2,1)}, u32[]{:S(2)}) copy-start(bf16[8,32,256]{2,1,0:T(8,128)(2,1)} %state_ref.3) | copy-start | bytes 393220
  7.3 17.8 %copy-start.4 = (bf16[256,1024]{1,0:T(8,128)(2,1)S(1)}, bf16[256,1024]{1,0:T(8,128)(2,1)}, u32[]{:S(2)}) copy-start(bf16[256,1024]{1,0:T(8,128)(2,1)} %in_ref.1) | copy-start | bytes 1572868
  9.6 15.5 %collective-permute-start.2 = (bf16[12,8,256]{2,1,0:T(8,128)(2,1)S(1)}, bf16[12,8,256]{2,1,0:T(8,128)(2,1)S(1)}, u32[]{:S(2)}, u32[]{:S(2)}) collective-permute-start(bf16[12,8,256]{2,1,0:T(8,128)(2,1)S(1)} %pad_maximum_fusion.2), channel_id=1, source_target_pairs={{0,1},{1,2},{2,3},{3,4},{4,5},{5,6},{6,7},{7,8},{8,9},{9,10},{10,1... | collective-permute-start | bytes 147464 | tf_op jit(solution)/shard_map/ppermute | solution.py:239
  14.1 10.9 %collective-permute-start.3 = (bf16[12,8,256]{2,1,0:T(8,128)(2,1)S(1)}, bf16[12,8,256]{2,1,0:T(8,128)(2,1)S(1)}, u32[]{:S(2)}, u32[]{:S(2)}) collective-permute-start(bf16[12,8,256]{2,1,0:T(8,128)(2,1)S(1)} %pad_maximum_fusion.3), channel_id=1, source_target_pairs={{0,31},{1,0},{2,1},{3,2},{4,3},{5,4},{6,5},{7,6},{8,7},{9,8},{10,9... | collective-permute-start | bytes 147464 | tf_op jit(solution)/shard_map/ppermute | solution.py:239
  20.3 1.0 copy-start.5
  21.3 0.9 copy-start.9
  27.5 1.1 copy-start.2
  28.6 0.8 copy-start.7
  29.4 11.3 %copy-start.6 = (bf16[1024,256]{1,0:T(8,128)(2,1)S(1)}, bf16[1024,256]{1,0:T(8,128)(2,1)}, u32[]{:S(2)}) copy-start(bf16[1024,256]{1,0:T(8,128)(2,1)} %out_ref.3) | copy-start | bytes 1572868
  29.4 33.5 %all-to-all-start = ((bf16[64,88,128]{2,1,0:T(8,128)(2,1)}), bf16[64,88,128]{2,1,0:T(8,128)(2,1)S(1)}, u32[]{:S(2)}, u32[]{:S(2)}) async-start(bf16[64,88,128]{2,1,0:T(8,128)(2,1)} %bitcast.4), calls=%async_computation | async-start | bytes 2883584 | tf_op jit(solution)/shard_map/all_to_all | solution.py:290
  40.8 1.0 copy-start.8
  44.2 36.6 %copy-start.12 = (f32[12,32,256]{2,1,0:T(8,128)S(1)}, f32[12,32,256]{2,1,0:T(8,128)}, u32[]{:S(2)}) copy-start(f32[12,32,256]{2,1,0:T(8,128)} %copy-done.11) | copy-start | bytes 1179652
  44.2 7.2 %collective-permute-start.4 = (bf16[12,8,256]{2,1,0:T(8,128)(2,1)S(1)}, bf16[12,8,256]{2,1,0:T(8,128)(2,1)S(1)}, u32[]{:S(2)}, u32[]{:S(2)}) collective-permute-start(bf16[12,8,256]{2,1,0:T(8,128)(2,1)S(1)} %get-tuple-element.25), channel_id=1, source_target_pairs={{0,1},{1,2},{2,3},{3,4},{4,5},{5,6},{6,7},{7,8},{8,9},{9,10},{10,1... | collective-permute-start | bytes 147464 | tf_op jit(solution)/shard_map/ppermute | solution.py:239
  47.9 8.8 %collective-permute-start.5 = (bf16[12,8,256]{2,1,0:T(8,128)(2,1)S(1)}, bf16[12,8,256]{2,1,0:T(8,128)(2,1)S(1)}, u32[]{:S(2)}, u32[]{:S(2)}) collective-permute-start(bf16[12,8,256]{2,1,0:T(8,128)(2,1)S(1)} %get-tuple-element.26), channel_id=1, source_target_pairs={{0,31},{1,0},{2,1},{3,2},{4,3},{5,4},{6,5},{7,6},{8,7},{9,8},{10,9... | collective-permute-start | bytes 147464 | tf_op jit(solution)/shard_map/ppermute | solution.py:239
  63.9 32.1 %all-to-all-start.1 = ((bf16[8,88,128]{2,1,0:T(8,128)(2,1)}), bf16[8,88,128]{2,1,0:T(8,128)(2,1)S(1)}, u32[]{:S(2)}, u32[]{:S(2)}) async-start(bf16[8,88,128]{2,1,0:T(8,128)(2,1)} %sum_and_copy.2), calls=%async_computation.1 | async-start | bytes 360448 | tf_op jit(solution)/shard_map/all_to_all | solution.py:313
  97.2 25.2 %copy-start.10 = (bf16[8,32,256]{2,1,0:T(8,128)(2,1)S(1)}, bf16[8,32,256]{2,1,0:T(8,128)(2,1)}, u32[]{:S(2)}) copy-start(bf16[8,32,256]{2,1,0:T(8,128)(2,1)} %cot_ref.1) | copy-start | bytes 393220
  97.3 29.8 %all-to-all-start.2 = ((bf16[64,88,128]{2,1,0:T(8,128)(2,1)}), bf16[64,88,128]{2,1,0:T(8,128)(2,1)S(1)}, u32[]{:S(2)}, u32[]{:S(2)}) async-start(bf16[64,88,128]{2,1,0:T(8,128)(2,1)} %sum_and_copy.3), calls=%async_computation.2 | async-start | bytes 2883584 | tf_op jit(solution)/shard_map/all_to_all | solution.py:326
  105.0 15.5 %collective-permute-start.6 = (bf16[2,32,256]{2,1,0:T(8,128)(2,1)S(1)}, bf16[2,32,256]{2,1,0:T(8,128)(2,1)S(1)}, u32[]{:S(2)}, u32[]{:S(2)}) collective-permute-start(bf16[2,32,256]{2,1,0:T(8,128)(2,1)S(1)} %get-tuple-element.28), channel_id=1, source_target_pairs={{0,32},{32,64},{64,96},{96,128},{128,160},{160,192},{192,224},{224... | collective-permute-start | bytes 98312 | tf_op jit(solution)/shard_map/ppermute | solution.py:239
  108.3 14.1 %collective-permute-start.7 = (bf16[2,32,256]{2,1,0:T(8,128)(2,1)S(1)}, bf16[2,32,256]{2,1,0:T(8,128)(2,1)S(1)}, u32[]{:S(2)}, u32[]{:S(2)}) collective-permute-start(bf16[2,32,256]{2,1,0:T(8,128)(2,1)S(1)} %get-tuple-element.29), channel_id=1, source_target_pairs={{32,0},{64,32},{96,64},{128,96},{160,128},{192,160},{224,192},{256... | collective-permute-start | bytes 98312 | tf_op jit(solution)/shard_map/ppermute | solution.py:239
  127.3 1.7 %copy-start.13 = (bf16[256,1024]{1,0:T(8,128)(2,1)}, bf16[256,1024]{1,0:T(8,128)(2,1)S(1)}, u32[]{:S(2)}) copy-start(bf16[256,1024]{1,0:T(8,128)(2,1)S(1)} %slice_dynamic-update-slice_fusion) | copy-start | bytes 1572868
  (1 other events, 0.7 us)

commit v3 on v2

v3 whole, which is shorter than its diff:
```python
import functools
import math

import jax
import jax.numpy as jnp
from jax import lax
from jax.experimental import pallas as pl
from jax.experimental.pallas import tpu as pltpu
from jax.sharding import Mesh
from jax.sharding import PartitionSpec as P

RAD = 2
WIDE = 8
LAGS = 2 * RAD + 1

FINE = (("z_hi", 4), ("x", 4), ("z_mid", 2), ("z_low", 2), ("y", 4), ("core", 2))
LAT = ("z_hi", "x")
LON = ("z_mid", "z_low", "y", "core")
CORE = "core"
NEAR = ("x", "z_low", "y")
FAR = ("z_hi", "z_mid")
LANES = 128
CHUNK = 256

ROWS, COLS = ((0,), (0,)), ((1,), (1,))
VMEM = pl.BlockSpec(memory_space=pltpu.VMEM)
SMEM = pl.BlockSpec(memory_space=pltpu.SMEM)
ANY = pl.BlockSpec(memory_space=pl.ANY)


def dot(a, b, contract=((1,), (0,))):
    return lax.dot_general(a, b, (contract, ((), ())), preferred_element_type=jnp.float32)


def kernel_call(body, operands, specs, outs, scratch=(), flops=0, mib=16, name=None):
    moved = sum(x.size * x.dtype.itemsize for x in (*operands, *outs))
    return pl.pallas_call(
        body,
        out_shape=tuple(outs),
        in_specs=specs,
        out_specs=tuple(VMEM for _ in outs),
        scratch_shapes=scratch,
        compiler_params=pltpu.CompilerParams(vmem_limit_bytes=mib << 20),
        cost_estimate=pl.CostEstimate(flops=flops, bytes_accessed=moved, transcendentals=0),
        name=name,
    )(*operands)


def like(shape, dtype):
    return jax.ShapeDtypeStruct(shape, dtype)


def bands_kernel(cols, offset_ref, value_ref, high_ref, low_ref):
    kinds, cycles, lags, slots = 3, high_ref.shape[0] // (3 * cols), LAGS, offset_ref.shape[0]
    slots = slots // (cycles * lags)
    span = cols + 2 * WIDE
    shape = (cols, LANES)
    ahead = lax.broadcasted_iota(jnp.int32, shape, 1) - lax.broadcasted_iota(jnp.int32, shape, 0)

    def cycle(i, carry):
        for start in range(0, high_ref.shape[1], LANES):
            sums = [jnp.zeros(shape, jnp.float32) for _ in range(kinds)]
            for q in range(lags):
                if q * span >= start + LANES or (q + 1) * span <= start:
                    continue
                for s in range(slots):
                    at = (i * lags + q) * slots + s
                    hit = ahead == offset_ref[at] + (q * span + WIDE - start)
                    for k in range(kinds):
                        value = value_ref[k * cycles * lags * slots + at]
                        sums[k] = sums[k] + jnp.where(hit, value, 0.0)
            for k in range(kinds):
                at = pl.ds(pl.multiple_of((i * kinds + k) * cols, cols), cols)
                high = sums[k].astype(jnp.bfloat16)
                high_ref[at, start : start + LANES] = high
                rest = sums[k] - high.astype(jnp.float32)
                low_ref[at, start : start + LANES] = rest.astype(jnp.bfloat16)
        return carry

    lax.fori_loop(0, cycles, cycle, 0)


def by_side(odd, near, far):
    near, far = near.astype(jnp.float32), far.astype(jnp.float32)
    return jnp.where(odd, near, far), jnp.where(odd, far, near)


def by_partner(odd, before, after):
    near, far = jnp.where(odd, before, after), jnp.where(odd, after, before)
    return near.astype(jnp.bfloat16), far.astype(jnp.bfloat16)


def whole_rows(side_ref, near_ref, state_ref, far_ref):
    above, below = [], []
    for r in range(RAD):
        first, second = by_side(side_ref[0] != 0, near_ref[r], far_ref[r])
        above.append(first)
        below.append(second)
    return above + [state_ref[r].astype(jnp.float32) for r in range(state_ref.shape[0])] + below


def gelu_and_slope(x):
    c, a = math.sqrt(2.0 / math.pi), 0.044715
    square = x * x
    t = jnp.tanh(c * (x + a * (square * x)))
    cdf = 0.5 * (1.0 + t)
    slope = cdf + (0.5 * x) * (1.0 - t * t) * (c * (1.0 + (3.0 * a) * square))
    return x * cdf, slope


def fetch(sources, targets, sems):
    copies = [
        pltpu.make_async_copy(source, target, sems.at[i])
        for i, (source, target) in enumerate(zip(sources, targets))
    ]
    for copy in copies:
        copy.start()

    def take(i):
        copies[i].wait()
        return targets[i]

    return take


def main_kernel(
    side_ref, high_ref, low_ref, lat_near_ref, state_ref, lat_far_ref, lon_near_ref, lon_far_ref,
    mix_hbm, in_hbm, out_hbm, cot_hbm, packed_ref, hidden_ref, grad_ref,
    cells_ref, basis_ref, mix_ref, in_ref, out_ref, cot_ref, sems,
):
    take = fetch((mix_hbm, in_hbm, out_hbm, cot_hbm), (mix_ref, in_ref, out_ref, cot_ref), sems)
    rows, cols, channels = state_ref.shape
    span = cols + 2 * WIDE
    kinds = basis_ref.shape[0]
    for r, line in enumerate(whole_rows(side_ref, lat_near_ref, state_ref, lat_far_ref)):
        left, right = by_side(side_ref[1] != 0, lon_near_ref[r], lon_far_ref[r])
        line = jnp.concatenate([left, line, right], axis=0)
        cells_ref[r * span : (r + 1) * span] = line.astype(jnp.bfloat16)
    used = (rows + 2 * RAD) * span
    cells_ref[used:] = jnp.zeros((cells_ref.shape[0] - used, channels), jnp.bfloat16)

    depth = high_ref.shape[1]
    for i in range(rows):
        window = cells_ref[i * span : i * span + depth]
        at = slice(i * kinds * cols, (i + 1) * kinds * cols)
        taken = dot(high_ref[at], window) + dot(low_ref[at], window)
        for k in range(kinds):
            piece = taken[k * cols : (k + 1) * cols].astype(jnp.bfloat16)
            basis_ref[k, i * cols : (i + 1) * cols] = piece
    mix_ref = take(0)
    mixed = sum(dot(basis_ref[k], mix_ref[k]) for k in range(kinds)).astype(jnp.bfloat16)

    in_ref, out_ref = take(1), take(2)
    cot = take(3)[...]
    core, half = side_ref[1], packed_ref.shape[1]

    def pack(matrix, place, height):
        for c in range(0, matrix.shape[1], LANES):
            owner, at = divmod(place + (c // LANES) * height, half)
            slot = core if owner == 0 else 1 - core
            packed_ref[slot, at : at + matrix.shape[0]] = matrix[:, c : c + LANES].astype(jnp.bfloat16)

    units = in_ref.shape[1]
    outer_at, inner_at = 0, units * (channels // LANES)
    basis_at = inner_at + channels * (units // LANES)
    back = jnp.zeros((rows * cols, channels), jnp.float32)
    for c in range(0, units, CHUNK):
        weight = in_ref[:, c : c + CHUNK]
        hidden, slope = gelu_and_slope(dot(mixed, weight))
        hidden = hidden.astype(jnp.bfloat16)
        upstream = dot(cot, out_ref[c : c + CHUNK], COLS)
        grad_pre = (upstream * slope).astype(jnp.bfloat16)
        hidden_ref[:, c : c + CHUNK] = hidden
        back = back + dot(grad_pre, weight, COLS)
        pack(dot(hidden, cot, ROWS), outer_at + c, units)
        pack(dot(mixed, grad_pre, ROWS), inner_at + (c // LANES) * channels, channels)
    grad_mixed = back.astype(jnp.bfloat16)
    grad_ref[...] = grad_mixed
    for k in range(kinds):
        pack(dot(basis_ref[k], grad_mixed, ROWS), basis_at + k * channels, kinds * channels)


def adjoint_kernel(
    side_ref, grad_ref, mix_ref, high_ref, low_ref, near_ref, far_ref, middle_ref, back_ref, landing_ref
):
    tall, cols, channels = middle_ref.shape
    rows, span = tall - 2 * RAD, cols + 2 * WIDE
    kinds = mix_ref.shape[0]
    grad = grad_ref[...]
    for k in range(kinds):
        back_ref[k] = dot(grad, mix_ref[k], COLS).astype(jnp.bfloat16)
    landing_ref[...] = jnp.zeros_like(landing_ref)
    depth = high_ref.shape[1]
    for i in range(rows):
        pieces = [back_ref[k, i * cols : (i + 1) * cols] for k in range(kinds)]
        taken = jnp.concatenate(pieces, axis=0)
        at = slice(i * kinds * cols, (i + 1) * kinds * cols)
        spread = dot(high_ref[at], taken, ROWS) + dot(low_ref[at], taken, ROWS)
        landing_ref[i * span : i * span + depth] += spread
    for r in range(rows + 2 * RAD):
        line = landing_ref[r * span : (r + 1) * span]
        near_ref[r], far_ref[r] = by_partner(side_ref[1] != 0, line[:WIDE], line[WIDE + cols :])
        middle_ref[r] = line[WIDE : WIDE + cols]


def rims_kernel(side_ref, middle_ref, near_ref, far_ref, to_near_ref, to_far_ref, core_ref):
    rows, cols = core_ref.shape[:2]
    lines = []
    for r in range(rows + 2 * RAD):
        left, right = by_side(side_ref[1] != 0, near_ref[r], far_ref[r])
        line = middle_ref[r]
        head, tail = line[:WIDE] + left, line[cols - WIDE :] + right
        lines.append(jnp.concatenate([head, line[WIDE : cols - WIDE], tail], axis=0))
    for r in range(RAD):
        above, below = lines[r], lines[rows + RAD + r]
        to_near_ref[r], to_far_ref[r] = by_partner(side_ref[0] != 0, above, below)
    for r in range(rows):
        core_ref[r] = lines[RAD + r]


def field_kernel(side_ref, cot_ref, core_ref, near_ref, far_ref, field_ref):
    rows = core_ref.shape[0]
    lines = [core_ref[r] for r in range(rows)]
    for r in range(RAD):
        above, below = by_side(side_ref[0] != 0, near_ref[r], far_ref[r])
        lines[r] = lines[r] + above
        lines[rows - RAD + r] = lines[rows - RAD + r] + below
    for r in range(rows):
        field_ref[r] = (cot_ref[r].astype(jnp.float32) + lines[r]).astype(jnp.bfloat16)


def edges_kernel(side_ref, lat_near_ref, state_ref, lat_far_ref, near_ref, far_ref):
    cols = state_ref.shape[1]
    for r, line in enumerate(whole_rows(side_ref, lat_near_ref, state_ref, lat_far_ref)):
        near_ref[r], far_ref[r] = by_partner(side_ref[1] != 0, line[:WIDE], line[cols - WIDE :])


def add_kernel(a_ref, b_ref, sum_ref):
    sum_ref[...] = (a_ref[0].astype(jnp.float32) + b_ref[...].astype(jnp.float32)).astype(jnp.bfloat16)


def tie_kernel(value_ref, *refs):
    refs[-1][...] = value_ref[...]


def tie(value, *later_than):
    return kernel_call(
        tie_kernel,
        (value, *later_than),
        [VMEM] + [ANY] * len(later_than),
        [like(value.shape, value.dtype)],
        name="tie",
    )[0]


def sum_kernel(scale, parts_ref, *refs):
    out_ref = refs[-1]
    total = parts_ref[0].astype(jnp.float32)
    for i in range(1, parts_ref.shape[0]):
        total = total + parts_ref[i].astype(jnp.float32)
    total = (total * scale).astype(out_ref.dtype)
    for i in range(out_ref.shape[0]):
        out_ref[i] = total


def sum_and_copy(parts, scale, copies, *later_than):
    return kernel_call(
        functools.partial(sum_kernel, scale),
        (parts, *later_than),
        [VMEM] + [ANY] * len(later_than),
        [like((copies,) + parts.shape[1:], jnp.bfloat16)],
        flops=parts.size,
        mib=16,
        name="sum_and_copy",
    )[0]


def unpack(whole, shapes):
    outs, start = [], 0
    for rows, cols in shapes:
        pieces = []
        for _ in range(0, cols, LANES):
            pieces.append(whole[start : start + rows])
            start += rows
        outs.append(jnp.concatenate(pieces, axis=1))
    return outs


def block_kernel(hidden_ref, out_ref, state_ref, block_ref):
    rows, cols = state_ref.shape[:2]
    branch = dot(hidden_ref[...], out_ref[...])
    for i in range(rows):
        line = state_ref[i].astype(jnp.float32) + branch[i * cols : (i + 1) * cols]
        block_ref[i] = line.astype(jnp.bfloat16)


def swap(cells, axes, lead, closed):
    count = lax.axis_size(axes)
    pairs = []
    for i in range(lead, count, 2):
        if closed or i + 1 < count:
            pairs += [(i, (i + 1) % count), ((i + 1) % count, i)]
    return lax.ppermute(cells, axes, pairs)


def swap_both(near, far, axes, closed):
    far = swap(far, axes, 1, closed)
    return swap(near, axes, 0, closed), far


def local(
    state_field, support_offsets, kernel_values, basis_weight, weight_in, weight_out, cotangent
):
    rows, cols, channels = state_field.shape
    kinds, units = basis_weight.shape[0], weight_in.shape[1]
    cells, span = rows * cols, cols + 2 * WIDE
    tall = rows + 2 * RAD
    depth = -(-LAGS * span // LANES) * LANES
    near, far = lax.axis_size(NEAR), lax.axis_size(FAR)
    cot_flat = cotangent.reshape(cells, channels)
    f32, bf16 = jnp.float32, jnp.bfloat16

    odd_lat, odd_lon = lax.axis_index(LAT) % 2, lax.axis_index(LON) % 2
    sides = jnp.stack([odd_lat, odd_lon])
    last = rows - RAD
    to_near = lax.dynamic_slice_in_dim(state_field, jnp.where(odd_lat == 0, last, 0), RAD, 0)
    to_far = lax.dynamic_slice_in_dim(state_field, jnp.where(odd_lat == 0, 0, last), RAD, 0)
    lat_near, lat_far = swap_both(to_near, to_far, LAT, False)

    band_start = lax.axis_index(LAT) * rows
    offsets = lax.dynamic_slice_in_dim(support_offsets, band_start, rows, 0)
    values = lax.dynamic_slice_in_dim(kernel_values, band_start, rows, 1).astype(f32)
    band_shape = (rows * kinds * cols, depth)
    high, low = kernel_call(
        functools.partial(bands_kernel, cols),
        (offsets.reshape(-1), values.reshape(-1)),
        [SMEM, SMEM],
        [like(band_shape, bf16), like(band_shape, bf16)],
        flops=8 * cells * channels * units,
        name="bands",
    )
    rim = like((tall, WIDE, channels), bf16)
    to_near, to_far = kernel_call(
        edges_kernel,
        (sides, lat_near, state_field, lat_far),
        [SMEM] + [VMEM] * 3,
        [rim, rim],
        name="edges",
    )
    lon_near, lon_far = swap_both(to_near, to_far, LON, True)
    packed_rows = channels * (2 * units + kinds * channels) // LANES
    core = lax.axis_index(CORE)
    half = like((packed_rows // 2, LANES), bf16)
    packed, hidden, grad_mixed = kernel_call(
        main_kernel,
        (
            sides, high, low, lat_near, state_field, lat_far, lon_near, lon_far,
            basis_weight, weight_in, weight_out, cot_flat,
        ),
        [SMEM] + [VMEM] * 7 + [ANY] * 4,
        [like((2,) + half.shape, bf16), like((cells, units), bf16), like((cells, channels), bf16)],
        [
            pltpu.VMEM((rows * span + depth, channels), bf16),
            pltpu.VMEM((kinds, cells, channels), bf16),
            pltpu.VMEM(basis_weight.shape, bf16),
            pltpu.VMEM(weight_in.shape, bf16),
            pltpu.VMEM(weight_out.shape, bf16),
            pltpu.VMEM(cot_flat.shape, bf16),
            pltpu.SemaphoreType.DMA((4,)),
        ],
        flops=10 * cells * channels * units,
        name="main",
    )

    arrived = swap(packed[1], CORE, 0, True)
    chip = kernel_call(add_kernel, (packed, arrived), [VMEM] * 2, [half], name="add")[0]
    shares = lax.all_to_all(chip.reshape(near, -1, LANES), NEAR, 0, 0)

    to_near, to_far, middle = kernel_call(
        adjoint_kernel,
        (sides, grad_mixed, basis_weight, high, low),
        [SMEM] + [VMEM] * 4,
        [rim, rim, like((tall, cols, channels), f32)],
        [
            pltpu.VMEM((kinds, cells, channels), bf16),
            pltpu.VMEM((rows * span + depth, channels), f32),
        ],
        flops=4 * cells * channels * units,
        name="adjoint",
    )
    near_rim, far_rim = swap_both(to_near, to_far, LON, True)
    planes = sum_and_copy(shares, 1.0, far, near_rim, far_rim)
    planes = lax.all_to_all(planes, FAR, 0, 0)
    edge = like((RAD, cols, channels), bf16)
    to_near, to_far, inside = kernel_call(
        rims_kernel,
        (sides, middle, near_rim, far_rim),
        [SMEM] + [VMEM] * 3,
        [edge, edge, like(state_field.shape, f32)],
        name="rims",
    )
    near_edge, far_edge = swap_both(to_near, to_far, LAT, False)
    scale = 1.0 / math.sqrt(cells * lax.axis_size(LAT) * lax.axis_size(LON))
    copies = sum_and_copy(planes, scale, near, inside)
    (grad_field,) = kernel_call(
        field_kernel,
        (sides, cotangent, inside, near_edge, far_edge),
        [SMEM] + [VMEM] * 4,
        [like(state_field.shape, bf16)],
        name="field",
    )
    (block_out,) = kernel_call(
        block_kernel,
        (hidden, weight_out, state_field),
        [VMEM] * 3,
        [like(state_field.shape, bf16)],
        flops=2 * cells * channels * units,
        name="block",
    )
    mine = lax.all_to_all(copies, NEAR, 0, 0).reshape(-1, LANES)
    mine = tie(mine, near_edge, far_edge, block_out)
    other = swap(mine, CORE, 0, True)
    shapes = ((units, channels), (channels, units), (kinds * channels, channels))
    whole = jnp.concatenate(
        [jnp.where(core == 0, mine, other), jnp.where(core == 0, other, mine)], axis=0
    )
    grad_out, grad_in, grad_basis = unpack(whole, shapes)
    return (block_out, grad_field, grad_basis.reshape(basis_weight.shape), grad_in, grad_out)


def solution(mesh):
    names, sizes = zip(*FINE)
    mesh = Mesh(mesh.devices.reshape(sizes), names)
    return jax.shard_map(
        local,
        mesh=mesh,
        in_specs=(P(LAT, LON, None), P(), P(), P(), P(), P(), P(LAT, LON, None)),
        out_specs=(P(LAT, LON, None), P(LAT, LON, None), P(), P(), P()),
        check_vma=False,
    )
```

time: 130 us -> 119 us (0.915)
  waiting for transfers between devices: 45.1 us -> 29.8 us
  Pallas kernels: 9.74 us -> 14 us
  local copies, waits for them, and re-layouts: 8.01 us -> 4.13 us
  starting transfers between devices: 62.7 us -> 65.4 us
    ppermute x8 -> x10, waiting for transfers between devices: 19.7 us -> 11.3 us  [swap(): return lax.ppermute(cells, axes, pairs)]
    ppermute x8 -> x10, starting transfers between devices: 26.7 us -> 34.3 us  [swap(): return lax.ppermute(cells, axes, pairs)]
    all_to_all x2, waiting for transfers between devices: 10.2 us -> 3.85 us  [the longest x1 3.05 us: local(): mine = lax.all_to_all(copies, NEAR, 0, 0).reshape(-1, LANES)]
    all_to_all x1, starting transfers between devices: 16.9 us -> 12.2 us  [local(): planes = lax.all_to_all(planes, FAR, 0, 0)]
    pallas_call x7 -> x11, Pallas kernels: 9.74 us -> 14 us  [kernel_call(): pl.pallas_call(body, out_shape=tuple(outs), in_specs=specs, out_specs=tup...]
    unnamed x35 -> x29, local copies, waits for them, and re-layouts: 5.83 us -> 2.72 us
    slice x6 -> x2, local copies, waits for them, and re-layouts: 1.72 us -> 0.06 us  [unpack(): pieces.append(whole[start:start + rows])]
  transfers between devices with their start and end apart: 11 -> 13, of which waited for: 7 -> 8; matrix products, arithmetic and copies ran while one was open for 2% -> 1% of each run, Pallas kernels for 4% -> 6%
where the time goes in v3:
time: 119 us; the launch traced here: 117 us
  starting transfers between devices  65.4 us (55%)
  waiting for transfers between devices  29.8 us (25%)
  Pallas kernels  14 us (12%)
  local copies, waits for them, and re-layouts  4.13 us (3%)
  other arithmetic  2.7 us (2%)
    ppermute x10, starting transfers between devices, swap(): return lax.ppermute(cells, axes, pairs)  34.3 us
    all_to_all x1, waiting for transfers between devices, local(): planes = lax.all_to_all(planes, FAR, 0, 0)  14.7 us
    pallas_call x11, Pallas kernels, kernel_call(): pl.pallas_call(body, out_shape=tuple(outs), in_specs=specs, out_specs=tup...  14 us
    all_to_all x1, starting transfers between devices, local(): planes = lax.all_to_all(planes, FAR, 0, 0)  12.2 us
    ppermute x10, waiting for transfers between devices, swap(): return lax.ppermute(cells, axes, pairs)  11.3 us
    all_to_all x1, starting transfers between devices, local(): shares = lax.all_to_all(chip.reshape(near, -1, LANES), NEAR, 0, 0)  9.49 us
    all_to_all x1, starting transfers between devices, local(): mine = lax.all_to_all(copies, NEAR, 0, 0).reshape(-1, LANES)  9.44 us
    all_to_all x1, waiting for transfers between devices, local(): mine = lax.all_to_all(copies, NEAR, 0, 0).reshape(-1, LANES)  3.05 us
  transfers between devices with their start and end apart: 13, of which 8 were waited for; matrix products, arithmetic and copies ran while one was open for 1% of the time, Pallas kernels for 6%

profile of v3, /device:TPU:1, one launch (start us, length us, event | category | flops | bytes accessed | tf_op | source)
XLA Modules:
  0.0 117.0 jit_solution(1683536577892668954)
XLA Ops:
  2.2 6.4 %collective-permute-start = (bf16[2,32,256]{2,1,0:T(8,128)(2,1)S(1)}, bf16[2,32,256]{2,1,0:T(8,128)(2,1)S(1)}, u32[]{:S(2)}, u32[]{:S(2)}) collective-permute-start(bf16[2,32,256]{2,1,0:T(8,128)(2,1)S(1)} %get-tuple-element.38), channel_id=1, source_target_pairs={{0,32},{32,0},{64,96},{96,64},{128,160},{160,128},{192,224},{224,1... | collective-permute-start | bytes 98312 | tf_op jit(solution)/shard_map/ppermute | solution.py:303
  11.5 6.8 %collective-permute-start.2 = (bf16[12,8,256]{2,1,0:T(8,128)(2,1)S(1)}, bf16[12,8,256]{2,1,0:T(8,128)(2,1)S(1)}, u32[]{:S(2)}, u32[]{:S(2)}) collective-permute-start(bf16[12,8,256]{2,1,0:T(8,128)(2,1)S(1)} %get-tuple-element.20), channel_id=1, source_target_pairs={{0,1},{1,0},{2,3},{3,2},{4,5},{5,4},{6,7},{7,6},{8,9},{9,8},{10,11... | collective-permute-start | bytes 147464 | tf_op jit(solution)/shard_map/ppermute | solution.py:303
  18.3 1.9 %collective-permute-start.3 = (bf16[12,8,256]{2,1,0:T(8,128)(2,1)S(1)}, bf16[12,8,256]{2,1,0:T(8,128)(2,1)S(1)}, u32[]{:S(2)}, u32[]{:S(2)}) collective-permute-start(bf16[12,8,256]{2,1,0:T(8,128)(2,1)S(1)} %get-tuple-element.21), channel_id=1, source_target_pairs={{1,2},{2,1},{3,4},{4,3},{5,6},{6,5},{7,8},{8,7},{9,10},{10,9},{11,... | collective-permute-start | bytes 147464 | tf_op jit(solution)/shard_map/ppermute | solution.py:303
  20.2 2.5 %bands.1 = (bf16[768,256]{1,0:T(8,128)(2,1)S(1)}, bf16[768,256]{1,0:T(8,128)(2,1)S(1)}) custom-call(s32[320]{0:T(512)S(1)} %reshape.30.offset_ref, f32[960]{0:T(1024)S(1)} %reshape.38.value_ref), custom_call_target="tpu_custom_call" | custom-call | flops 536870912 | bytes 791552 | tf_op jit(solution)/shard_map/bands/pallas_call | solution.py:37
  22.8 0.9 collective-permute-done.3.lon_far_ref
  23.7 3.6 %main.1 = (bf16[2,2816,128]{2,1,0:T(8,128)(2,1)S(1)}, bf16[256,1024]{1,0:T(8,128)(2,1)S(1)}, bf16[256,256]{1,0:T(8,128)(2,1)S(1)}) custom-call(s32[2]{0:T(128)S(1)} %pad_add_fusion.side_ref, bf16[768,256]{1,0:T(8,128)(2,1)S(1)} %get-tuple-element.18.high_ref, bf16[768,256]{1,0:T(8,128)(2,1)S(1)} %get-tuple-element.19.low_ref, ...), custom_call_target="tpu_custom_call" | custom-call | flops 671088640 | bytes 4751368 | tf_op jit(solution)/shard_map/main/pallas_call | solution.py:37
  27.4 5.8 %collective-permute-start.8 = (bf16[2816,128]{1,0:T(8,128)(2,1)S(1)}, bf16[2816,128]{1,0:T(8,128)(2,1)S(1)}, u32[]{:S(2)}, u32[]{:S(2)}) collective-permute-start(bf16[2816,128]{1,0:T(8,128)(2,1)S(1)} %slice_bitcast_fusion), channel_id=1, source_target_pairs={{0,1},{1,0},{2,3},{3,2},{4,5},{5,4},{6,7},{7,6},{8,9},{9,8},{10,11... | collective-permute-start | bytes 2162696 | tf_op jit(solution)/shard_map/ppermute | solution.py:303
  33.3 1.8 %collective-permute-done.8.b_ref = bf16[2816,128]{1,0:T(8,128)(2,1)S(1)} collective-permute-done((bf16[2816,128]{1,0:T(8,128)(2,1)S(1)}, bf16[2816,128]{1,0:T(8,128)(2,1)S(1)}, u32[]{:S(2)}, u32[]{:S(2)}) %collective-permute-start.8) | collective-permute-done | bytes 720928 | tf_op jit(solution)/shard_map/ppermute | solution.py:303
  35.0 1.0 add.36
  36.1 9.5 %all-to-all-start = ((bf16[32,88,128]{2,1,0:T(8,128)(2,1)}), bf16[32,88,128]{2,1,0:T(8,128)(2,1)S(1)}, u32[]{:S(2)}, u32[]{:S(2)}) async-start(bf16[32,88,128]{2,1,0:T(8,128)(2,1)} %bitcast.4), calls=%async_computation | async-start | bytes 1441792 | tf_op jit(solution)/shard_map/all_to_all | solution.py:377
  45.6 1.7 %adjoint.1 = (bf16[12,8,256]{2,1,0:T(8,128)(2,1)S(1)}, bf16[12,8,256]{2,1,0:T(8,128)(2,1)S(1)}, f32[12,32,256]{2,1,0:T(8,128)S(1)}) custom-call(s32[2]{0:T(128)S(1)} %pad_add_fusion.side_ref, bf16[256,256]{1,0:T(8,128)(2,1)S(1)} %get-tuple-element.23.grad_ref, bf16[3,256,256]{2,1,0:T(8,128)(2,1)S(1)} %copy-done.4, ...), custom_call_target="tpu_custom_call" | custom-call | flops 268435456 | bytes 1802248 | tf_op jit(solution)/shard_map/adjoint/pallas_call | solution.py:37
  48.0 2.7 %collective-permute-start.4 = (bf16[12,8,256]{2,1,0:T(8,128)(2,1)S(1)}, bf16[12,8,256]{2,1,0:T(8,128)(2,1)S(1)}, u32[]{:S(2)}, u32[]{:S(2)}) collective-permute-start(bf16[12,8,256]{2,1,0:T(8,128)(2,1)S(1)} %get-tuple-element.25), channel_id=1, source_target_pairs={{0,1},{1,0},{2,3},{3,2},{4,5},{5,4},{6,7},{7,6},{8,9},{9,8},{10,11... | collective-permute-start | bytes 147464 | tf_op jit(solution)/shard_map/ppermute | solution.py:303
  50.7 3.3 %collective-permute-start.5 = (bf16[12,8,256]{2,1,0:T(8,128)(2,1)S(1)}, bf16[12,8,256]{2,1,0:T(8,128)(2,1)S(1)}, u32[]{:S(2)}, u32[]{:S(2)}) collective-permute-start(bf16[12,8,256]{2,1,0:T(8,128)(2,1)S(1)} %get-tuple-element.26), channel_id=1, source_target_pairs={{1,2},{2,1},{3,4},{4,3},{5,6},{6,5},{7,8},{8,7},{9,10},{10,9},{11,... | collective-permute-start | bytes 147464 | tf_op jit(solution)/shard_map/ppermute | solution.py:303
  54.1 3.0 %collective-permute-done.5.far_ref.refs_1_ = bf16[12,8,256]{2,1,0:T(8,128)(2,1)S(1)} collective-permute-done((bf16[12,8,256]{2,1,0:T(8,128)(2,1)S(1)}, bf16[12,8,256]{2,1,0:T(8,128)(2,1)S(1)}, u32[]{:S(2)}, u32[]{:S(2)}) %collective-permute-start.5) | collective-permute-done | bytes 49184 | tf_op jit(solution)/shard_map/ppermute | solution.py:303
  58.7 12.2 %all-to-all-start.1 = ((bf16[8,88,128]{2,1,0:T(8,128)(2,1)}), bf16[8,88,128]{2,1,0:T(8,128)(2,1)S(1)}, u32[]{:S(2)}, u32[]{:S(2)}) async-start(bf16[8,88,128]{2,1,0:T(8,128)(2,1)} %sum_and_copy.2), calls=%async_computation.1 | async-start | bytes 360448 | tf_op jit(solution)/shard_map/all_to_all | solution.py:393
  71.5 14.7 %all-to-all-done.1.parts_ref = bf16[8,88,128]{2,1,0:T(8,128)(2,1)S(1)} async-done(((bf16[8,88,128]{2,1,0:T(8,128)(2,1)}), bf16[8,88,128]{2,1,0:T(8,128)(2,1)S(1)}, u32[]{:S(2)}, u32[]{:S(2)}) %all-to-all-start.1) | async-done | bytes 180256 | tf_op jit(solution)/shard_map/all_to_all | solution.py:393
  86.1 0.9 sum_and_copy.3
  87.0 9.4 %all-to-all-start.2 = ((bf16[32,88,128]{2,1,0:T(8,128)(2,1)}), bf16[32,88,128]{2,1,0:T(8,128)(2,1)S(1)}, u32[]{:S(2)}, u32[]{:S(2)}) async-start(bf16[32,88,128]{2,1,0:T(8,128)(2,1)} %sum_and_copy.3), calls=%async_computation.2 | async-start | bytes 1441792 | tf_op jit(solution)/shard_map/all_to_all | solution.py:420
  96.5 3.1 %collective-permute-start.6 = (bf16[2,32,256]{2,1,0:T(8,128)(2,1)S(1)}, bf16[2,32,256]{2,1,0:T(8,128)(2,1)S(1)}, u32[]{:S(2)}, u32[]{:S(2)}) collective-permute-start(bf16[2,32,256]{2,1,0:T(8,128)(2,1)S(1)} %get-tuple-element.28), channel_id=1, source_target_pairs={{0,32},{32,0},{64,96},{96,64},{128,160},{160,128},{192,224},{224,1... | collective-permute-start | bytes 98312 | tf_op jit(solution)/shard_map/ppermute | solution.py:303
  100.3 1.0 block.1.refs_2_
  101.3 5.0 %collective-permute-done.6.near_ref.refs_0_ = bf16[2,32,256]{2,1,0:T(8,128)(2,1)S(1)} collective-permute-done((bf16[2,32,256]{2,1,0:T(8,128)(2,1)S(1)}, bf16[2,32,256]{2,1,0:T(8,128)(2,1)S(1)}, u32[]{:S(2)}, u32[]{:S(2)}) %collective-permute-start.6) | collective-permute-done | bytes 32800 | tf_op jit(solution)/shard_map/ppermute | solution.py:303
  106.2 3.0 %all-to-all-done.2 = bf16[32,88,128]{2,1,0:T(8,128)(2,1)S(1)} async-done(((bf16[32,88,128]{2,1,0:T(8,128)(2,1)}), bf16[32,88,128]{2,1,0:T(8,128)(2,1)S(1)}, u32[]{:S(2)}, u32[]{:S(2)}) %all-to-all-start.2) | async-done | bytes 720928 | tf_op jit(solution)/shard_map/all_to_all | solution.py:420
  110.2 2.9 %collective-permute-start.9 = (bf16[2816,128]{1,0:T(8,128)(2,1)S(1)}, bf16[2816,128]{1,0:T(8,128)(2,1)S(1)}, u32[]{:S(2)}, u32[]{:S(2)}) collective-permute-start(bf16[2816,128]{1,0:T(8,128)(2,1)S(1)} %tie.1), channel_id=1, source_target_pairs={{0,1},{1,0},{2,3},{3,2},{4,5},{5,4},{6,7},{7,6},{8,9},{9,8},{10,11... | collective-permute-start | bytes 2162696 | tf_op jit(solution)/shard_map/ppermute | solution.py:303
  113.2 1.2 %field.1 = bf16[8,32,256]{2,1,0:T(8,128)(2,1)} custom-call(s32[2]{0:T(128)S(1)} %pad_add_fusion.side_ref, bf16[8,32,256]{2,1,0:T(8,128)(2,1)S(1)} %copy-done.6, f32[8,32,256]{2,1,0:T(8,128)S(1)} %get-tuple-element.27.core_ref.refs_0_, bf16[2,32,256]{2,1,0:T(8,128)(2,1)S(1)} %collective-permute-done.6.near_ref.refs_0_, ...), custom_call_target="tpu_custom_call" | custom-call | bytes 589832 | tf_op jit(solution)/shard_map/field/pallas_call | solution.py:37
  (57 shorter events, 11.5 us)
Async XLA Ops:
  0.6 8.0 %copy-start = (s32[128,5,8]{0,2,1:T(8,128)S(1)}, s32[128,5,8]{0,2,1:T(8,128)}, u32[]{:S(2)}) copy-start(s32[128,5,8]{0,2,1:T(8,128)} %param.8) | copy-start | bytes 61444
  0.7 23.0 %copy-start.1 = (bf16[1024,256]{1,0:T(8,128)(2,1)S(1)}, bf16[1024,256]{1,0:T(8,128)(2,1)}, u32[]{:S(2)}) copy-start(bf16[1024,256]{1,0:T(8,128)(2,1)} %out_ref.1) | copy-start | bytes 1572868
  0.7 23.0 %copy-start.3 = (bf16[8,32,256]{2,1,0:T(8,128)(2,1)S(1)}, bf16[8,32,256]{2,1,0:T(8,128)(2,1)}, u32[]{:S(2)}) copy-start(bf16[8,32,256]{2,1,0:T(8,128)(2,1)} %state_ref.5) | copy-start | bytes 393220
  1.5 8.5 %collective-permute-start.1 = (bf16[2,32,256]{2,1,0:T(8,128)(2,1)S(1)}, bf16[2,32,256]{2,1,0:T(8,128)(2,1)S(1)}, u32[]{:S(2)}, u32[]{:S(2)}) collective-permute-start(bf16[2,32,256]{2,1,0:T(8,128)(2,1)S(1)} %get-tuple-element.37), channel_id=1, source_target_pairs={{32,64},{64,32},{96,128},{128,96},{160,192},{192,160},{224,256},{2... | collective-permute-start | bytes 98312 | tf_op jit(solution)/shard_map/ppermute | solution.py:303
  2.2 7.8 %collective-permute-start = (bf16[2,32,256]{2,1,0:T(8,128)(2,1)S(1)}, bf16[2,32,256]{2,1,0:T(8,128)(2,1)S(1)}, u32[]{:S(2)}, u32[]{:S(2)}) collective-permute-start(bf16[2,32,256]{2,1,0:T(8,128)(2,1)S(1)} %get-tuple-element.38), channel_id=1, source_target_pairs={{0,32},{32,0},{64,96},{96,64},{128,160},{160,128},{192,224},{224,1... | collective-permute-start | bytes 98312 | tf_op jit(solution)/shard_map/ppermute | solution.py:303
  10.0 0.9 copy-start.2
  10.9 12.8 %copy-start.4 = (bf16[3,256,256]{2,1,0:T(8,128)(2,1)S(1)}, bf16[3,256,256]{2,1,0:T(8,128)(2,1)}, u32[]{:S(2)}) copy-start(bf16[3,256,256]{2,1,0:T(8,128)(2,1)} %mix_ref.1) | copy-start | bytes 1179652
  10.9 12.8 %copy-start.6 = (bf16[8,32,256]{2,1,0:T(8,128)(2,1)S(1)}, bf16[8,32,256]{2,1,0:T(8,128)(2,1)}, u32[]{:S(2)}) copy-start(bf16[8,32,256]{2,1,0:T(8,128)(2,1)} %cot_ref.1) | copy-start | bytes 393220
  10.9 12.8 %copy-start.7 = (bf16[256,1024]{1,0:T(8,128)(2,1)S(1)}, bf16[256,1024]{1,0:T(8,128)(2,1)}, u32[]{:S(2)}) copy-start(bf16[256,1024]{1,0:T(8,128)(2,1)} %in_hbm.1) | copy-start | bytes 1572868
  11.5 11.3 %collective-permute-start.2 = (bf16[12,8,256]{2,1,0:T(8,128)(2,1)S(1)}, bf16[12,8,256]{2,1,0:T(8,128)(2,1)S(1)}, u32[]{:S(2)}, u32[]{:S(2)}) collective-permute-start(bf16[12,8,256]{2,1,0:T(8,128)(2,1)S(1)} %get-tuple-element.20), channel_id=1, source_target_pairs={{0,1},{1,0},{2,3},{3,2},{4,5},{5,4},{6,7},{7,6},{8,9},{9,8},{10,11... | collective-permute-start | bytes 147464 | tf_op jit(solution)/shard_map/ppermute | solution.py:303
  18.3 5.4 %collective-permute-start.3 = (bf16[12,8,256]{2,1,0:T(8,128)(2,1)S(1)}, bf16[12,8,256]{2,1,0:T(8,128)(2,1)S(1)}, u32[]{:S(2)}, u32[]{:S(2)}) collective-permute-start(bf16[12,8,256]{2,1,0:T(8,128)(2,1)S(1)} %get-tuple-element.21), channel_id=1, source_target_pairs={{1,2},{2,1},{3,4},{4,3},{5,6},{6,5},{7,8},{8,7},{9,10},{10,9},{11,... | collective-permute-start | bytes 147464 | tf_op jit(solution)/shard_map/ppermute | solution.py:303
  27.4 7.6 %collective-permute-start.8 = (bf16[2816,128]{1,0:T(8,128)(2,1)S(1)}, bf16[2816,128]{1,0:T(8,128)(2,1)S(1)}, u32[]{:S(2)}, u32[]{:S(2)}) collective-permute-start(bf16[2816,128]{1,0:T(8,128)(2,1)S(1)} %slice_bitcast_fusion), channel_id=1, source_target_pairs={{0,1},{1,0},{2,3},{3,2},{4,5},{5,4},{6,7},{7,6},{8,9},{9,8},{10,11... | collective-permute-start | bytes 2162696 | tf_op jit(solution)/shard_map/ppermute | solution.py:303
  36.1 21.8 %all-to-all-start = ((bf16[32,88,128]{2,1,0:T(8,128)(2,1)}), bf16[32,88,128]{2,1,0:T(8,128)(2,1)S(1)}, u32[]{:S(2)}, u32[]{:S(2)}) async-start(bf16[32,88,128]{2,1,0:T(8,128)(2,1)} %bitcast.4), calls=%async_computation | async-start | bytes 1441792 | tf_op jit(solution)/shard_map/all_to_all | solution.py:377
  47.3 0.7 copy-start.8
  48.0 22.8 %copy-start.9 = (f32[12,32,256]{2,1,0:T(8,128)S(1)}, f32[12,32,256]{2,1,0:T(8,128)}, u32[]{:S(2)}) copy-start(f32[12,32,256]{2,1,0:T(8,128)} %copy-done.8) | copy-start | bytes 1179652
  48.0 6.0 %collective-permute-start.4 = (bf16[12,8,256]{2,1,0:T(8,128)(2,1)S(1)}, bf16[12,8,256]{2,1,0:T(8,128)(2,1)S(1)}, u32[]{:S(2)}, u32[]{:S(2)}) collective-permute-start(bf16[12,8,256]{2,1,0:T(8,128)(2,1)S(1)} %get-tuple-element.25), channel_id=1, source_target_pairs={{0,1},{1,0},{2,3},{3,2},{4,5},{5,4},{6,7},{7,6},{8,9},{9,8},{10,11... | collective-permute-start | bytes 147464 | tf_op jit(solution)/shard_map/ppermute | solution.py:303
  50.7 6.3 %collective-permute-start.5 = (bf16[12,8,256]{2,1,0:T(8,128)(2,1)S(1)}, bf16[12,8,256]{2,1,0:T(8,128)(2,1)S(1)}, u32[]{:S(2)}, u32[]{:S(2)}) collective-permute-start(bf16[12,8,256]{2,1,0:T(8,128)(2,1)S(1)} %get-tuple-element.26), channel_id=1, source_target_pairs={{1,2},{2,1},{3,4},{4,3},{5,6},{6,5},{7,8},{8,7},{9,10},{10,9},{11,... | collective-permute-start | bytes 147464 | tf_op jit(solution)/shard_map/ppermute | solution.py:303
  58.7 27.5 %all-to-all-start.1 = ((bf16[8,88,128]{2,1,0:T(8,128)(2,1)}), bf16[8,88,128]{2,1,0:T(8,128)(2,1)S(1)}, u32[]{:S(2)}, u32[]{:S(2)}) async-start(bf16[8,88,128]{2,1,0:T(8,128)(2,1)} %sum_and_copy.2), calls=%async_computation.1 | async-start | bytes 360448 | tf_op jit(solution)/shard_map/all_to_all | solution.py:393
  87.0 22.2 %all-to-all-start.2 = ((bf16[32,88,128]{2,1,0:T(8,128)(2,1)}), bf16[32,88,128]{2,1,0:T(8,128)(2,1)S(1)}, u32[]{:S(2)}, u32[]{:S(2)}) async-start(bf16[32,88,128]{2,1,0:T(8,128)(2,1)} %sum_and_copy.3), calls=%async_computation.2 | async-start | bytes 1441792 | tf_op jit(solution)/shard_map/all_to_all | solution.py:420
  96.5 9.7 %collective-permute-start.6 = (bf16[2,32,256]{2,1,0:T(8,128)(2,1)S(1)}, bf16[2,32,256]{2,1,0:T(8,128)(2,1)S(1)}, u32[]{:S(2)}, u32[]{:S(2)}) collective-permute-start(bf16[2,32,256]{2,1,0:T(8,128)(2,1)S(1)} %get-tuple-element.28), channel_id=1, source_target_pairs={{0,32},{32,0},{64,96},{96,64},{128,160},{160,128},{192,224},{224,1... | collective-permute-start | bytes 98312 | tf_op jit(solution)/shard_map/ppermute | solution.py:303
  99.7 6.6 %collective-permute-start.7 = (bf16[2,32,256]{2,1,0:T(8,128)(2,1)S(1)}, bf16[2,32,256]{2,1,0:T(8,128)(2,1)S(1)}, u32[]{:S(2)}, u32[]{:S(2)}) collective-permute-start(bf16[2,32,256]{2,1,0:T(8,128)(2,1)S(1)} %get-tuple-element.29), channel_id=1, source_target_pairs={{32,64},{64,32},{96,128},{128,96},{160,192},{192,160},{224,256},{2... | collective-permute-start | bytes 98312 | tf_op jit(solution)/shard_map/ppermute | solution.py:303
  109.3 0.9 copy-start.5
  110.2 4.7 %collective-permute-start.9 = (bf16[2816,128]{1,0:T(8,128)(2,1)S(1)}, bf16[2816,128]{1,0:T(8,128)(2,1)S(1)}, u32[]{:S(2)}, u32[]{:S(2)}) collective-permute-start(bf16[2816,128]{1,0:T(8,128)(2,1)S(1)} %tie.1), channel_id=1, source_target_pairs={{0,1},{1,0},{2,3},{3,2},{4,5},{5,4},{6,7},{7,6},{8,9},{9,8},{10,11... | collective-permute-start | bytes 2162696 | tf_op jit(solution)/shard_map/ppermute | solution.py:303
  115.3 1.7 %copy-start.10 = (bf16[256,1024]{1,0:T(8,128)(2,1)}, bf16[256,1024]{1,0:T(8,128)(2,1)S(1)}, u32[]{:S(2)}) copy-start(bf16[256,1024]{1,0:T(8,128)(2,1)S(1)} %slice_dynamic-update-slice_fusion) | copy-start | bytes 1572868

commit v4 on v3

--- a/solution.py
+++ b/solution.py
@@ -50,34 +50,31 @@
     return jax.ShapeDtypeStruct(shape, dtype)
 
 
-def bands_kernel(cols, offset_ref, value_ref, high_ref, low_ref):
-    kinds, cycles, lags, slots = 3, high_ref.shape[0] // (3 * cols), LAGS, offset_ref.shape[0]
-    slots = slots // (cycles * lags)
-    span = cols + 2 * WIDE
-    shape = (cols, LANES)
-    ahead = lax.broadcasted_iota(jnp.int32, shape, 1) - lax.broadcasted_iota(jnp.int32, shape, 0)
-
-    def cycle(i, carry):
-        for start in range(0, high_ref.shape[1], LANES):
-            sums = [jnp.zeros(shape, jnp.float32) for _ in range(kinds)]
-            for q in range(lags):
-                if q * span >= start + LANES or (q + 1) * span <= start:
-                    continue
-                for s in range(slots):
-                    at = (i * lags + q) * slots + s
-                    hit = ahead == offset_ref[at] + (q * span + WIDE - start)
-                    for k in range(kinds):
-                        value = value_ref[k * cycles * lags * slots + at]
-                        sums[k] = sums[k] + jnp.where(hit, value, 0.0)
-            for k in range(kinds):
-                at = pl.ds(pl.multiple_of((i * kinds + k) * cols, cols), cols)
-                high = sums[k].astype(jnp.bfloat16)
-                high_ref[at, start : start + LANES] = high
-                rest = sums[k] - high.astype(jnp.float32)
-                low_ref[at, start : start + LANES] = rest.astype(jnp.bfloat16)
-        return carry
-
-    lax.fori_loop(0, cycles, cycle, 0)
+def bands_kernel(cols, offset_ref, value_ref, bands_ref, first_ref):
+    cycles, height, depth = bands_ref.shape
+    kinds, span = height // (2 * cols), cols + 2 * WIDE
+    slots = offset_ref.shape[1] // LAGS
+    lane = lax.broadcasted_iota(jnp.int32, (cycles, LANES), 1)
+    for start in range(0, depth, LANES):
+        sums = [jnp.zeros((cycles, LANES), jnp.float32) for _ in range(kinds)]
+        for q in range(LAGS):
+            if q * span + 2 * WIDE < start or q * span >= start + LANES:
+                continue
+            for s in range(slots):
+                at = slice(q * slots + s, q * slots + s + 1)
+                hit = lane == offset_ref[:, at] + (q * span + WIDE - start)
+                for k in range(kinds):
+                    sums[k] = sums[k] + jnp.where(hit, value_ref[k, :, at], 0.0)
+        for k in range(kinds):
+            first_ref[k, :, start : start + LANES] = sums[k]
+    for i in range(cycles):
+        for k in range(kinds):
+            block = jnp.broadcast_to(first_ref[k, i : i + 1, :], (cols, depth))
+            block = pltpu.roll(block, 0, 1, stride=1, stride_axis=0)
+            high = block.astype(jnp.bfloat16)
+            low = (block - high.astype(jnp.float32)).astype(jnp.bfloat16)
+            bands_ref[i, k * cols : (k + 1) * cols] = high
+            bands_ref[i, (kinds + k) * cols : (kinds + k + 1) * cols] = low
 
 
 def by_side(odd, near, far):
@@ -108,27 +105,10 @@
     return x * cdf, slope
 
 
-def fetch(sources, targets, sems):
-    copies = [
-        pltpu.make_async_copy(source, target, sems.at[i])
-        for i, (source, target) in enumerate(zip(sources, targets))
-    ]
-    for copy in copies:
-        copy.start()
-
-    def take(i):
-        copies[i].wait()
-        return targets[i]
-
-    return take
-
-
 def main_kernel(
-    side_ref, high_ref, low_ref, lat_near_ref, state_ref, lat_far_ref, lon_near_ref, lon_far_ref,
-    mix_hbm, in_hbm, out_hbm, cot_hbm, packed_ref, hidden_ref, grad_ref,
-    cells_ref, basis_ref, mix_ref, in_ref, out_ref, cot_ref, sems,
+    side_ref, bands_ref, lat_near_ref, state_ref, lat_far_ref, lon_near_ref, lon_far_ref,
+    mix_ref, in_ref, out_ref, cot_ref, packed_ref, hidden_ref, grad_ref, cells_ref, basis_ref,
 ):
-    take = fetch((mix_hbm, in_hbm, out_hbm, cot_hbm), (mix_ref, in_ref, out_ref, cot_ref), sems)
     rows, cols, channels = state_ref.shape
     span = cols + 2 * WIDE
     kinds = basis_ref.shape[0]
@@ -139,19 +119,16 @@
     used = (rows + 2 * RAD) * span
     cells_ref[used:] = jnp.zeros((cells_ref.shape[0] - used, channels), jnp.bfloat16)
 
-    depth = high_ref.shape[1]
+    depth = bands_ref.shape[2]
     for i in range(rows):
-        window = cells_ref[i * span : i * span + depth]
-        at = slice(i * kinds * cols, (i + 1) * kinds * cols)
-        taken = dot(high_ref[at], window) + dot(low_ref[at], window)
+        taken = dot(bands_ref[i], cells_ref[i * span : i * span + depth])
+        taken = taken[: kinds * cols] + taken[kinds * cols :]
         for k in range(kinds):
             piece = taken[k * cols : (k + 1) * cols].astype(jnp.bfloat16)
             basis_ref[k, i * cols : (i + 1) * cols] = piece
-    mix_ref = take(0)
     mixed = sum(dot(basis_ref[k], mix_ref[k]) for k in range(kinds)).astype(jnp.bfloat16)
 
-    in_ref, out_ref = take(1), take(2)
-    cot = take(3)[...]
+    cot = cot_ref[...]
     core, half = side_ref[1], packed_ref.shape[1]
 
     def pack(matrix, place, height):
@@ -181,7 +158,7 @@
 
 
 def adjoint_kernel(
-    side_ref, grad_ref, mix_ref, high_ref, low_ref, near_ref, far_ref, middle_ref, back_ref, landing_ref
+    side_ref, grad_ref, mix_ref, bands_ref, far_ref, near_ref, middle_ref, back_ref, landing_ref
 ):
     tall, cols, channels = middle_ref.shape
     rows, span = tall - 2 * RAD, cols + 2 * WIDE
@@ -190,20 +167,18 @@
     for k in range(kinds):
         back_ref[k] = dot(grad, mix_ref[k], COLS).astype(jnp.bfloat16)
     landing_ref[...] = jnp.zeros_like(landing_ref)
-    depth = high_ref.shape[1]
+    depth = bands_ref.shape[2]
     for i in range(rows):
         pieces = [back_ref[k, i * cols : (i + 1) * cols] for k in range(kinds)]
-        taken = jnp.concatenate(pieces, axis=0)
-        at = slice(i * kinds * cols, (i + 1) * kinds * cols)
-        spread = dot(high_ref[at], taken, ROWS) + dot(low_ref[at], taken, ROWS)
-        landing_ref[i * span : i * span + depth] += spread
+        taken = jnp.concatenate(pieces + pieces, axis=0)
+        landing_ref[i * span : i * span + depth] += dot(bands_ref[i], taken, ROWS)
     for r in range(rows + 2 * RAD):
         line = landing_ref[r * span : (r + 1) * span]
         near_ref[r], far_ref[r] = by_partner(side_ref[1] != 0, line[:WIDE], line[WIDE + cols :])
         middle_ref[r] = line[WIDE : WIDE + cols]
 
 
-def rims_kernel(side_ref, middle_ref, near_ref, far_ref, to_near_ref, to_far_ref, core_ref):
+def rims_kernel(side_ref, middle_ref, near_ref, far_ref, to_far_ref, to_near_ref, core_ref):
     rows, cols = core_ref.shape[:2]
     lines = []
     for r in range(rows + 2 * RAD):
@@ -218,21 +193,37 @@
         core_ref[r] = lines[RAD + r]
 
 
-def field_kernel(side_ref, cot_ref, core_ref, near_ref, far_ref, field_ref):
-    rows = core_ref.shape[0]
+def final_kernel(
+    side_ref, hidden_ref, out_ref, state_ref, cot_ref, core_ref, near_ref, far_ref, block_ref, field_ref
+):
+    rows, cols = core_ref.shape[:2]
+    branch = dot(hidden_ref[...], out_ref[...])
     lines = [core_ref[r] for r in range(rows)]
     for r in range(RAD):
         above, below = by_side(side_ref[0] != 0, near_ref[r], far_ref[r])
         lines[r] = lines[r] + above
         lines[rows - RAD + r] = lines[rows - RAD + r] + below
     for r in range(rows):
-        field_ref[r] = (cot_ref[r].astype(jnp.float32) + lines[r]).astype(jnp.bfloat16)
-
-
-def edges_kernel(side_ref, lat_near_ref, state_ref, lat_far_ref, near_ref, far_ref):
-    cols = state_ref.shape[1]
-    for r, line in enumerate(whole_rows(side_ref, lat_near_ref, state_ref, lat_far_ref)):
+        at = slice(r * cols, (r + 1) * cols)
+        block_ref[r] = (state_ref[r].astype(jnp.float32) + branch[at]).astype(jnp.bfloat16)
+        field_ref[r] = (cot_ref[at].astype(jnp.float32) + lines[r]).astype(jnp.bfloat16)
+
+
+def inner_edges_kernel(side_ref, state_ref, near_ref, far_ref):
+    rows, cols = state_ref.shape[:2]
+    for r in range(rows):
+        line = state_ref[r].astype(jnp.float32)
         near_ref[r], far_ref[r] = by_partner(side_ref[1] != 0, line[:WIDE], line[cols - WIDE :])
+
+
+def edges_kernel(side_ref, lat_near_ref, lat_far_ref, own_near_ref, own_far_ref, far_ref, near_ref):
+    rows, cols = own_near_ref.shape[0], lat_near_ref.shape[1]
+    near_ref[RAD : RAD + rows] = own_near_ref[...]
+    far_ref[RAD : RAD + rows] = own_far_ref[...]
+    for r in range(RAD):
+        lines = by_side(side_ref[0] != 0, lat_near_ref[r], lat_far_ref[r])
+        for at, line in zip((r, RAD + rows + r), lines):
+            near_ref[at], far_ref[at] = by_partner(side_ref[1] != 0, line[:WIDE], line[cols - WIDE :])
 
 
 def add_kernel(a_ref, b_ref, sum_ref):
@@ -275,23 +266,29 @@
     )[0]
 
 
-def unpack(whole, shapes):
-    outs, start = [], 0
-    for rows, cols in shapes:
-        pieces = []
-        for _ in range(0, cols, LANES):
-            pieces.append(whole[start : start + rows])
+def runs_of(shapes, half):
+    runs, start = ([], []), 0
+    for out, (rows, cols) in enumerate(shapes):
+        for col in range(0, cols, LANES):
+            at = start
+            while at < start + rows:
+                which = at // half
+                height = min(start + rows, (which + 1) * half) - at
+                runs[which].append((out, at - start, col, at - which * half, height))
+                at += height
             start += rows
-        outs.append(jnp.concatenate(pieces, axis=1))
-    return outs
-
-
-def block_kernel(hidden_ref, out_ref, state_ref, block_ref):
-    rows, cols = state_ref.shape[:2]
-    branch = dot(hidden_ref[...], out_ref[...])
-    for i in range(rows):
-        line = state_ref[i].astype(jnp.float32) + branch[i * cols : (i + 1) * cols]
-        block_ref[i] = line.astype(jnp.bfloat16)
+    return runs
+
+
+def place_kernel(runs, side_ref, mine_ref, other_ref, *outs):
+    for core in range(2):
+
+        @pl.when(side_ref[1] == core)
+        def _(core=core):
+            for which in range(2):
+                half_ref = mine_ref if which == core else other_ref
+                for out, row, col, at, height in runs[which]:
+                    outs[out][row : row + height, col : col + LANES] = half_ref[at : at + height]
 
 
 def swap(cells, axes, lead, closed):
@@ -313,6 +310,7 @@
 ):
     rows, cols, channels = state_field.shape
     kinds, units = basis_weight.shape[0], weight_in.shape[1]
+    grid = state_field.shape
     cells, span = rows * cols, cols + 2 * WIDE
     tall = rows + 2 * RAD
     depth = -(-LAGS * span // LANES) * LANES
@@ -322,6 +320,7 @@
 
     odd_lat, odd_lon = lax.axis_index(LAT) % 2, lax.axis_index(LON) % 2
     sides = jnp.stack([odd_lat, odd_lon])
+    edge = like((RAD, cols, channels), bf16)
     last = rows - RAD
     to_near = lax.dynamic_slice_in_dim(state_field, jnp.where(odd_lat == 0, last, 0), RAD, 0)
     to_far = lax.dynamic_slice_in_dim(state_field, jnp.where(odd_lat == 0, 0, last), RAD, 0)
@@ -330,20 +329,24 @@
     band_start = lax.axis_index(LAT) * rows
     offsets = lax.dynamic_slice_in_dim(support_offsets, band_start, rows, 0)
     values = lax.dynamic_slice_in_dim(kernel_values, band_start, rows, 1).astype(f32)
-    band_shape = (rows * kinds * cols, depth)
-    high, low = kernel_call(
+    (bands,) = kernel_call(
         functools.partial(bands_kernel, cols),
-        (offsets.reshape(-1), values.reshape(-1)),
-        [SMEM, SMEM],
-        [like(band_shape, bf16), like(band_shape, bf16)],
-        flops=8 * cells * channels * units,
+        (offsets.reshape(rows, -1), values.reshape(kinds, rows, -1)),
+        [VMEM, VMEM],
+        [like((rows, 2 * kinds * cols, depth), bf16)],
+        [pltpu.VMEM((kinds, rows, depth), f32)],
+        flops=4 * 10**9,
         name="bands",
     )
     rim = like((tall, WIDE, channels), bf16)
-    to_near, to_far = kernel_call(
+    own = like((rows, WIDE, channels), bf16)
+    own_near, own_far = kernel_call(
+        inner_edges_kernel, (sides, state_field), [SMEM, VMEM], [own, own], name="inner_edges"
+    )
+    to_far, to_near = kernel_call(
         edges_kernel,
-        (sides, lat_near, state_field, lat_far),
-        [SMEM] + [VMEM] * 3,
+        (sides, lat_near, lat_far, own_near, own_far),
+        [SMEM] + [VMEM] * 4,
         [rim, rim],
         name="edges",
     )
@@ -354,19 +357,14 @@
     packed, hidden, grad_mixed = kernel_call(
         main_kernel,
         (
-            sides, high, low, lat_near, state_field, lat_far, lon_near, lon_far,
+            sides, bands, lat_near, state_field, lat_far, lon_near, lon_far,
             basis_weight, weight_in, weight_out, cot_flat,
         ),
-        [SMEM] + [VMEM] * 7 + [ANY] * 4,
+        [SMEM] + [VMEM] * 10,
         [like((2,) + half.shape, bf16), like((cells, units), bf16), like((cells, channels), bf16)],
         [
             pltpu.VMEM((rows * span + depth, channels), bf16),
             pltpu.VMEM((kinds, cells, channels), bf16),
-            pltpu.VMEM(basis_weight.shape, bf16),
-            pltpu.VMEM(weight_in.shape, bf16),
-            pltpu.VMEM(weight_out.shape, bf16),
-            pltpu.VMEM(cot_flat.shape, bf16),
-            pltpu.SemaphoreType.DMA((4,)),
         ],
         flops=10 * cells * channels * units,
         name="main",
@@ -376,10 +374,10 @@
     chip = kernel_call(add_kernel, (packed, arrived), [VMEM] * 2, [half], name="add")[0]
     shares = lax.all_to_all(chip.reshape(near, -1, LANES), NEAR, 0, 0)
 
-    to_near, to_far, middle = kernel_call(
+    to_far, to_near, middle = kernel_call(
         adjoint_kernel,
-        (sides, grad_mixed, basis_weight, high, low),
-        [SMEM] + [VMEM] * 4,
+        (sides, grad_mixed, basis_weight, bands),
+        [SMEM] + [VMEM] * 3,
         [rim, rim, like((tall, cols, channels), f32)],
         [
             pltpu.VMEM((kinds, cells, channels), bf16),
@@ -391,40 +389,34 @@
     near_rim, far_rim = swap_both(to_near, to_far, LON, True)
     planes = sum_and_copy(shares, 1.0, far, near_rim, far_rim)
     planes = lax.all_to_all(planes, FAR, 0, 0)
-    edge = like((RAD, cols, channels), bf16)
-    to_near, to_far, inside = kernel_call(
+    to_far, to_near, inside = kernel_call(
         rims_kernel,
         (sides, middle, near_rim, far_rim),
         [SMEM] + [VMEM] * 3,
-        [edge, edge, like(state_field.shape, f32)],
+        [edge, edge, like(grid, f32)],
         name="rims",
     )
     near_edge, far_edge = swap_both(to_near, to_far, LAT, False)
     scale = 1.0 / math.sqrt(cells * lax.axis_size(LAT) * lax.axis_size(LON))
-    copies = sum_and_copy(planes, scale, near, inside)
-    (grad_field,) = kernel_call(
-        field_kernel,
-        (sides, cotangent, inside, near_edge, far_edge),
-        [SMEM] + [VMEM] * 4,
-        [like(state_field.shape, bf16)],
-        name="field",
-    )
-    (block_out,) = kernel_call(
-        block_kernel,
-        (hidden, weight_out, state_field),
-        [VMEM] * 3,
-        [like(state_field.shape, bf16)],
+    copies = sum_and_copy(planes, scale, near, near_edge, far_edge)
+    block_out, grad_field = kernel_call(
+        final_kernel,
+        (sides, hidden, weight_out, state_field, cot_flat, inside, near_edge, far_edge),
+        [SMEM] + [VMEM] * 7,
+        [like(grid, bf16), like(grid, bf16)],
         flops=2 * cells * channels * units,
-        name="block",
+        name="final",
     )
     mine = lax.all_to_all(copies, NEAR, 0, 0).reshape(-1, LANES)
-    mine = tie(mine, near_edge, far_edge, block_out)
     other = swap(mine, CORE, 0, True)
     shapes = ((units, channels), (channels, units), (kinds * channels, channels))
-    whole = jnp.concatenate(
-        [jnp.where(core == 0, mine, other), jnp.where(core == 0, other, mine)], axis=0
-    )
-    grad_out, grad_in, grad_basis = unpack(whole, shapes)
+    grad_out, grad_in, grad_basis = kernel_call(
+        functools.partial(place_kernel, runs_of(shapes, packed_rows // 2)),
+        (sides, mine, other),
+        [SMEM, VMEM, VMEM],
+        [like(shape, bf16) for shape in shapes],
+        name="place",
+    )
     return (block_out, grad_field, grad_basis.reshape(basis_weight.shape), grad_in, grad_out)
 
 

time: 119 us -> 114 us (0.958); the launches traced: 117 us -> 113 us
  blocking collectives: 0 us -> 22.5 us
  starting transfers between devices: 65.4 us -> 54 us
  waiting for transfers between devices: 29.8 us -> 20.4 us
  Pallas kernels: 14 us -> 11.9 us
  other arithmetic: 2.7 us -> 0.91 us
  local copies, waits for them, and re-layouts: 4.13 us -> 2.75 us
    all_to_all x0 -> x1, blocking collectives: none -> 22.5 us  [local(): mine = lax.all_to_all(copies, NEAR, 0, 0).reshape(-1, LANES)]
    all_to_all x1 -> x0, starting transfers between devices: 9.44 us -> none  [local(): mine = lax.all_to_all(copies, NEAR, 0, 0).reshape(-1, LANES)]
    all_to_all x1, waiting for transfers between devices: 14.7 us -> 8.82 us  [local(): planes = lax.all_to_all(planes, FAR, 0, 0)]
    all_to_all x1 -> x0, waiting for transfers between devices: 3.05 us -> none  [local(): mine = lax.all_to_all(copies, NEAR, 0, 0).reshape(-1, LANES)]
    pallas_call x11, Pallas kernels: 14 us -> 11.9 us  [kernel_call(): pl.pallas_call(body, out_shape=tuple(outs), in_specs=specs, out_specs=tup...]
    ppermute x10, starting transfers between devices: 34.3 us -> 32.5 us  [swap(): return lax.ppermute(cells, axes, pairs)]
    concatenate x2 -> x0, other arithmetic: 1.7 us -> none  [unpack(): outs.append(jnp.concatenate(pieces, axis=1))]
    unnamed x29 -> x18, local copies, waits for them, and re-layouts: 2.72 us -> 1.71 us
  transfers between devices with their start and end apart: 13 -> 12, of which waited for: 8 -> 7; matrix products, arithmetic and copies ran while one was open for 1% -> 1% of each run, Pallas kernels for 6% -> 4%
where the time goes in v4:
time: 114 us; the launch traced here: 113 us
  starting transfers between devices  54 us (47%)
  blocking collectives  22.5 us (20%)
  waiting for transfers between devices  20.4 us (18%)
  Pallas kernels  11.9 us (10%)
  local copies, waits for them, and re-layouts  2.75 us (2%)
    ppermute x10, starting transfers between devices, swap(): return lax.ppermute(cells, axes, pairs)  32.5 us
    all_to_all x1, blocking collectives, local(): mine = lax.all_to_all(copies, NEAR, 0, 0).reshape(-1, LANES)  22.5 us
    pallas_call x11, Pallas kernels, kernel_call(): pl.pallas_call(body, out_shape=tuple(outs), in_specs=specs, out_specs=tup...  11.9 us
    all_to_all x1, starting transfers between devices, local(): planes = lax.all_to_all(planes, FAR, 0, 0)  11.8 us
    ppermute x10, waiting for transfers between devices, swap(): return lax.ppermute(cells, axes, pairs)  10.7 us
    all_to_all x1, starting transfers between devices, local(): shares = lax.all_to_all(chip.reshape(near, -1, LANES), NEAR, 0, 0)  9.71 us
    all_to_all x1, waiting for transfers between devices, local(): planes = lax.all_to_all(planes, FAR, 0, 0)  8.82 us
  transfers between devices with their start and end apart: 12, of which 7 were waited for; matrix products, arithmetic and copies ran while one was open for 1% of the time, Pallas kernels for 4%

profile of v4, /device:TPU:1, one launch (start us, length us, event | category | flops | bytes accessed | tf_op | source)
XLA Modules:
  0.0 113.3 jit_solution(10975240770387344181)
XLA Ops:
  2.1 6.4 %collective-permute-start = (bf16[2,32,256]{2,1,0:T(8,128)(2,1)S(1)}, bf16[2,32,256]{2,1,0:T(8,128)(2,1)S(1)}, u32[]{:S(2)}, u32[]{:S(2)}) collective-permute-start(bf16[2,32,256]{2,1,0:T(8,128)(2,1)S(1)} %get-tuple-element.42), channel_id=1, source_target_pairs={{0,32},{32,0},{64,96},{96,64},{128,160},{160,128},{192,224},{224,1... | collective-permute-start | bytes 98312 | tf_op jit(solution)/shard_map/ppermute | solution.py:300
  8.6 0.8 bitcast_convert_fusion
  9.7 0.9 copy-done.2
  11.7 5.5 %collective-permute-start.2 = (bf16[12,8,256]{2,1,0:T(8,128)(2,1)S(1)}, bf16[12,8,256]{2,1,0:T(8,128)(2,1)S(1)}, u32[]{:S(2)}, u32[]{:S(2)}) collective-permute-start(bf16[12,8,256]{2,1,0:T(8,128)(2,1)S(1)} %get-tuple-element.25), channel_id=1, source_target_pairs={{0,1},{1,0},{2,3},{3,2},{4,5},{5,4},{6,7},{7,6},{8,9},{9,8},{10,11... | collective-permute-start | bytes 147464 | tf_op jit(solution)/shard_map/ppermute | solution.py:300
  17.3 2.1 %collective-permute-start.3 = (bf16[12,8,256]{2,1,0:T(8,128)(2,1)S(1)}, bf16[12,8,256]{2,1,0:T(8,128)(2,1)S(1)}, u32[]{:S(2)}, u32[]{:S(2)}) collective-permute-start(bf16[12,8,256]{2,1,0:T(8,128)(2,1)S(1)} %get-tuple-element.26), channel_id=1, source_target_pairs={{1,2},{2,1},{3,4},{4,3},{5,6},{6,5},{7,8},{8,7},{9,10},{10,9},{11,... | collective-permute-start | bytes 147464 | tf_op jit(solution)/shard_map/ppermute | solution.py:300
  20.0 2.9 %collective-permute-done.3.lon_far_ref = bf16[12,8,256]{2,1,0:T(8,128)(2,1)S(1)} collective-permute-done((bf16[12,8,256]{2,1,0:T(8,128)(2,1)S(1)}, bf16[12,8,256]{2,1,0:T(8,128)(2,1)S(1)}, u32[]{:S(2)}, u32[]{:S(2)}) %collective-permute-start.3) | collective-permute-done | bytes 49184 | tf_op jit(solution)/shard_map/ppermute | solution.py:300
  22.9 2.9 %main.1 = (bf16[2,2816,128]{2,1,0:T(8,128)(2,1)S(1)}, bf16[256,1024]{1,0:T(8,128)(2,1)S(1)}, bf16[256,256]{1,0:T(8,128)(2,1)S(1)}) custom-call(s32[2]{0:T(128)S(1)} %pad_add_fusion.side_ref, bf16[8,192,256]{2,1,0:T(8,128)(2,1)S(1)} %bands.1.bands_ref, bf16[2,32,256]{2,1,0:T(8,128)(2,1)S(1)} %collective-permute-done.lat_near_ref, ...), custom_call_target="tpu_custom_call" | custom-call | flops 671088640 | bytes 4751368 | tf_op jit(solution)/shard_map/main/pallas_call | solution.py:37
  25.8 5.8 %collective-permute-start.8 = (bf16[2816,128]{1,0:T(8,128)(2,1)S(1)}, bf16[2816,128]{1,0:T(8,128)(2,1)S(1)}, u32[]{:S(2)}, u32[]{:S(2)}) collective-permute-start(bf16[2816,128]{1,0:T(8,128)(2,1)S(1)} %slice_bitcast_fusion), channel_id=1, source_target_pairs={{0,1},{1,0},{2,3},{3,2},{4,5},{5,4},{6,7},{7,6},{8,9},{9,8},{10,11... | collective-permute-start | bytes 2162696 | tf_op jit(solution)/shard_map/ppermute | solution.py:300
  31.7 1.8 %collective-permute-done.8.b_ref = bf16[2816,128]{1,0:T(8,128)(2,1)S(1)} collective-permute-done((bf16[2816,128]{1,0:T(8,128)(2,1)S(1)}, bf16[2816,128]{1,0:T(8,128)(2,1)S(1)}, u32[]{:S(2)}, u32[]{:S(2)}) %collective-permute-start.8) | collective-permute-done | bytes 720928 | tf_op jit(solution)/shard_map/ppermute | solution.py:300
  33.5 1.0 add.36
  34.5 9.7 %all-to-all-start = ((bf16[32,88,128]{2,1,0:T(8,128)(2,1)}), bf16[32,88,128]{2,1,0:T(8,128)(2,1)S(1)}, u32[]{:S(2)}, u32[]{:S(2)}) async-start(bf16[32,88,128]{2,1,0:T(8,128)(2,1)} %bitcast.6), calls=%async_computation | async-start | bytes 1441792 | tf_op jit(solution)/shard_map/all_to_all | solution.py:375
  44.2 1.4 %adjoint.1 = (bf16[12,8,256]{2,1,0:T(8,128)(2,1)S(1)}, bf16[12,8,256]{2,1,0:T(8,128)(2,1)S(1)}, f32[12,32,256]{2,1,0:T(8,128)S(1)}) custom-call(s32[2]{0:T(128)S(1)} %pad_add_fusion.side_ref, bf16[256,256]{1,0:T(8,128)(2,1)S(1)} %get-tuple-element.28.grad_ref, bf16[3,256,256]{2,1,0:T(8,128)(2,1)S(1)} %copy-done.4, bf16[8,192,256]{2,1,0:T(8,128)(2,1)S(1)} %bands.1.bands_ref), custom_call_target="tpu_custom_call" | custom-call | flops 268435456 | bytes 1802248 | tf_op jit(solution)/shard_map/adjoint/pallas_call | solution.py:37
  46.4 2.5 %collective-permute-start.4 = (bf16[12,8,256]{2,1,0:T(8,128)(2,1)S(1)}, bf16[12,8,256]{2,1,0:T(8,128)(2,1)S(1)}, u32[]{:S(2)}, u32[]{:S(2)}) collective-permute-start(bf16[12,8,256]{2,1,0:T(8,128)(2,1)S(1)} %get-tuple-element.30), channel_id=1, source_target_pairs={{0,1},{1,0},{2,3},{3,2},{4,5},{5,4},{6,7},{7,6},{8,9},{9,8},{10,11... | collective-permute-start | bytes 147464 | tf_op jit(solution)/shard_map/ppermute | solution.py:300
  48.9 3.3 %collective-permute-start.5 = (bf16[12,8,256]{2,1,0:T(8,128)(2,1)S(1)}, bf16[12,8,256]{2,1,0:T(8,128)(2,1)S(1)}, u32[]{:S(2)}, u32[]{:S(2)}) collective-permute-start(bf16[12,8,256]{2,1,0:T(8,128)(2,1)S(1)} %get-tuple-element.31), channel_id=1, source_target_pairs={{1,2},{2,1},{3,4},{4,3},{5,6},{6,5},{7,8},{8,7},{9,10},{10,9},{11,... | collective-permute-start | bytes 147464 | tf_op jit(solution)/shard_map/ppermute | solution.py:300
  52.2 3.7 %collective-permute-done.5.far_ref.refs_1_ = bf16[12,8,256]{2,1,0:T(8,128)(2,1)S(1)} collective-permute-done((bf16[12,8,256]{2,1,0:T(8,128)(2,1)S(1)}, bf16[12,8,256]{2,1,0:T(8,128)(2,1)S(1)}, u32[]{:S(2)}, u32[]{:S(2)}) %collective-permute-start.5) | collective-permute-done | bytes 49184 | tf_op jit(solution)/shard_map/ppermute | solution.py:300
  55.9 0.8 all-to-all-done.parts_ref
  57.5 11.8 %all-to-all-start.1 = ((bf16[8,88,128]{2,1,0:T(8,128)(2,1)}), bf16[8,88,128]{2,1,0:T(8,128)(2,1)S(1)}, u32[]{:S(2)}, u32[]{:S(2)}) async-start(bf16[8,88,128]{2,1,0:T(8,128)(2,1)} %sum_and_copy.2), calls=%async_computation.1 | async-start | bytes 360448 | tf_op jit(solution)/shard_map/all_to_all | solution.py:391
  69.9 1.9 %collective-permute-start.6 = (bf16[2,32,256]{2,1,0:T(8,128)(2,1)S(1)}, bf16[2,32,256]{2,1,0:T(8,128)(2,1)S(1)}, u32[]{:S(2)}, u32[]{:S(2)}) collective-permute-start(bf16[2,32,256]{2,1,0:T(8,128)(2,1)S(1)} %get-tuple-element.33), channel_id=1, source_target_pairs={{0,32},{32,0},{64,96},{96,64},{128,160},{160,128},{192,224},{224,1... | collective-permute-start | bytes 98312 | tf_op jit(solution)/shard_map/ppermute | solution.py:300
  72.5 2.1 %collective-permute-done.6.near_ref.refs_0_ = bf16[2,32,256]{2,1,0:T(8,128)(2,1)S(1)} collective-permute-done((bf16[2,32,256]{2,1,0:T(8,128)(2,1)S(1)}, bf16[2,32,256]{2,1,0:T(8,128)(2,1)S(1)}, u32[]{:S(2)}, u32[]{:S(2)}) %collective-permute-start.6) | collective-permute-done | bytes 32800 | tf_op jit(solution)/shard_map/ppermute | solution.py:300
  74.5 8.8 %all-to-all-done.1.parts_ref = bf16[8,88,128]{2,1,0:T(8,128)(2,1)S(1)} async-done(((bf16[8,88,128]{2,1,0:T(8,128)(2,1)}), bf16[8,88,128]{2,1,0:T(8,128)(2,1)S(1)}, u32[]{:S(2)}, u32[]{:S(2)}) %all-to-all-start.1) | async-done | bytes 180256 | tf_op jit(solution)/shard_map/all_to_all | solution.py:391
  83.4 22.5 %all_to_all.15 = bf16[32,88,128]{2,1,0:T(8,128)(2,1)S(1)} all-to-all(bf16[32,88,128]{2,1,0:T(8,128)(2,1)S(1)} %sum_and_copy.3), channel_id=1, replica_groups=mesh['z_hi'=4,'x'=4,'z_mid'=2,'z_low'=2,'y'=4,'core'=2] {'x','z_low','y'}, dimensions={0} | all-to-all | bytes 1441792 | tf_op jit(solution)/shard_map/all_to_all | solution.py:410
  105.9 3.7 %collective-permute-start.9 = (bf16[2816,128]{1,0:T(8,128)(2,1)S(1)}, bf16[2816,128]{1,0:T(8,128)(2,1)S(1)}, u32[]{:S(2)}, u32[]{:S(2)}) collective-permute-start(bf16[2816,128]{1,0:T(8,128)(2,1)S(1)} %bitcast.13), channel_id=1, source_target_pairs={{0,1},{1,0},{2,3},{3,2},{4,5},{5,4},{6,7},{7,6},{8,9},{9,8},{10,11... | collective-permute-start | bytes 2162696 | tf_op jit(solution)/shard_map/ppermute | solution.py:300
  109.6 1.5 %final.1 = (bf16[8,32,256]{2,1,0:T(8,128)(2,1)}, bf16[8,32,256]{2,1,0:T(8,128)(2,1)}) custom-call(s32[2]{0:T(128)S(1)} %pad_add_fusion.side_ref, bf16[256,1024]{1,0:T(8,128)(2,1)S(1)} %get-tuple-element.27.hidden_ref, bf16[1024,256]{1,0:T(8,128)(2,1)S(1)} %copy-done.1, bf16[8,32,256]{2,1,0:T(8,128)(2,1)S(1)} %copy-done.3, bf16[256,256]{1,0:T(8,128)(2,1)S(1)} %bitcast.16, ...), custom_call_target="tpu_custom_call" | custom-call | flops 134217728 | bytes 1900552 | tf_op jit(solution)/shard_map/final/pallas_call | solution.py:37
  111.4 1.9 %place.1 = (bf16[1024,256]{1,0:T(8,128)(2,1)}, bf16[256,1024]{1,0:T(8,128)(2,1)}, bf16[768,256]{1,0:T(8,128)(2,1)}) custom-call(s32[2]{0:T(128)S(1)} %pad_add_fusion.side_ref, bf16[2816,128]{1,0:T(8,128)(2,1)S(1)} %bitcast.14, bf16[2816,128]{1,0:T(8,128)(2,1)S(1)} %collective-permute-done.9.other_ref), custom_call_target="tpu_custom_call" | custom-call | bytes 2883592 | tf_op jit(solution)/shard_map/place/pallas_call | solution.py:37
  (37 shorter events, 6.6 us)
Async XLA Ops:
  0.6 7.9 %copy-start = (s32[128,5,8]{0,2,1:T(8,128)S(1)}, s32[128,5,8]{0,2,1:T(8,128)}, u32[]{:S(2)}) copy-start(s32[128,5,8]{0,2,1:T(8,128)} %param.8) | copy-start | bytes 61444
  1.5 9.7 %collective-permute-start.1 = (bf16[2,32,256]{2,1,0:T(8,128)(2,1)S(1)}, bf16[2,32,256]{2,1,0:T(8,128)(2,1)S(1)}, u32[]{:S(2)}, u32[]{:S(2)}) collective-permute-start(bf16[2,32,256]{2,1,0:T(8,128)(2,1)S(1)} %get-tuple-element.41), channel_id=1, source_target_pairs={{32,64},{64,32},{96,128},{128,96},{160,192},{192,160},{224,256},{2... | collective-permute-start | bytes 98312 | tf_op jit(solution)/shard_map/ppermute | solution.py:300
  2.1 9.1 %collective-permute-start = (bf16[2,32,256]{2,1,0:T(8,128)(2,1)S(1)}, bf16[2,32,256]{2,1,0:T(8,128)(2,1)S(1)}, u32[]{:S(2)}, u32[]{:S(2)}) collective-permute-start(bf16[2,32,256]{2,1,0:T(8,128)(2,1)S(1)} %get-tuple-element.42), channel_id=1, source_target_pairs={{0,32},{32,0},{64,96},{96,64},{128,160},{160,128},{192,224},{224,1... | collective-permute-start | bytes 98312 | tf_op jit(solution)/shard_map/ppermute | solution.py:300
  9.7 0.9 copy-start.2
  11.7 8.2 %collective-permute-start.2 = (bf16[12,8,256]{2,1,0:T(8,128)(2,1)S(1)}, bf16[12,8,256]{2,1,0:T(8,128)(2,1)S(1)}, u32[]{:S(2)}, u32[]{:S(2)}) collective-permute-start(bf16[12,8,256]{2,1,0:T(8,128)(2,1)S(1)} %get-tuple-element.25), channel_id=1, source_target_pairs={{0,1},{1,0},{2,3},{3,2},{4,5},{5,4},{6,7},{7,6},{8,9},{9,8},{10,11... | collective-permute-start | bytes 147464 | tf_op jit(solution)/shard_map/ppermute | solution.py:300
  17.3 5.6 %copy-start.1 = (bf16[1024,256]{1,0:T(8,128)(2,1)S(1)}, bf16[1024,256]{1,0:T(8,128)(2,1)}, u32[]{:S(2)}) copy-start(bf16[1024,256]{1,0:T(8,128)(2,1)} %out_ref.3) | copy-start | bytes 1572868
  17.3 5.6 %copy-start.3 = (bf16[8,32,256]{2,1,0:T(8,128)(2,1)S(1)}, bf16[8,32,256]{2,1,0:T(8,128)(2,1)}, u32[]{:S(2)}) copy-start(bf16[8,32,256]{2,1,0:T(8,128)(2,1)} %state_ref.5) | copy-start | bytes 393220
  17.3 5.6 %copy-start.4 = (bf16[3,256,256]{2,1,0:T(8,128)(2,1)S(1)}, bf16[3,256,256]{2,1,0:T(8,128)(2,1)}, u32[]{:S(2)}) copy-start(bf16[3,256,256]{2,1,0:T(8,128)(2,1)} %mix_ref.3) | copy-start | bytes 1179652
  17.3 5.6 %copy-start.5 = (bf16[8,32,256]{2,1,0:T(8,128)(2,1)S(1)}, bf16[8,32,256]{2,1,0:T(8,128)(2,1)}, u32[]{:S(2)}) copy-start(bf16[8,32,256]{2,1,0:T(8,128)(2,1)} %param.13) | copy-start | bytes 393220
  17.3 5.6 %copy-start.6 = (bf16[256,1024]{1,0:T(8,128)(2,1)S(1)}, bf16[256,1024]{1,0:T(8,128)(2,1)}, u32[]{:S(2)}) copy-start(bf16[256,1024]{1,0:T(8,128)(2,1)} %in_ref.1) | copy-start | bytes 1572868
  17.3 5.5 %collective-permute-start.3 = (bf16[12,8,256]{2,1,0:T(8,128)(2,1)S(1)}, bf16[12,8,256]{2,1,0:T(8,128)(2,1)S(1)}, u32[]{:S(2)}, u32[]{:S(2)}) collective-permute-start(bf16[12,8,256]{2,1,0:T(8,128)(2,1)S(1)} %get-tuple-element.26), channel_id=1, source_target_pairs={{1,2},{2,1},{3,4},{4,3},{5,6},{6,5},{7,8},{8,7},{9,10},{10,9},{11,... | collective-permute-start | bytes 147464 | tf_op jit(solution)/shard_map/ppermute | solution.py:300
  25.8 7.6 %collective-permute-start.8 = (bf16[2816,128]{1,0:T(8,128)(2,1)S(1)}, bf16[2816,128]{1,0:T(8,128)(2,1)S(1)}, u32[]{:S(2)}, u32[]{:S(2)}) collective-permute-start(bf16[2816,128]{1,0:T(8,128)(2,1)S(1)} %slice_bitcast_fusion), channel_id=1, source_target_pairs={{0,1},{1,0},{2,3},{3,2},{4,5},{5,4},{6,7},{7,6},{8,9},{9,8},{10,11... | collective-permute-start | bytes 2162696 | tf_op jit(solution)/shard_map/ppermute | solution.py:300
  34.5 22.2 %all-to-all-start = ((bf16[32,88,128]{2,1,0:T(8,128)(2,1)}), bf16[32,88,128]{2,1,0:T(8,128)(2,1)S(1)}, u32[]{:S(2)}, u32[]{:S(2)}) async-start(bf16[32,88,128]{2,1,0:T(8,128)(2,1)} %bitcast.6), calls=%async_computation | async-start | bytes 1441792 | tf_op jit(solution)/shard_map/all_to_all | solution.py:375
  45.6 0.7 copy-start.7
  46.4 22.9 %copy-start.8 = (f32[12,32,256]{2,1,0:T(8,128)S(1)}, f32[12,32,256]{2,1,0:T(8,128)}, u32[]{:S(2)}) copy-start(f32[12,32,256]{2,1,0:T(8,128)} %copy-done.7) | copy-start | bytes 1179652
  46.4 5.8 %collective-permute-start.4 = (bf16[12,8,256]{2,1,0:T(8,128)(2,1)S(1)}, bf16[12,8,256]{2,1,0:T(8,128)(2,1)S(1)}, u32[]{:S(2)}, u32[]{:S(2)}) collective-permute-start(bf16[12,8,256]{2,1,0:T(8,128)(2,1)S(1)} %get-tuple-element.30), channel_id=1, source_target_pairs={{0,1},{1,0},{2,3},{3,2},{4,5},{5,4},{6,7},{7,6},{8,9},{9,8},{10,11... | collective-permute-start | bytes 147464 | tf_op jit(solution)/shard_map/ppermute | solution.py:300
  48.9 7.0 %collective-permute-start.5 = (bf16[12,8,256]{2,1,0:T(8,128)(2,1)S(1)}, bf16[12,8,256]{2,1,0:T(8,128)(2,1)S(1)}, u32[]{:S(2)}, u32[]{:S(2)}) collective-permute-start(bf16[12,8,256]{2,1,0:T(8,128)(2,1)S(1)} %get-tuple-element.31), channel_id=1, source_target_pairs={{1,2},{2,1},{3,4},{4,3},{5,6},{6,5},{7,8},{8,7},{9,10},{10,9},{11,... | collective-permute-start | bytes 147464 | tf_op jit(solution)/shard_map/ppermute | solution.py:300
  57.5 25.8 %all-to-all-start.1 = ((bf16[8,88,128]{2,1,0:T(8,128)(2,1)}), bf16[8,88,128]{2,1,0:T(8,128)(2,1)S(1)}, u32[]{:S(2)}, u32[]{:S(2)}) async-start(bf16[8,88,128]{2,1,0:T(8,128)(2,1)} %sum_and_copy.2), calls=%async_computation.1 | async-start | bytes 360448 | tf_op jit(solution)/shard_map/all_to_all | solution.py:391
  69.9 4.7 %collective-permute-start.6 = (bf16[2,32,256]{2,1,0:T(8,128)(2,1)S(1)}, bf16[2,32,256]{2,1,0:T(8,128)(2,1)S(1)}, u32[]{:S(2)}, u32[]{:S(2)}) collective-permute-start(bf16[2,32,256]{2,1,0:T(8,128)(2,1)S(1)} %get-tuple-element.33), channel_id=1, source_target_pairs={{0,32},{32,0},{64,96},{96,64},{128,160},{160,128},{192,224},{224,1... | collective-permute-start | bytes 98312 | tf_op jit(solution)/shard_map/ppermute | solution.py:300
  71.8 2.7 %collective-permute-start.7 = (bf16[2,32,256]{2,1,0:T(8,128)(2,1)S(1)}, bf16[2,32,256]{2,1,0:T(8,128)(2,1)S(1)}, u32[]{:S(2)}, u32[]{:S(2)}) collective-permute-start(bf16[2,32,256]{2,1,0:T(8,128)(2,1)S(1)} %get-tuple-element.34), channel_id=1, source_target_pairs={{32,64},{64,32},{96,128},{128,96},{160,192},{192,160},{224,256},{2... | collective-permute-start | bytes 98312 | tf_op jit(solution)/shard_map/ppermute | solution.py:300
  105.9 5.5 %collective-permute-start.9 = (bf16[2816,128]{1,0:T(8,128)(2,1)S(1)}, bf16[2816,128]{1,0:T(8,128)(2,1)S(1)}, u32[]{:S(2)}, u32[]{:S(2)}) collective-permute-start(bf16[2816,128]{1,0:T(8,128)(2,1)S(1)} %bitcast.13), channel_id=1, source_target_pairs={{0,1},{1,0},{2,3},{3,2},{4,5},{5,4},{6,7},{7,6},{8,9},{9,8},{10,11... | collective-permute-start | bytes 2162696 | tf_op jit(solution)/shard_map/ppermute | solution.py:300

commit v5 on v4

--- a/solution.py
+++ b/solution.py
@@ -32,13 +32,15 @@
     return lax.dot_general(a, b, (contract, ((), ())), preferred_element_type=jnp.float32)
 
 
-def kernel_call(body, operands, specs, outs, scratch=(), flops=0, mib=16, name=None):
+def kernel_call(
+    body, operands, specs, outs, scratch=(), flops=0, mib=16, name=None, out_spec=VMEM
+):
     moved = sum(x.size * x.dtype.itemsize for x in (*operands, *outs))
     return pl.pallas_call(
         body,
         out_shape=tuple(outs),
         in_specs=specs,
-        out_specs=tuple(VMEM for _ in outs),
+        out_specs=tuple(out_spec for _ in outs),
         scratch_shapes=scratch,
         compiler_params=pltpu.CompilerParams(vmem_limit_bytes=mib << 20),
         cost_estimate=pl.CostEstimate(flops=flops, bytes_accessed=moved, transcendentals=0),
@@ -106,7 +108,7 @@
 
 
 def main_kernel(
-    side_ref, bands_ref, lat_near_ref, state_ref, lat_far_ref, lon_near_ref, lon_far_ref,
+    side_ref, bands_ref, lat_near_ref, state_ref, lat_far_ref, lon_far_ref, lon_near_ref,
     mix_ref, in_ref, out_ref, cot_ref, packed_ref, hidden_ref, grad_ref, cells_ref, basis_ref,
 ):
     rows, cols, channels = state_ref.shape
@@ -226,8 +228,19 @@
             near_ref[at], far_ref[at] = by_partner(side_ref[1] != 0, line[:WIDE], line[cols - WIDE :])
 
 
-def add_kernel(a_ref, b_ref, sum_ref):
-    sum_ref[...] = (a_ref[0].astype(jnp.float32) + b_ref[...].astype(jnp.float32)).astype(jnp.bfloat16)
+def add_kernel(a_ref, b_ref, later_than_ref, sum_hbm, sum_ref, sems):
+    pieces = sems.shape[0]
+    height = sum_ref.shape[0] // pieces
+    copies = []
+    for i in range(pieces):
+        at = slice(i * height, (i + 1) * height)
+        total = a_ref[0, at].astype(jnp.float32) + b_ref[at].astype(jnp.float32)
+        sum_ref[at] = total.astype(jnp.bfloat16)
+        span = pl.ds(i * height, height)
+        copies.append(pltpu.make_async_copy(sum_ref.at[span], sum_hbm.at[span], sems.at[i]))
+        copies[i].start()
+    for copy in copies:
+        copy.wait()
 
 
 def tie_kernel(value_ref, *refs):
@@ -280,15 +293,26 @@
     return runs
 
 
-def place_kernel(runs, side_ref, mine_ref, other_ref, *outs):
-    for core in range(2):
-
-        @pl.when(side_ref[1] == core)
-        def _(core=core):
-            for which in range(2):
-                half_ref = mine_ref if which == core else other_ref
-                for out, row, col, at, height in runs[which]:
-                    outs[out][row : row + height, col : col + LANES] = half_ref[at : at + height]
+def place_kernel(runs, side_ref, mine_ref, other_ref, *refs):
+    *refs, sems = refs
+    count = len(refs) // 2
+    outs, places = refs[:count], refs[count:]
+    copies = []
+    for o, place_ref in enumerate(places):
+        for core in range(2):
+
+            @pl.when(side_ref[1] == core)
+            def _(core=core, o=o, place_ref=place_ref):
+                for which in range(2):
+                    half_ref = mine_ref if which == core else other_ref
+                    for out, row, col, at, height in runs[which]:
+                        if out == o:
+                            place_ref[row : row + height, col : col + LANES] = half_ref[at : at + height]
+
+        copies.append(pltpu.make_async_copy(place_ref, outs[o], sems.at[o]))
+        copies[o].start()
+    for copy in copies:
+        copy.wait()
 
 
 def swap(cells, axes, lead, closed):
@@ -357,7 +381,7 @@
     packed, hidden, grad_mixed = kernel_call(
         main_kernel,
         (
-            sides, bands, lat_near, state_field, lat_far, lon_near, lon_far,
+            sides, bands, lat_near, state_field, lat_far, lon_far, lon_near,
             basis_weight, weight_in, weight_out, cot_flat,
         ),
         [SMEM] + [VMEM] * 10,
@@ -371,9 +395,6 @@
     )
 
     arrived = swap(packed[1], CORE, 0, True)
-    chip = kernel_call(add_kernel, (packed, arrived), [VMEM] * 2, [half], name="add")[0]
-    shares = lax.all_to_all(chip.reshape(near, -1, LANES), NEAR, 0, 0)
-
     to_far, to_near, middle = kernel_call(
         adjoint_kernel,
         (sides, grad_mixed, basis_weight, bands),
@@ -386,6 +407,17 @@
         flops=4 * cells * channels * units,
         name="adjoint",
     )
+    chip = kernel_call(
+        add_kernel,
+        (packed, arrived, to_near),
+        [VMEM, VMEM, ANY],
+        [half],
+        [pltpu.VMEM(half.shape, bf16), pltpu.SemaphoreType.DMA((4,))],
+        name="add",
+        out_spec=ANY,
+    )[0]
+    shares = lax.all_to_all(chip.reshape(near, -1, LANES), NEAR, 0, 0)
+
     near_rim, far_rim = swap_both(to_near, to_far, LON, True)
     planes = sum_and_copy(shares, 1.0, far, near_rim, far_rim)
     planes = lax.all_to_all(planes, FAR, 0, 0)
@@ -415,7 +447,9 @@
         (sides, mine, other),
         [SMEM, VMEM, VMEM],
         [like(shape, bf16) for shape in shapes],
+        [*(pltpu.VMEM(shape, bf16) for shape in shapes), pltpu.SemaphoreType.DMA((3,))],
         name="place",
+        out_spec=ANY,
     )
     return (block_out, grad_field, grad_basis.reshape(basis_weight.shape), grad_in, grad_out)
 

time: 114 us -> 107 us (0.939)
  starting transfers between devices: 54 us -> 62 us
  waiting for transfers between devices: 20.4 us -> 12.6 us
  blocking collectives: 22.5 us -> 16.4 us
    ppermute x10, starting transfers between devices: 32.5 us -> 41.6 us  [swap(): return lax.ppermute(cells, axes, pairs)]
    ppermute x10, waiting for transfers between devices: 10.7 us -> 3.81 us  [swap(): return lax.ppermute(cells, axes, pairs)]
    all_to_all x1, blocking collectives: 22.5 us -> 16.4 us  [local(): mine = lax.all_to_all(copies, NEAR, 0, 0).reshape(-1, LANES)]
  transfers between devices with their start and end apart: 12 -> 12, of which waited for: 7 -> 8; matrix products, arithmetic and copies ran while one was open for 1% -> 1% of each run, Pallas kernels for 4% -> 4%
where the time goes in v5:
time: 107 us
  starting transfers between devices  62 us (58%)
  blocking collectives  16.4 us (15%)
  waiting for transfers between devices  12.6 us (12%)
  Pallas kernels  11.6 us (11%)
  local copies, waits for them, and re-layouts  2 us (2%)
    ppermute x10, starting transfers between devices, swap(): return lax.ppermute(cells, axes, pairs)  41.6 us
    all_to_all x1, blocking collectives, local(): mine = lax.all_to_all(copies, NEAR, 0, 0).reshape(-1, LANES)  16.4 us
    pallas_call x11, Pallas kernels, kernel_call(): pl.pallas_call(body, out_shape=tuple(outs), in_specs=specs, out_specs=tup...  11.6 us
    all_to_all x1, starting transfers between devices, local(): planes = lax.all_to_all(planes, FAR, 0, 0)  11.2 us
    all_to_all x1, starting transfers between devices, local(): shares = lax.all_to_all(chip.reshape(near, -1, LANES), NEAR, 0, 0)  9.23 us
    all_to_all x1, waiting for transfers between devices, local(): planes = lax.all_to_all(planes, FAR, 0, 0)  8.72 us
    ppermute x10, waiting for transfers between devices, swap(): return lax.ppermute(cells, axes, pairs)  3.81 us
  transfers between devices with their start and end apart: 12, of which 8 were waited for; matrix products, arithmetic and copies ran while one was open for 1% of the time, Pallas kernels for 4%

profile of v5, /device:TPU:1, one launch (start us, length us, event | category | flops | bytes accessed | tf_op | source)
XLA Modules:
  0.0 106.6 jit_solution(9352116143925351560)
XLA Ops:
  0.7 0.8 constant_dynamic-slice_fusion
  2.1 6.4 %collective-permute-start = (bf16[2,32,256]{2,1,0:T(8,128)(2,1)S(1)}, bf16[2,32,256]{2,1,0:T(8,128)(2,1)S(1)}, u32[]{:S(2)}, u32[]{:S(2)}) collective-permute-start(bf16[2,32,256]{2,1,0:T(8,128)(2,1)S(1)} %get-tuple-element.42), channel_id=1, source_target_pairs={{0,32},{32,0},{64,96},{96,64},{128,160},{160,128},{192,224},{224,1... | collective-permute-start | bytes 98312 | tf_op jit(solution)/shard_map/ppermute | solution.py:324
  8.6 0.8 bitcast_convert_fusion
  9.7 0.9 copy-done.2
  11.7 4.3 %collective-permute-start.2 = (bf16[12,8,256]{2,1,0:T(8,128)(2,1)S(1)}, bf16[12,8,256]{2,1,0:T(8,128)(2,1)S(1)}, u32[]{:S(2)}, u32[]{:S(2)}) collective-permute-start(bf16[12,8,256]{2,1,0:T(8,128)(2,1)S(1)} %get-tuple-element.25), channel_id=1, source_target_pairs={{1,2},{2,1},{3,4},{4,3},{5,6},{6,5},{7,8},{8,7},{9,10},{10,9},{11,... | collective-permute-start | bytes 147464 | tf_op jit(solution)/shard_map/ppermute | solution.py:324
  16.1 6.8 %collective-permute-start.3 = (bf16[12,8,256]{2,1,0:T(8,128)(2,1)S(1)}, bf16[12,8,256]{2,1,0:T(8,128)(2,1)S(1)}, u32[]{:S(2)}, u32[]{:S(2)}) collective-permute-start(bf16[12,8,256]{2,1,0:T(8,128)(2,1)S(1)} %get-tuple-element.26), channel_id=1, source_target_pairs={{0,1},{1,0},{2,3},{3,2},{4,5},{5,4},{6,7},{7,6},{8,9},{9,8},{10,11... | collective-permute-start | bytes 147464 | tf_op jit(solution)/shard_map/ppermute | solution.py:324
  23.8 2.9 %main.1 = (bf16[2,2816,128]{2,1,0:T(8,128)(2,1)S(1)}, bf16[256,1024]{1,0:T(8,128)(2,1)S(1)}, bf16[256,256]{1,0:T(8,128)(2,1)S(1)}) custom-call(s32[2]{0:T(128)S(1)} %pad_add_fusion.side_ref, bf16[8,192,256]{2,1,0:T(8,128)(2,1)S(1)} %bands.1.bands_ref, bf16[2,32,256]{2,1,0:T(8,128)(2,1)S(1)} %collective-permute-done.lat_near_ref, ...), custom_call_target="tpu_custom_call" | custom-call | flops 671088640 | bytes 4751368 | tf_op jit(solution)/shard_map/main/pallas_call | solution.py:39
  26.8 2.8 %collective-permute-start.8 = (bf16[2816,128]{1,0:T(8,128)(2,1)S(1)}, bf16[2816,128]{1,0:T(8,128)(2,1)S(1)}, u32[]{:S(2)}, u32[]{:S(2)}) collective-permute-start(bf16[2816,128]{1,0:T(8,128)(2,1)S(1)} %slice_bitcast_fusion), channel_id=1, source_target_pairs={{0,1},{1,0},{2,3},{3,2},{4,5},{5,4},{6,7},{7,6},{8,9},{9,8},{10,11... | collective-permute-start | bytes 2162696 | tf_op jit(solution)/shard_map/ppermute | solution.py:324
  29.6 1.4 %adjoint.1 = (bf16[12,8,256]{2,1,0:T(8,128)(2,1)S(1)}, bf16[12,8,256]{2,1,0:T(8,128)(2,1)S(1)}, f32[12,32,256]{2,1,0:T(8,128)S(1)}) custom-call(s32[2]{0:T(128)S(1)} %pad_add_fusion.side_ref, bf16[256,256]{1,0:T(8,128)(2,1)S(1)} %get-tuple-element.28.grad_ref, bf16[3,256,256]{2,1,0:T(8,128)(2,1)S(1)} %copy-done.4, bf16[8,192,256]{2,1,0:T(8,128)(2,1)S(1)} %bands.1.bands_ref), custom_call_target="tpu_custom_call" | custom-call | flops 268435456 | bytes 1802248 | tf_op jit(solution)/shard_map/adjoint/pallas_call | solution.py:39
  31.4 0.9 add.36
  32.3 9.2 %all-to-all-start = ((bf16[32,88,128]{2,1,0:T(8,128)(2,1)}), bf16[32,88,128]{2,1,0:T(8,128)(2,1)S(1)}, u32[]{:S(2)}, u32[]{:S(2)}) async-start(bf16[32,88,128]{2,1,0:T(8,128)(2,1)} %bitcast.6), calls=%async_computation | async-start | bytes 1441792 | tf_op jit(solution)/shard_map/all_to_all | solution.py:419
  41.5 3.9 %collective-permute-start.5 = (bf16[12,8,256]{2,1,0:T(8,128)(2,1)S(1)}, bf16[12,8,256]{2,1,0:T(8,128)(2,1)S(1)}, u32[]{:S(2)}, u32[]{:S(2)}) collective-permute-start(bf16[12,8,256]{2,1,0:T(8,128)(2,1)S(1)} %get-tuple-element.31), channel_id=1, source_target_pairs={{1,2},{2,1},{3,4},{4,3},{5,6},{6,5},{7,8},{8,7},{9,10},{10,9},{11,... | collective-permute-start | bytes 147464 | tf_op jit(solution)/shard_map/ppermute | solution.py:324
  45.5 7.4 %collective-permute-start.4 = (bf16[12,8,256]{2,1,0:T(8,128)(2,1)S(1)}, bf16[12,8,256]{2,1,0:T(8,128)(2,1)S(1)}, u32[]{:S(2)}, u32[]{:S(2)}) collective-permute-start(bf16[12,8,256]{2,1,0:T(8,128)(2,1)S(1)} %get-tuple-element.30.later_than_ref), channel_id=1, source_target_pairs={{0,1},{1,0},{2,3},{3,2},{4,5},{5,4},{6,7},{7,6},{8,9},{9,8},{10,11... | collective-permute-start | bytes 147464 | tf_op jit(solution)/shard_map/ppermute | solution.py:324
  53.0 0.7 collective-permute-done.4.near_ref.refs_0_
  53.8 0.8 sum_and_copy.2
  54.6 11.2 %all-to-all-start.1 = ((bf16[8,88,128]{2,1,0:T(8,128)(2,1)}), bf16[8,88,128]{2,1,0:T(8,128)(2,1)S(1)}, u32[]{:S(2)}, u32[]{:S(2)}) async-start(bf16[8,88,128]{2,1,0:T(8,128)(2,1)} %sum_and_copy.2), calls=%async_computation.1 | async-start | bytes 360448 | tf_op jit(solution)/shard_map/all_to_all | solution.py:423
  66.4 1.9 %collective-permute-start.6 = (bf16[2,32,256]{2,1,0:T(8,128)(2,1)S(1)}, bf16[2,32,256]{2,1,0:T(8,128)(2,1)S(1)}, u32[]{:S(2)}, u32[]{:S(2)}) collective-permute-start(bf16[2,32,256]{2,1,0:T(8,128)(2,1)S(1)} %get-tuple-element.33), channel_id=1, source_target_pairs={{0,32},{32,0},{64,96},{96,64},{128,160},{160,128},{192,224},{224,1... | collective-permute-start | bytes 98312 | tf_op jit(solution)/shard_map/ppermute | solution.py:324
  68.3 0.7 collective-permute-start.7
  69.0 2.1 %collective-permute-done.6.near_ref.refs_0_ = bf16[2,32,256]{2,1,0:T(8,128)(2,1)S(1)} collective-permute-done((bf16[2,32,256]{2,1,0:T(8,128)(2,1)S(1)}, bf16[2,32,256]{2,1,0:T(8,128)(2,1)S(1)}, u32[]{:S(2)}, u32[]{:S(2)}) %collective-permute-start.6) | collective-permute-done | bytes 32800 | tf_op jit(solution)/shard_map/ppermute | solution.py:324
  71.1 8.7 %all-to-all-done.1.parts_ref = bf16[8,88,128]{2,1,0:T(8,128)(2,1)S(1)} async-done(((bf16[8,88,128]{2,1,0:T(8,128)(2,1)}), bf16[8,88,128]{2,1,0:T(8,128)(2,1)S(1)}, u32[]{:S(2)}, u32[]{:S(2)}) %all-to-all-start.1) | async-done | bytes 180256 | tf_op jit(solution)/shard_map/all_to_all | solution.py:423
  79.9 16.4 %all_to_all.15 = bf16[32,88,128]{2,1,0:T(8,128)(2,1)S(1)} all-to-all(bf16[32,88,128]{2,1,0:T(8,128)(2,1)S(1)} %sum_and_copy.3), channel_id=1, replica_groups=mesh['z_hi'=4,'x'=4,'z_mid'=2,'z_low'=2,'y'=4,'core'=2] {'x','z_low','y'}, dimensions={0} | all-to-all | bytes 1441792 | tf_op jit(solution)/shard_map/all_to_all | solution.py:442
  96.3 6.7 %collective-permute-start.9 = (bf16[2816,128]{1,0:T(8,128)(2,1)S(1)}, bf16[2816,128]{1,0:T(8,128)(2,1)S(1)}, u32[]{:S(2)}, u32[]{:S(2)}) collective-permute-start(bf16[2816,128]{1,0:T(8,128)(2,1)S(1)} %bitcast.13), channel_id=1, source_target_pairs={{0,1},{1,0},{2,3},{3,2},{4,5},{5,4},{6,7},{7,6},{8,9},{9,8},{10,11... | collective-permute-start | bytes 2162696 | tf_op jit(solution)/shard_map/ppermute | solution.py:324
  103.0 1.5 %final.1 = (bf16[8,32,256]{2,1,0:T(8,128)(2,1)}, bf16[8,32,256]{2,1,0:T(8,128)(2,1)}) custom-call(s32[2]{0:T(128)S(1)} %pad_add_fusion.side_ref, bf16[256,1024]{1,0:T(8,128)(2,1)S(1)} %get-tuple-element.27.hidden_ref, bf16[1024,256]{1,0:T(8,128)(2,1)S(1)} %copy-done.1, bf16[8,32,256]{2,1,0:T(8,128)(2,1)S(1)} %copy-done.3, bf16[256,256]{1,0:T(8,128)(2,1)S(1)} %bitcast.16, ...), custom_call_target="tpu_custom_call" | custom-call | flops 134217728 | bytes 1900552 | tf_op jit(solution)/shard_map/final/pallas_call | solution.py:39
  104.8 1.8 %place.1 = (bf16[1024,256]{1,0:T(8,128)(2,1)}, bf16[256,1024]{1,0:T(8,128)(2,1)}, bf16[768,256]{1,0:T(8,128)(2,1)}) custom-call(s32[2]{0:T(128)S(1)} %pad_add_fusion.side_ref, bf16[2816,128]{1,0:T(8,128)(2,1)S(1)} %bitcast.14, bf16[2816,128]{1,0:T(8,128)(2,1)S(1)} %collective-permute-done.9.other_ref), custom_call_target="tpu_custom_call" | custom-call | bytes 2883592 | tf_op jit(solution)/shard_map/place/pallas_call | solution.py:39
  (33 shorter events, 4.4 us)
Async XLA Ops:
  0.6 7.9 %copy-start = (s32[128,5,8]{0,2,1:T(8,128)S(1)}, s32[128,5,8]{0,2,1:T(8,128)}, u32[]{:S(2)}) copy-start(s32[128,5,8]{0,2,1:T(8,128)} %param.8) | copy-start | bytes 61444
  1.5 9.7 %collective-permute-start.1 = (bf16[2,32,256]{2,1,0:T(8,128)(2,1)S(1)}, bf16[2,32,256]{2,1,0:T(8,128)(2,1)S(1)}, u32[]{:S(2)}, u32[]{:S(2)}) collective-permute-start(bf16[2,32,256]{2,1,0:T(8,128)(2,1)S(1)} %get-tuple-element.41), channel_id=1, source_target_pairs={{32,64},{64,32},{96,128},{128,96},{160,192},{192,160},{224,256},{2... | collective-permute-start | bytes 98312 | tf_op jit(solution)/shard_map/ppermute | solution.py:324
  2.1 9.1 %collective-permute-start = (bf16[2,32,256]{2,1,0:T(8,128)(2,1)S(1)}, bf16[2,32,256]{2,1,0:T(8,128)(2,1)S(1)}, u32[]{:S(2)}, u32[]{:S(2)}) collective-permute-start(bf16[2,32,256]{2,1,0:T(8,128)(2,1)S(1)} %get-tuple-element.42), channel_id=1, source_target_pairs={{0,32},{32,0},{64,96},{96,64},{128,160},{160,128},{192,224},{224,1... | collective-permute-start | bytes 98312 | tf_op jit(solution)/shard_map/ppermute | solution.py:324
  9.7 0.9 copy-start.2
  11.7 11.8 %collective-permute-start.2 = (bf16[12,8,256]{2,1,0:T(8,128)(2,1)S(1)}, bf16[12,8,256]{2,1,0:T(8,128)(2,1)S(1)}, u32[]{:S(2)}, u32[]{:S(2)}) collective-permute-start(bf16[12,8,256]{2,1,0:T(8,128)(2,1)S(1)} %get-tuple-element.25), channel_id=1, source_target_pairs={{1,2},{2,1},{3,4},{4,3},{5,6},{6,5},{7,8},{8,7},{9,10},{10,9},{11,... | collective-permute-start | bytes 147464 | tf_op jit(solution)/shard_map/ppermute | solution.py:324
  16.1 7.7 %copy-start.1 = (bf16[1024,256]{1,0:T(8,128)(2,1)S(1)}, bf16[1024,256]{1,0:T(8,128)(2,1)}, u32[]{:S(2)}) copy-start(bf16[1024,256]{1,0:T(8,128)(2,1)} %out_ref.3) | copy-start | bytes 1572868
  16.1 7.7 %copy-start.3 = (bf16[8,32,256]{2,1,0:T(8,128)(2,1)S(1)}, bf16[8,32,256]{2,1,0:T(8,128)(2,1)}, u32[]{:S(2)}) copy-start(bf16[8,32,256]{2,1,0:T(8,128)(2,1)} %state_ref.5) | copy-start | bytes 393220
  16.1 7.7 %copy-start.4 = (bf16[3,256,256]{2,1,0:T(8,128)(2,1)S(1)}, bf16[3,256,256]{2,1,0:T(8,128)(2,1)}, u32[]{:S(2)}) copy-start(bf16[3,256,256]{2,1,0:T(8,128)(2,1)} %mix_ref.3) | copy-start | bytes 1179652
  16.1 7.7 %copy-start.5 = (bf16[8,32,256]{2,1,0:T(8,128)(2,1)S(1)}, bf16[8,32,256]{2,1,0:T(8,128)(2,1)}, u32[]{:S(2)}) copy-start(bf16[8,32,256]{2,1,0:T(8,128)(2,1)} %param.13) | copy-start | bytes 393220
  16.1 7.7 %copy-start.6 = (bf16[256,1024]{1,0:T(8,128)(2,1)S(1)}, bf16[256,1024]{1,0:T(8,128)(2,1)}, u32[]{:S(2)}) copy-start(bf16[256,1024]{1,0:T(8,128)(2,1)} %in_ref.1) | copy-start | bytes 1572868
  16.1 7.7 %collective-permute-start.3 = (bf16[12,8,256]{2,1,0:T(8,128)(2,1)S(1)}, bf16[12,8,256]{2,1,0:T(8,128)(2,1)S(1)}, u32[]{:S(2)}, u32[]{:S(2)}) collective-permute-start(bf16[12,8,256]{2,1,0:T(8,128)(2,1)S(1)} %get-tuple-element.26), channel_id=1, source_target_pairs={{0,1},{1,0},{2,3},{3,2},{4,5},{5,4},{6,7},{7,6},{8,9},{9,8},{10,11... | collective-permute-start | bytes 147464 | tf_op jit(solution)/shard_map/ppermute | solution.py:324
  26.8 4.6 %collective-permute-start.8 = (bf16[2816,128]{1,0:T(8,128)(2,1)S(1)}, bf16[2816,128]{1,0:T(8,128)(2,1)S(1)}, u32[]{:S(2)}, u32[]{:S(2)}) collective-permute-start(bf16[2816,128]{1,0:T(8,128)(2,1)S(1)} %slice_bitcast_fusion), channel_id=1, source_target_pairs={{0,1},{1,0},{2,3},{3,2},{4,5},{5,4},{6,7},{7,6},{8,9},{9,8},{10,11... | collective-permute-start | bytes 2162696 | tf_op jit(solution)/shard_map/ppermute | solution.py:324
  32.3 21.5 %all-to-all-start = ((bf16[32,88,128]{2,1,0:T(8,128)(2,1)}), bf16[32,88,128]{2,1,0:T(8,128)(2,1)S(1)}, u32[]{:S(2)}, u32[]{:S(2)}) async-start(bf16[32,88,128]{2,1,0:T(8,128)(2,1)} %bitcast.6), calls=%async_computation | async-start | bytes 1441792 | tf_op jit(solution)/shard_map/all_to_all | solution.py:419
  41.5 11.5 %collective-permute-start.5 = (bf16[12,8,256]{2,1,0:T(8,128)(2,1)S(1)}, bf16[12,8,256]{2,1,0:T(8,128)(2,1)S(1)}, u32[]{:S(2)}, u32[]{:S(2)}) collective-permute-start(bf16[12,8,256]{2,1,0:T(8,128)(2,1)S(1)} %get-tuple-element.31), channel_id=1, source_target_pairs={{1,2},{2,1},{3,4},{4,3},{5,6},{6,5},{7,8},{8,7},{9,10},{10,9},{11,... | collective-permute-start | bytes 147464 | tf_op jit(solution)/shard_map/ppermute | solution.py:324
  45.5 8.2 %collective-permute-start.4 = (bf16[12,8,256]{2,1,0:T(8,128)(2,1)S(1)}, bf16[12,8,256]{2,1,0:T(8,128)(2,1)S(1)}, u32[]{:S(2)}, u32[]{:S(2)}) collective-permute-start(bf16[12,8,256]{2,1,0:T(8,128)(2,1)S(1)} %get-tuple-element.30.later_than_ref), channel_id=1, source_target_pairs={{0,1},{1,0},{2,3},{3,2},{4,5},{5,4},{6,7},{7,6},{8,9},{9,8},{10,11... | collective-permute-start | bytes 147464 | tf_op jit(solution)/shard_map/ppermute | solution.py:324
  54.6 25.2 %all-to-all-start.1 = ((bf16[8,88,128]{2,1,0:T(8,128)(2,1)}), bf16[8,88,128]{2,1,0:T(8,128)(2,1)S(1)}, u32[]{:S(2)}, u32[]{:S(2)}) async-start(bf16[8,88,128]{2,1,0:T(8,128)(2,1)} %sum_and_copy.2), calls=%async_computation.1 | async-start | bytes 360448 | tf_op jit(solution)/shard_map/all_to_all | solution.py:423
  66.4 4.7 %collective-permute-start.6 = (bf16[2,32,256]{2,1,0:T(8,128)(2,1)S(1)}, bf16[2,32,256]{2,1,0:T(8,128)(2,1)S(1)}, u32[]{:S(2)}, u32[]{:S(2)}) collective-permute-start(bf16[2,32,256]{2,1,0:T(8,128)(2,1)S(1)} %get-tuple-element.33), channel_id=1, source_target_pairs={{0,32},{32,0},{64,96},{96,64},{128,160},{160,128},{192,224},{224,1... | collective-permute-start | bytes 98312 | tf_op jit(solution)/shard_map/ppermute | solution.py:324
  68.3 2.7 %collective-permute-start.7 = (bf16[2,32,256]{2,1,0:T(8,128)(2,1)S(1)}, bf16[2,32,256]{2,1,0:T(8,128)(2,1)S(1)}, u32[]{:S(2)}, u32[]{:S(2)}) collective-permute-start(bf16[2,32,256]{2,1,0:T(8,128)(2,1)S(1)} %get-tuple-element.34), channel_id=1, source_target_pairs={{32,64},{64,32},{96,128},{128,96},{160,192},{192,160},{224,256},{2... | collective-permute-start | bytes 98312 | tf_op jit(solution)/shard_map/ppermute | solution.py:324
  96.3 8.5 %collective-permute-start.9 = (bf16[2816,128]{1,0:T(8,128)(2,1)S(1)}, bf16[2816,128]{1,0:T(8,128)(2,1)S(1)}, u32[]{:S(2)}, u32[]{:S(2)}) collective-permute-start(bf16[2816,128]{1,0:T(8,128)(2,1)S(1)} %bitcast.13), channel_id=1, source_target_pairs={{0,1},{1,0},{2,3},{3,2},{4,5},{5,4},{6,7},{7,6},{8,9},{9,8},{10,11... | collective-permute-start | bytes 2162696 | tf_op jit(solution)/shard_map/ppermute | solution.py:324

commit v6 on v5

--- a/solution.py
+++ b/solution.py
@@ -20,7 +20,7 @@
 NEAR = ("x", "z_low", "y")
 FAR = ("z_hi", "z_mid")
 LANES = 128
-CHUNK = 256
+CHUNK = 1024
 
 ROWS, COLS = ((0,), (0,)), ((1,), (1,))
 VMEM = pl.BlockSpec(memory_space=pltpu.VMEM)

time: 107 us -> 107 us (level)
  no operation moved by 1% of the time
where the time goes in v6:
time: 107 us; the launch traced here: 106 us
  starting transfers between devices  62 us (58%)
  blocking collectives  16.4 us (15%)
  waiting for transfers between devices  12.6 us (12%)
  Pallas kernels  11.3 us (11%)
  local copies, waits for them, and re-layouts  2 us (2%)
    ppermute x10, starting transfers between devices, swap(): return lax.ppermute(cells, axes, pairs)  41.6 us
    all_to_all x1, blocking collectives, local(): mine = lax.all_to_all(copies, NEAR, 0, 0).reshape(-1, LANES)  16.4 us
    pallas_call x11, Pallas kernels, kernel_call(): pl.pallas_call(body, out_shape=tuple(outs), in_specs=specs, out_specs=tup...  11.3 us
    all_to_all x1, starting transfers between devices, local(): planes = lax.all_to_all(planes, FAR, 0, 0)  11.2 us
    all_to_all x1, starting transfers between devices, local(): shares = lax.all_to_all(chip.reshape(near, -1, LANES), NEAR, 0, 0)  9.23 us
    all_to_all x1, waiting for transfers between devices, local(): planes = lax.all_to_all(planes, FAR, 0, 0)  8.72 us
    ppermute x10, waiting for transfers between devices, swap(): return lax.ppermute(cells, axes, pairs)  3.82 us
  transfers between devices with their start and end apart: 12, of which 8 were waited for; matrix products, arithmetic and copies ran while one was open for 1% of the time, Pallas kernels for 4%

profile of v6, /device:TPU:1, one launch (start us, length us, event | category | flops | bytes accessed | tf_op | source)
XLA Modules:
  0.0 106.3 jit_solution(10702440689918906871)
XLA Ops:
  0.7 0.8 constant_dynamic-slice_fusion
  2.1 6.4 %collective-permute-start = (bf16[2,32,256]{2,1,0:T(8,128)(2,1)S(1)}, bf16[2,32,256]{2,1,0:T(8,128)(2,1)S(1)}, u32[]{:S(2)}, u32[]{:S(2)}) collective-permute-start(bf16[2,32,256]{2,1,0:T(8,128)(2,1)S(1)} %get-tuple-element.42), channel_id=1, source_target_pairs={{0,32},{32,0},{64,96},{96,64},{128,160},{160,128},{192,224},{224,1... | collective-permute-start | bytes 98312 | tf_op jit(solution)/shard_map/ppermute | solution.py:324
  8.6 0.8 bitcast_convert_fusion
  9.7 0.9 copy-done.2
  11.7 4.3 %collective-permute-start.2 = (bf16[12,8,256]{2,1,0:T(8,128)(2,1)S(1)}, bf16[12,8,256]{2,1,0:T(8,128)(2,1)S(1)}, u32[]{:S(2)}, u32[]{:S(2)}) collective-permute-start(bf16[12,8,256]{2,1,0:T(8,128)(2,1)S(1)} %get-tuple-element.25), channel_id=1, source_target_pairs={{1,2},{2,1},{3,4},{4,3},{5,6},{6,5},{7,8},{8,7},{9,10},{10,9},{11,... | collective-permute-start | bytes 147464 | tf_op jit(solution)/shard_map/ppermute | solution.py:324
  16.1 6.8 %collective-permute-start.3 = (bf16[12,8,256]{2,1,0:T(8,128)(2,1)S(1)}, bf16[12,8,256]{2,1,0:T(8,128)(2,1)S(1)}, u32[]{:S(2)}, u32[]{:S(2)}) collective-permute-start(bf16[12,8,256]{2,1,0:T(8,128)(2,1)S(1)} %get-tuple-element.26), channel_id=1, source_target_pairs={{0,1},{1,0},{2,3},{3,2},{4,5},{5,4},{6,7},{7,6},{8,9},{9,8},{10,11... | collective-permute-start | bytes 147464 | tf_op jit(solution)/shard_map/ppermute | solution.py:324
  23.8 2.6 %main.1 = (bf16[2,2816,128]{2,1,0:T(8,128)(2,1)S(1)}, bf16[256,1024]{1,0:T(8,128)(2,1)S(1)}, bf16[256,256]{1,0:T(8,128)(2,1)S(1)}) custom-call(s32[2]{0:T(128)S(1)} %pad_add_fusion.side_ref, bf16[8,192,256]{2,1,0:T(8,128)(2,1)S(1)} %bands.1.bands_ref, bf16[2,32,256]{2,1,0:T(8,128)(2,1)S(1)} %collective-permute-done.lat_near_ref, ...), custom_call_target="tpu_custom_call" | custom-call | flops 671088640 | bytes 4751368 | tf_op jit(solution)/shard_map/main/pallas_call | solution.py:39
  26.5 2.8 %collective-permute-start.8 = (bf16[2816,128]{1,0:T(8,128)(2,1)S(1)}, bf16[2816,128]{1,0:T(8,128)(2,1)S(1)}, u32[]{:S(2)}, u32[]{:S(2)}) collective-permute-start(bf16[2816,128]{1,0:T(8,128)(2,1)S(1)} %slice_bitcast_fusion), channel_id=1, source_target_pairs={{0,1},{1,0},{2,3},{3,2},{4,5},{5,4},{6,7},{7,6},{8,9},{9,8},{10,11... | collective-permute-start | bytes 2162696 | tf_op jit(solution)/shard_map/ppermute | solution.py:324
  29.3 1.4 %adjoint.1 = (bf16[12,8,256]{2,1,0:T(8,128)(2,1)S(1)}, bf16[12,8,256]{2,1,0:T(8,128)(2,1)S(1)}, f32[12,32,256]{2,1,0:T(8,128)S(1)}) custom-call(s32[2]{0:T(128)S(1)} %pad_add_fusion.side_ref, bf16[256,256]{1,0:T(8,128)(2,1)S(1)} %get-tuple-element.28.grad_ref, bf16[3,256,256]{2,1,0:T(8,128)(2,1)S(1)} %copy-done.4, bf16[8,192,256]{2,1,0:T(8,128)(2,1)S(1)} %bands.1.bands_ref), custom_call_target="tpu_custom_call" | custom-call | flops 268435456 | bytes 1802248 | tf_op jit(solution)/shard_map/adjoint/pallas_call | solution.py:39
  31.1 0.9 add.36
  32.0 9.2 %all-to-all-start = ((bf16[32,88,128]{2,1,0:T(8,128)(2,1)}), bf16[32,88,128]{2,1,0:T(8,128)(2,1)S(1)}, u32[]{:S(2)}, u32[]{:S(2)}) async-start(bf16[32,88,128]{2,1,0:T(8,128)(2,1)} %bitcast.6), calls=%async_computation | async-start | bytes 1441792 | tf_op jit(solution)/shard_map/all_to_all | solution.py:419
  41.3 3.9 %collective-permute-start.5 = (bf16[12,8,256]{2,1,0:T(8,128)(2,1)S(1)}, bf16[12,8,256]{2,1,0:T(8,128)(2,1)S(1)}, u32[]{:S(2)}, u32[]{:S(2)}) collective-permute-start(bf16[12,8,256]{2,1,0:T(8,128)(2,1)S(1)} %get-tuple-element.31), channel_id=1, source_target_pairs={{1,2},{2,1},{3,4},{4,3},{5,6},{6,5},{7,8},{8,7},{9,10},{10,9},{11,... | collective-permute-start | bytes 147464 | tf_op jit(solution)/shard_map/ppermute | solution.py:324
  45.2 7.4 %collective-permute-start.4 = (bf16[12,8,256]{2,1,0:T(8,128)(2,1)S(1)}, bf16[12,8,256]{2,1,0:T(8,128)(2,1)S(1)}, u32[]{:S(2)}, u32[]{:S(2)}) collective-permute-start(bf16[12,8,256]{2,1,0:T(8,128)(2,1)S(1)} %get-tuple-element.30.later_than_ref), channel_id=1, source_target_pairs={{0,1},{1,0},{2,3},{3,2},{4,5},{5,4},{6,7},{7,6},{8,9},{9,8},{10,11... | collective-permute-start | bytes 147464 | tf_op jit(solution)/shard_map/ppermute | solution.py:324
  52.7 0.7 collective-permute-done.4.near_ref.refs_0_
  53.5 0.8 sum_and_copy.2
  54.3 11.2 %all-to-all-start.1 = ((bf16[8,88,128]{2,1,0:T(8,128)(2,1)}), bf16[8,88,128]{2,1,0:T(8,128)(2,1)S(1)}, u32[]{:S(2)}, u32[]{:S(2)}) async-start(bf16[8,88,128]{2,1,0:T(8,128)(2,1)} %sum_and_copy.2), calls=%async_computation.1 | async-start | bytes 360448 | tf_op jit(solution)/shard_map/all_to_all | solution.py:423
  66.1 1.9 %collective-permute-start.6 = (bf16[2,32,256]{2,1,0:T(8,128)(2,1)S(1)}, bf16[2,32,256]{2,1,0:T(8,128)(2,1)S(1)}, u32[]{:S(2)}, u32[]{:S(2)}) collective-permute-start(bf16[2,32,256]{2,1,0:T(8,128)(2,1)S(1)} %get-tuple-element.33), channel_id=1, source_target_pairs={{0,32},{32,0},{64,96},{96,64},{128,160},{160,128},{192,224},{224,1... | collective-permute-start | bytes 98312 | tf_op jit(solution)/shard_map/ppermute | solution.py:324
  68.0 0.7 collective-permute-start.7
  68.7 2.1 %collective-permute-done.6.near_ref.refs_0_ = bf16[2,32,256]{2,1,0:T(8,128)(2,1)S(1)} collective-permute-done((bf16[2,32,256]{2,1,0:T(8,128)(2,1)S(1)}, bf16[2,32,256]{2,1,0:T(8,128)(2,1)S(1)}, u32[]{:S(2)}, u32[]{:S(2)}) %collective-permute-start.6) | collective-permute-done | bytes 32800 | tf_op jit(solution)/shard_map/ppermute | solution.py:324
  70.8 8.7 %all-to-all-done.1.parts_ref = bf16[8,88,128]{2,1,0:T(8,128)(2,1)S(1)} async-done(((bf16[8,88,128]{2,1,0:T(8,128)(2,1)}), bf16[8,88,128]{2,1,0:T(8,128)(2,1)S(1)}, u32[]{:S(2)}, u32[]{:S(2)}) %all-to-all-start.1) | async-done | bytes 180256 | tf_op jit(solution)/shard_map/all_to_all | solution.py:423
  79.6 16.4 %all_to_all.15 = bf16[32,88,128]{2,1,0:T(8,128)(2,1)S(1)} all-to-all(bf16[32,88,128]{2,1,0:T(8,128)(2,1)S(1)} %sum_and_copy.3), channel_id=1, replica_groups=mesh['z_hi'=4,'x'=4,'z_mid'=2,'z_low'=2,'y'=4,'core'=2] {'x','z_low','y'}, dimensions={0} | all-to-all | bytes 1441792 | tf_op jit(solution)/shard_map/all_to_all | solution.py:442
  96.0 6.7 %collective-permute-start.9 = (bf16[2816,128]{1,0:T(8,128)(2,1)S(1)}, bf16[2816,128]{1,0:T(8,128)(2,1)S(1)}, u32[]{:S(2)}, u32[]{:S(2)}) collective-permute-start(bf16[2816,128]{1,0:T(8,128)(2,1)S(1)} %bitcast.13), channel_id=1, source_target_pairs={{0,1},{1,0},{2,3},{3,2},{4,5},{5,4},{6,7},{7,6},{8,9},{9,8},{10,11... | collective-permute-start | bytes 2162696 | tf_op jit(solution)/shard_map/ppermute | solution.py:324
  102.7 1.5 %final.1 = (bf16[8,32,256]{2,1,0:T(8,128)(2,1)}, bf16[8,32,256]{2,1,0:T(8,128)(2,1)}) custom-call(s32[2]{0:T(128)S(1)} %pad_add_fusion.side_ref, bf16[256,1024]{1,0:T(8,128)(2,1)S(1)} %get-tuple-element.27.hidden_ref, bf16[1024,256]{1,0:T(8,128)(2,1)S(1)} %copy-done.1, bf16[8,32,256]{2,1,0:T(8,128)(2,1)S(1)} %copy-done.3, bf16[256,256]{1,0:T(8,128)(2,1)S(1)} %bitcast.16, ...), custom_call_target="tpu_custom_call" | custom-call | flops 134217728 | bytes 1900552 | tf_op jit(solution)/shard_map/final/pallas_call | solution.py:39
  104.5 1.8 %place.1 = (bf16[1024,256]{1,0:T(8,128)(2,1)}, bf16[256,1024]{1,0:T(8,128)(2,1)}, bf16[768,256]{1,0:T(8,128)(2,1)}) custom-call(s32[2]{0:T(128)S(1)} %pad_add_fusion.side_ref, bf16[2816,128]{1,0:T(8,128)(2,1)S(1)} %bitcast.14, bf16[2816,128]{1,0:T(8,128)(2,1)S(1)} %collective-permute-done.9.other_ref), custom_call_target="tpu_custom_call" | custom-call | bytes 2883592 | tf_op jit(solution)/shard_map/place/pallas_call | solution.py:39
  (33 shorter events, 4.4 us)
Async XLA Ops:
  0.6 7.9 %copy-start = (s32[128,5,8]{0,2,1:T(8,128)S(1)}, s32[128,5,8]{0,2,1:T(8,128)}, u32[]{:S(2)}) copy-start(s32[128,5,8]{0,2,1:T(8,128)} %param.8) | copy-start | bytes 61444
  1.5 9.7 %collective-permute-start.1 = (bf16[2,32,256]{2,1,0:T(8,128)(2,1)S(1)}, bf16[2,32,256]{2,1,0:T(8,128)(2,1)S(1)}, u32[]{:S(2)}, u32[]{:S(2)}) collective-permute-start(bf16[2,32,256]{2,1,0:T(8,128)(2,1)S(1)} %get-tuple-element.41), channel_id=1, source_target_pairs={{32,64},{64,32},{96,128},{128,96},{160,192},{192,160},{224,256},{2... | collective-permute-start | bytes 98312 | tf_op jit(solution)/shard_map/ppermute | solution.py:324
  2.1 9.1 %collective-permute-start = (bf16[2,32,256]{2,1,0:T(8,128)(2,1)S(1)}, bf16[2,32,256]{2,1,0:T(8,128)(2,1)S(1)}, u32[]{:S(2)}, u32[]{:S(2)}) collective-permute-start(bf16[2,32,256]{2,1,0:T(8,128)(2,1)S(1)} %get-tuple-element.42), channel_id=1, source_target_pairs={{0,32},{32,0},{64,96},{96,64},{128,160},{160,128},{192,224},{224,1... | collective-permute-start | bytes 98312 | tf_op jit(solution)/shard_map/ppermute | solution.py:324
  9.7 0.9 copy-start.2
  11.7 11.8 %collective-permute-start.2 = (bf16[12,8,256]{2,1,0:T(8,128)(2,1)S(1)}, bf16[12,8,256]{2,1,0:T(8,128)(2,1)S(1)}, u32[]{:S(2)}, u32[]{:S(2)}) collective-permute-start(bf16[12,8,256]{2,1,0:T(8,128)(2,1)S(1)} %get-tuple-element.25), channel_id=1, source_target_pairs={{1,2},{2,1},{3,4},{4,3},{5,6},{6,5},{7,8},{8,7},{9,10},{10,9},{11,... | collective-permute-start | bytes 147464 | tf_op jit(solution)/shard_map/ppermute | solution.py:324
  16.1 7.7 %copy-start.1 = (bf16[1024,256]{1,0:T(8,128)(2,1)S(1)}, bf16[1024,256]{1,0:T(8,128)(2,1)}, u32[]{:S(2)}) copy-start(bf16[1024,256]{1,0:T(8,128)(2,1)} %out_ref.3) | copy-start | bytes 1572868
  16.1 7.7 %copy-start.3 = (bf16[8,32,256]{2,1,0:T(8,128)(2,1)S(1)}, bf16[8,32,256]{2,1,0:T(8,128)(2,1)}, u32[]{:S(2)}) copy-start(bf16[8,32,256]{2,1,0:T(8,128)(2,1)} %state_ref.5) | copy-start | bytes 393220
  16.1 7.7 %copy-start.4 = (bf16[3,256,256]{2,1,0:T(8,128)(2,1)S(1)}, bf16[3,256,256]{2,1,0:T(8,128)(2,1)}, u32[]{:S(2)}) copy-start(bf16[3,256,256]{2,1,0:T(8,128)(2,1)} %mix_ref.3) | copy-start | bytes 1179652
  16.1 7.7 %copy-start.5 = (bf16[8,32,256]{2,1,0:T(8,128)(2,1)S(1)}, bf16[8,32,256]{2,1,0:T(8,128)(2,1)}, u32[]{:S(2)}) copy-start(bf16[8,32,256]{2,1,0:T(8,128)(2,1)} %param.13) | copy-start | bytes 393220
  16.1 7.7 %copy-start.6 = (bf16[256,1024]{1,0:T(8,128)(2,1)S(1)}, bf16[256,1024]{1,0:T(8,128)(2,1)}, u32[]{:S(2)}) copy-start(bf16[256,1024]{1,0:T(8,128)(2,1)} %in_ref.1) | copy-start | bytes 1572868
  16.1 7.7 %collective-permute-start.3 = (bf16[12,8,256]{2,1,0:T(8,128)(2,1)S(1)}, bf16[12,8,256]{2,1,0:T(8,128)(2,1)S(1)}, u32[]{:S(2)}, u32[]{:S(2)}) collective-permute-start(bf16[12,8,256]{2,1,0:T(8,128)(2,1)S(1)} %get-tuple-element.26), channel_id=1, source_target_pairs={{0,1},{1,0},{2,3},{3,2},{4,5},{5,4},{6,7},{7,6},{8,9},{9,8},{10,11... | collective-permute-start | bytes 147464 | tf_op jit(solution)/shard_map/ppermute | solution.py:324
  26.5 4.6 %collective-permute-start.8 = (bf16[2816,128]{1,0:T(8,128)(2,1)S(1)}, bf16[2816,128]{1,0:T(8,128)(2,1)S(1)}, u32[]{:S(2)}, u32[]{:S(2)}) collective-permute-start(bf16[2816,128]{1,0:T(8,128)(2,1)S(1)} %slice_bitcast_fusion), channel_id=1, source_target_pairs={{0,1},{1,0},{2,3},{3,2},{4,5},{5,4},{6,7},{7,6},{8,9},{9,8},{10,11... | collective-permute-start | bytes 2162696 | tf_op jit(solution)/shard_map/ppermute | solution.py:324
  32.0 21.5 %all-to-all-start = ((bf16[32,88,128]{2,1,0:T(8,128)(2,1)}), bf16[32,88,128]{2,1,0:T(8,128)(2,1)S(1)}, u32[]{:S(2)}, u32[]{:S(2)}) async-start(bf16[32,88,128]{2,1,0:T(8,128)(2,1)} %bitcast.6), calls=%async_computation | async-start | bytes 1441792 | tf_op jit(solution)/shard_map/all_to_all | solution.py:419
  41.3 11.5 %collective-permute-start.5 = (bf16[12,8,256]{2,1,0:T(8,128)(2,1)S(1)}, bf16[12,8,256]{2,1,0:T(8,128)(2,1)S(1)}, u32[]{:S(2)}, u32[]{:S(2)}) collective-permute-start(bf16[12,8,256]{2,1,0:T(8,128)(2,1)S(1)} %get-tuple-element.31), channel_id=1, source_target_pairs={{1,2},{2,1},{3,4},{4,3},{5,6},{6,5},{7,8},{8,7},{9,10},{10,9},{11,... | collective-permute-start | bytes 147464 | tf_op jit(solution)/shard_map/ppermute | solution.py:324
  45.2 8.3 %collective-permute-start.4 = (bf16[12,8,256]{2,1,0:T(8,128)(2,1)S(1)}, bf16[12,8,256]{2,1,0:T(8,128)(2,1)S(1)}, u32[]{:S(2)}, u32[]{:S(2)}) collective-permute-start(bf16[12,8,256]{2,1,0:T(8,128)(2,1)S(1)} %get-tuple-element.30.later_than_ref), channel_id=1, source_target_pairs={{0,1},{1,0},{2,3},{3,2},{4,5},{5,4},{6,7},{7,6},{8,9},{9,8},{10,11... | collective-permute-start | bytes 147464 | tf_op jit(solution)/shard_map/ppermute | solution.py:324
  54.3 25.2 %all-to-all-start.1 = ((bf16[8,88,128]{2,1,0:T(8,128)(2,1)}), bf16[8,88,128]{2,1,0:T(8,128)(2,1)S(1)}, u32[]{:S(2)}, u32[]{:S(2)}) async-start(bf16[8,88,128]{2,1,0:T(8,128)(2,1)} %sum_and_copy.2), calls=%async_computation.1 | async-start | bytes 360448 | tf_op jit(solution)/shard_map/all_to_all | solution.py:423
  66.1 4.7 %collective-permute-start.6 = (bf16[2,32,256]{2,1,0:T(8,128)(2,1)S(1)}, bf16[2,32,256]{2,1,0:T(8,128)(2,1)S(1)}, u32[]{:S(2)}, u32[]{:S(2)}) collective-permute-start(bf16[2,32,256]{2,1,0:T(8,128)(2,1)S(1)} %get-tuple-element.33), channel_id=1, source_target_pairs={{0,32},{32,0},{64,96},{96,64},{128,160},{160,128},{192,224},{224,1... | collective-permute-start | bytes 98312 | tf_op jit(solution)/shard_map/ppermute | solution.py:324
  68.0 2.7 %collective-permute-start.7 = (bf16[2,32,256]{2,1,0:T(8,128)(2,1)S(1)}, bf16[2,32,256]{2,1,0:T(8,128)(2,1)S(1)}, u32[]{:S(2)}, u32[]{:S(2)}) collective-permute-start(bf16[2,32,256]{2,1,0:T(8,128)(2,1)S(1)} %get-tuple-element.34), channel_id=1, source_target_pairs={{32,64},{64,32},{96,128},{128,96},{160,192},{192,160},{224,256},{2... | collective-permute-start | bytes 98312 | tf_op jit(solution)/shard_map/ppermute | solution.py:324
  96.0 8.5 %collective-permute-start.9 = (bf16[2816,128]{1,0:T(8,128)(2,1)S(1)}, bf16[2816,128]{1,0:T(8,128)(2,1)S(1)}, u32[]{:S(2)}, u32[]{:S(2)}) collective-permute-start(bf16[2816,128]{1,0:T(8,128)(2,1)S(1)} %bitcast.13), channel_id=1, source_target_pairs={{0,1},{1,0},{2,3},{3,2},{4,5},{5,4},{6,7},{7,6},{8,9},{9,8},{10,11... | collective-permute-start | bytes 2162696 | tf_op jit(solution)/shard_map/ppermute | solution.py:324

commit v7 on v6

--- a/solution.py
+++ b/solution.py
@@ -33,7 +33,7 @@
 
 
 def kernel_call(
-    body, operands, specs, outs, scratch=(), flops=0, mib=16, name=None, out_spec=VMEM
+    body, operands, specs, outs, scratch=(), flops=0, mib=40, name=None, out_spec=VMEM
 ):
     moved = sum(x.size * x.dtype.itemsize for x in (*operands, *outs))
     return pl.pallas_call(
@@ -274,7 +274,7 @@
         [VMEM] + [ANY] * len(later_than),
         [like((copies,) + parts.shape[1:], jnp.bfloat16)],
         flops=parts.size,
-        mib=16,
+        mib=40,
         name="sum_and_copy",
     )[0]
 
@@ -412,7 +412,7 @@
         (packed, arrived, to_near),
         [VMEM, VMEM, ANY],
         [half],
-        [pltpu.VMEM(half.shape, bf16), pltpu.SemaphoreType.DMA((4,))],
+        [pltpu.VMEM(half.shape, bf16), pltpu.SemaphoreType.DMA((2,))],
         name="add",
         out_spec=ANY,
     )[0]

time: 107 us -> 107 us (level)
  no operation moved by 1% of the time
where the time goes in v7:
time: 107 us; the launch traced here: 106 us
  starting transfers between devices  62 us (58%)
  blocking collectives  16.4 us (15%)
  waiting for transfers between devices  12.6 us (12%)
  Pallas kernels  11.4 us (11%)
  local copies, waits for them, and re-layouts  2 us (2%)
    ppermute x10, starting transfers between devices, swap(): return lax.ppermute(cells, axes, pairs)  41.6 us
    all_to_all x1, blocking collectives, local(): mine = lax.all_to_all(copies, NEAR, 0, 0).reshape(-1, LANES)  16.4 us
    pallas_call x11, Pallas kernels, kernel_call(): pl.pallas_call(body, out_shape=tuple(outs), in_specs=specs, out_specs=tup...  11.4 us
    all_to_all x1, starting transfers between devices, local(): planes = lax.all_to_all(planes, FAR, 0, 0)  11.2 us
    all_to_all x1, starting transfers between devices, local(): shares = lax.all_to_all(chip.reshape(near, -1, LANES), NEAR, 0, 0)  9.23 us
    all_to_all x1, waiting for transfers between devices, local(): planes = lax.all_to_all(planes, FAR, 0, 0)  8.72 us
    ppermute x10, waiting for transfers between devices, swap(): return lax.ppermute(cells, axes, pairs)  3.82 us
  transfers between devices with their start and end apart: 12, of which 8 were waited for; matrix products, arithmetic and copies ran while one was open for 1% of the time, Pallas kernels for 4%

profile of v7, /device:TPU:1, one launch (start us, length us, event | category | flops | bytes accessed | tf_op | source)
XLA Modules:
  0.0 106.3 jit_solution(5154599454174447905)
XLA Ops:
  0.7 0.8 constant_dynamic-slice_fusion
  2.1 6.4 %collective-permute-start = (bf16[2,32,256]{2,1,0:T(8,128)(2,1)S(1)}, bf16[2,32,256]{2,1,0:T(8,128)(2,1)S(1)}, u32[]{:S(2)}, u32[]{:S(2)}) collective-permute-start(bf16[2,32,256]{2,1,0:T(8,128)(2,1)S(1)} %get-tuple-element.42), channel_id=1, source_target_pairs={{0,32},{32,0},{64,96},{96,64},{128,160},{160,128},{192,224},{224,1... | collective-permute-start | bytes 98312 | tf_op jit(solution)/shard_map/ppermute | solution.py:324
  8.6 0.8 bitcast_convert_fusion
  9.7 0.9 copy-done.2
  11.7 4.3 %collective-permute-start.2 = (bf16[12,8,256]{2,1,0:T(8,128)(2,1)S(1)}, bf16[12,8,256]{2,1,0:T(8,128)(2,1)S(1)}, u32[]{:S(2)}, u32[]{:S(2)}) collective-permute-start(bf16[12,8,256]{2,1,0:T(8,128)(2,1)S(1)} %get-tuple-element.25), channel_id=1, source_target_pairs={{1,2},{2,1},{3,4},{4,3},{5,6},{6,5},{7,8},{8,7},{9,10},{10,9},{11,... | collective-permute-start | bytes 147464 | tf_op jit(solution)/shard_map/ppermute | solution.py:324
  16.1 6.8 %collective-permute-start.3 = (bf16[12,8,256]{2,1,0:T(8,128)(2,1)S(1)}, bf16[12,8,256]{2,1,0:T(8,128)(2,1)S(1)}, u32[]{:S(2)}, u32[]{:S(2)}) collective-permute-start(bf16[12,8,256]{2,1,0:T(8,128)(2,1)S(1)} %get-tuple-element.26), channel_id=1, source_target_pairs={{0,1},{1,0},{2,3},{3,2},{4,5},{5,4},{6,7},{7,6},{8,9},{9,8},{10,11... | collective-permute-start | bytes 147464 | tf_op jit(solution)/shard_map/ppermute | solution.py:324
  23.8 2.6 %main.1 = (bf16[2,2816,128]{2,1,0:T(8,128)(2,1)S(1)}, bf16[256,1024]{1,0:T(8,128)(2,1)S(1)}, bf16[256,256]{1,0:T(8,128)(2,1)S(1)}) custom-call(s32[2]{0:T(128)S(1)} %pad_add_fusion.side_ref, bf16[8,192,256]{2,1,0:T(8,128)(2,1)S(1)} %bands.1.bands_ref, bf16[2,32,256]{2,1,0:T(8,128)(2,1)S(1)} %collective-permute-done.lat_near_ref, ...), custom_call_target="tpu_custom_call" | custom-call | flops 671088640 | bytes 4751368 | tf_op jit(solution)/shard_map/main/pallas_call | solution.py:39
  26.5 2.8 %collective-permute-start.8 = (bf16[2816,128]{1,0:T(8,128)(2,1)S(1)}, bf16[2816,128]{1,0:T(8,128)(2,1)S(1)}, u32[]{:S(2)}, u32[]{:S(2)}) collective-permute-start(bf16[2816,128]{1,0:T(8,128)(2,1)S(1)} %slice_bitcast_fusion), channel_id=1, source_target_pairs={{0,1},{1,0},{2,3},{3,2},{4,5},{5,4},{6,7},{7,6},{8,9},{9,8},{10,11... | collective-permute-start | bytes 2162696 | tf_op jit(solution)/shard_map/ppermute | solution.py:324
  29.3 1.4 %adjoint.1 = (bf16[12,8,256]{2,1,0:T(8,128)(2,1)S(1)}, bf16[12,8,256]{2,1,0:T(8,128)(2,1)S(1)}, f32[12,32,256]{2,1,0:T(8,128)S(1)}) custom-call(s32[2]{0:T(128)S(1)} %pad_add_fusion.side_ref, bf16[256,256]{1,0:T(8,128)(2,1)S(1)} %get-tuple-element.28.grad_ref, bf16[3,256,256]{2,1,0:T(8,128)(2,1)S(1)} %copy-done.4, bf16[8,192,256]{2,1,0:T(8,128)(2,1)S(1)} %bands.1.bands_ref), custom_call_target="tpu_custom_call" | custom-call | flops 268435456 | bytes 1802248 | tf_op jit(solution)/shard_map/adjoint/pallas_call | solution.py:39
  31.1 1.0 add.36
  32.0 9.2 %all-to-all-start = ((bf16[32,88,128]{2,1,0:T(8,128)(2,1)}), bf16[32,88,128]{2,1,0:T(8,128)(2,1)S(1)}, u32[]{:S(2)}, u32[]{:S(2)}) async-start(bf16[32,88,128]{2,1,0:T(8,128)(2,1)} %bitcast.6), calls=%async_computation | async-start | bytes 1441792 | tf_op jit(solution)/shard_map/all_to_all | solution.py:419
  41.3 3.9 %collective-permute-start.5 = (bf16[12,8,256]{2,1,0:T(8,128)(2,1)S(1)}, bf16[12,8,256]{2,1,0:T(8,128)(2,1)S(1)}, u32[]{:S(2)}, u32[]{:S(2)}) collective-permute-start(bf16[12,8,256]{2,1,0:T(8,128)(2,1)S(1)} %get-tuple-element.31), channel_id=1, source_target_pairs={{1,2},{2,1},{3,4},{4,3},{5,6},{6,5},{7,8},{8,7},{9,10},{10,9},{11,... | collective-permute-start | bytes 147464 | tf_op jit(solution)/shard_map/ppermute | solution.py:324
  45.2 7.4 %collective-permute-start.4 = (bf16[12,8,256]{2,1,0:T(8,128)(2,1)S(1)}, bf16[12,8,256]{2,1,0:T(8,128)(2,1)S(1)}, u32[]{:S(2)}, u32[]{:S(2)}) collective-permute-start(bf16[12,8,256]{2,1,0:T(8,128)(2,1)S(1)} %get-tuple-element.30.later_than_ref), channel_id=1, source_target_pairs={{0,1},{1,0},{2,3},{3,2},{4,5},{5,4},{6,7},{7,6},{8,9},{9,8},{10,11... | collective-permute-start | bytes 147464 | tf_op jit(solution)/shard_map/ppermute | solution.py:324
  52.7 0.7 collective-permute-done.4.near_ref.refs_0_
  53.5 0.8 sum_and_copy.2
  54.3 11.2 %all-to-all-start.1 = ((bf16[8,88,128]{2,1,0:T(8,128)(2,1)}), bf16[8,88,128]{2,1,0:T(8,128)(2,1)S(1)}, u32[]{:S(2)}, u32[]{:S(2)}) async-start(bf16[8,88,128]{2,1,0:T(8,128)(2,1)} %sum_and_copy.2), calls=%async_computation.1 | async-start | bytes 360448 | tf_op jit(solution)/shard_map/all_to_all | solution.py:423
  66.1 1.9 %collective-permute-start.6 = (bf16[2,32,256]{2,1,0:T(8,128)(2,1)S(1)}, bf16[2,32,256]{2,1,0:T(8,128)(2,1)S(1)}, u32[]{:S(2)}, u32[]{:S(2)}) collective-permute-start(bf16[2,32,256]{2,1,0:T(8,128)(2,1)S(1)} %get-tuple-element.33), channel_id=1, source_target_pairs={{0,32},{32,0},{64,96},{96,64},{128,160},{160,128},{192,224},{224,1... | collective-permute-start | bytes 98312 | tf_op jit(solution)/shard_map/ppermute | solution.py:324
  68.1 0.7 collective-permute-start.7
  68.7 2.1 %collective-permute-done.6.near_ref.refs_0_ = bf16[2,32,256]{2,1,0:T(8,128)(2,1)S(1)} collective-permute-done((bf16[2,32,256]{2,1,0:T(8,128)(2,1)S(1)}, bf16[2,32,256]{2,1,0:T(8,128)(2,1)S(1)}, u32[]{:S(2)}, u32[]{:S(2)}) %collective-permute-start.6) | collective-permute-done | bytes 32800 | tf_op jit(solution)/shard_map/ppermute | solution.py:324
  70.8 8.7 %all-to-all-done.1.parts_ref = bf16[8,88,128]{2,1,0:T(8,128)(2,1)S(1)} async-done(((bf16[8,88,128]{2,1,0:T(8,128)(2,1)}), bf16[8,88,128]{2,1,0:T(8,128)(2,1)S(1)}, u32[]{:S(2)}, u32[]{:S(2)}) %all-to-all-start.1) | async-done | bytes 180256 | tf_op jit(solution)/shard_map/all_to_all | solution.py:423
  79.6 16.4 %all_to_all.15 = bf16[32,88,128]{2,1,0:T(8,128)(2,1)S(1)} all-to-all(bf16[32,88,128]{2,1,0:T(8,128)(2,1)S(1)} %sum_and_copy.3), channel_id=1, replica_groups=mesh['z_hi'=4,'x'=4,'z_mid'=2,'z_low'=2,'y'=4,'core'=2] {'x','z_low','y'}, dimensions={0} | all-to-all | bytes 1441792 | tf_op jit(solution)/shard_map/all_to_all | solution.py:442
  96.0 6.7 %collective-permute-start.9 = (bf16[2816,128]{1,0:T(8,128)(2,1)S(1)}, bf16[2816,128]{1,0:T(8,128)(2,1)S(1)}, u32[]{:S(2)}, u32[]{:S(2)}) collective-permute-start(bf16[2816,128]{1,0:T(8,128)(2,1)S(1)} %bitcast.13), channel_id=1, source_target_pairs={{0,1},{1,0},{2,3},{3,2},{4,5},{5,4},{6,7},{7,6},{8,9},{9,8},{10,11... | collective-permute-start | bytes 2162696 | tf_op jit(solution)/shard_map/ppermute | solution.py:324
  102.7 1.5 %final.1 = (bf16[8,32,256]{2,1,0:T(8,128)(2,1)}, bf16[8,32,256]{2,1,0:T(8,128)(2,1)}) custom-call(s32[2]{0:T(128)S(1)} %pad_add_fusion.side_ref, bf16[256,1024]{1,0:T(8,128)(2,1)S(1)} %get-tuple-element.27.hidden_ref, bf16[1024,256]{1,0:T(8,128)(2,1)S(1)} %copy-done.1, bf16[8,32,256]{2,1,0:T(8,128)(2,1)S(1)} %copy-done.3, bf16[256,256]{1,0:T(8,128)(2,1)S(1)} %bitcast.16, ...), custom_call_target="tpu_custom_call" | custom-call | flops 134217728 | bytes 1900552 | tf_op jit(solution)/shard_map/final/pallas_call | solution.py:39
  104.5 1.8 %place.1 = (bf16[1024,256]{1,0:T(8,128)(2,1)}, bf16[256,1024]{1,0:T(8,128)(2,1)}, bf16[768,256]{1,0:T(8,128)(2,1)}) custom-call(s32[2]{0:T(128)S(1)} %pad_add_fusion.side_ref, bf16[2816,128]{1,0:T(8,128)(2,1)S(1)} %bitcast.14, bf16[2816,128]{1,0:T(8,128)(2,1)S(1)} %collective-permute-done.9.other_ref), custom_call_target="tpu_custom_call" | custom-call | bytes 2883592 | tf_op jit(solution)/shard_map/place/pallas_call | solution.py:39
  (33 shorter events, 4.4 us)
Async XLA Ops:
  0.6 7.9 %copy-start = (s32[128,5,8]{0,2,1:T(8,128)S(1)}, s32[128,5,8]{0,2,1:T(8,128)}, u32[]{:S(2)}) copy-start(s32[128,5,8]{0,2,1:T(8,128)} %param.8) | copy-start | bytes 61444
  1.5 9.7 %collective-permute-start.1 = (bf16[2,32,256]{2,1,0:T(8,128)(2,1)S(1)}, bf16[2,32,256]{2,1,0:T(8,128)(2,1)S(1)}, u32[]{:S(2)}, u32[]{:S(2)}) collective-permute-start(bf16[2,32,256]{2,1,0:T(8,128)(2,1)S(1)} %get-tuple-element.41), channel_id=1, source_target_pairs={{32,64},{64,32},{96,128},{128,96},{160,192},{192,160},{224,256},{2... | collective-permute-start | bytes 98312 | tf_op jit(solution)/shard_map/ppermute | solution.py:324
  2.1 9.1 %collective-permute-start = (bf16[2,32,256]{2,1,0:T(8,128)(2,1)S(1)}, bf16[2,32,256]{2,1,0:T(8,128)(2,1)S(1)}, u32[]{:S(2)}, u32[]{:S(2)}) collective-permute-start(bf16[2,32,256]{2,1,0:T(8,128)(2,1)S(1)} %get-tuple-element.42), channel_id=1, source_target_pairs={{0,32},{32,0},{64,96},{96,64},{128,160},{160,128},{192,224},{224,1... | collective-permute-start | bytes 98312 | tf_op jit(solution)/shard_map/ppermute | solution.py:324
  9.7 0.9 copy-start.2
  11.7 11.8 %collective-permute-start.2 = (bf16[12,8,256]{2,1,0:T(8,128)(2,1)S(1)}, bf16[12,8,256]{2,1,0:T(8,128)(2,1)S(1)}, u32[]{:S(2)}, u32[]{:S(2)}) collective-permute-start(bf16[12,8,256]{2,1,0:T(8,128)(2,1)S(1)} %get-tuple-element.25), channel_id=1, source_target_pairs={{1,2},{2,1},{3,4},{4,3},{5,6},{6,5},{7,8},{8,7},{9,10},{10,9},{11,... | collective-permute-start | bytes 147464 | tf_op jit(solution)/shard_map/ppermute | solution.py:324
  16.1 7.7 %copy-start.1 = (bf16[1024,256]{1,0:T(8,128)(2,1)S(1)}, bf16[1024,256]{1,0:T(8,128)(2,1)}, u32[]{:S(2)}) copy-start(bf16[1024,256]{1,0:T(8,128)(2,1)} %out_ref.3) | copy-start | bytes 1572868
  16.1 7.7 %copy-start.3 = (bf16[8,32,256]{2,1,0:T(8,128)(2,1)S(1)}, bf16[8,32,256]{2,1,0:T(8,128)(2,1)}, u32[]{:S(2)}) copy-start(bf16[8,32,256]{2,1,0:T(8,128)(2,1)} %state_ref.5) | copy-start | bytes 393220
  16.1 7.7 %copy-start.4 = (bf16[3,256,256]{2,1,0:T(8,128)(2,1)S(1)}, bf16[3,256,256]{2,1,0:T(8,128)(2,1)}, u32[]{:S(2)}) copy-start(bf16[3,256,256]{2,1,0:T(8,128)(2,1)} %mix_ref.3) | copy-start | bytes 1179652
  16.1 7.7 %copy-start.5 = (bf16[8,32,256]{2,1,0:T(8,128)(2,1)S(1)}, bf16[8,32,256]{2,1,0:T(8,128)(2,1)}, u32[]{:S(2)}) copy-start(bf16[8,32,256]{2,1,0:T(8,128)(2,1)} %param.13) | copy-start | bytes 393220
  16.1 7.7 %copy-start.6 = (bf16[256,1024]{1,0:T(8,128)(2,1)S(1)}, bf16[256,1024]{1,0:T(8,128)(2,1)}, u32[]{:S(2)}) copy-start(bf16[256,1024]{1,0:T(8,128)(2,1)} %in_ref.1) | copy-start | bytes 1572868
  16.1 7.7 %collective-permute-start.3 = (bf16[12,8,256]{2,1,0:T(8,128)(2,1)S(1)}, bf16[12,8,256]{2,1,0:T(8,128)(2,1)S(1)}, u32[]{:S(2)}, u32[]{:S(2)}) collective-permute-start(bf16[12,8,256]{2,1,0:T(8,128)(2,1)S(1)} %get-tuple-element.26), channel_id=1, source_target_pairs={{0,1},{1,0},{2,3},{3,2},{4,5},{5,4},{6,7},{7,6},{8,9},{9,8},{10,11... | collective-permute-start | bytes 147464 | tf_op jit(solution)/shard_map/ppermute | solution.py:324
  26.5 4.6 %collective-permute-start.8 = (bf16[2816,128]{1,0:T(8,128)(2,1)S(1)}, bf16[2816,128]{1,0:T(8,128)(2,1)S(1)}, u32[]{:S(2)}, u32[]{:S(2)}) collective-permute-start(bf16[2816,128]{1,0:T(8,128)(2,1)S(1)} %slice_bitcast_fusion), channel_id=1, source_target_pairs={{0,1},{1,0},{2,3},{3,2},{4,5},{5,4},{6,7},{7,6},{8,9},{9,8},{10,11... | collective-permute-start | bytes 2162696 | tf_op jit(solution)/shard_map/ppermute | solution.py:324
  32.0 21.5 %all-to-all-start = ((bf16[32,88,128]{2,1,0:T(8,128)(2,1)}), bf16[32,88,128]{2,1,0:T(8,128)(2,1)S(1)}, u32[]{:S(2)}, u32[]{:S(2)}) async-start(bf16[32,88,128]{2,1,0:T(8,128)(2,1)} %bitcast.6), calls=%async_computation | async-start | bytes 1441792 | tf_op jit(solution)/shard_map/all_to_all | solution.py:419
  41.3 11.5 %collective-permute-start.5 = (bf16[12,8,256]{2,1,0:T(8,128)(2,1)S(1)}, bf16[12,8,256]{2,1,0:T(8,128)(2,1)S(1)}, u32[]{:S(2)}, u32[]{:S(2)}) collective-permute-start(bf16[12,8,256]{2,1,0:T(8,128)(2,1)S(1)} %get-tuple-element.31), channel_id=1, source_target_pairs={{1,2},{2,1},{3,4},{4,3},{5,6},{6,5},{7,8},{8,7},{9,10},{10,9},{11,... | collective-permute-start | bytes 147464 | tf_op jit(solution)/shard_map/ppermute | solution.py:324
  45.2 8.3 %collective-permute-start.4 = (bf16[12,8,256]{2,1,0:T(8,128)(2,1)S(1)}, bf16[12,8,256]{2,1,0:T(8,128)(2,1)S(1)}, u32[]{:S(2)}, u32[]{:S(2)}) collective-permute-start(bf16[12,8,256]{2,1,0:T(8,128)(2,1)S(1)} %get-tuple-element.30.later_than_ref), channel_id=1, source_target_pairs={{0,1},{1,0},{2,3},{3,2},{4,5},{5,4},{6,7},{7,6},{8,9},{9,8},{10,11... | collective-permute-start | bytes 147464 | tf_op jit(solution)/shard_map/ppermute | solution.py:324
  54.3 25.2 %all-to-all-start.1 = ((bf16[8,88,128]{2,1,0:T(8,128)(2,1)}), bf16[8,88,128]{2,1,0:T(8,128)(2,1)S(1)}, u32[]{:S(2)}, u32[]{:S(2)}) async-start(bf16[8,88,128]{2,1,0:T(8,128)(2,1)} %sum_and_copy.2), calls=%async_computation.1 | async-start | bytes 360448 | tf_op jit(solution)/shard_map/all_to_all | solution.py:423
  66.1 4.7 %collective-permute-start.6 = (bf16[2,32,256]{2,1,0:T(8,128)(2,1)S(1)}, bf16[2,32,256]{2,1,0:T(8,128)(2,1)S(1)}, u32[]{:S(2)}, u32[]{:S(2)}) collective-permute-start(bf16[2,32,256]{2,1,0:T(8,128)(2,1)S(1)} %get-tuple-element.33), channel_id=1, source_target_pairs={{0,32},{32,0},{64,96},{96,64},{128,160},{160,128},{192,224},{224,1... | collective-permute-start | bytes 98312 | tf_op jit(solution)/shard_map/ppermute | solution.py:324
  68.1 2.7 %collective-permute-start.7 = (bf16[2,32,256]{2,1,0:T(8,128)(2,1)S(1)}, bf16[2,32,256]{2,1,0:T(8,128)(2,1)S(1)}, u32[]{:S(2)}, u32[]{:S(2)}) collective-permute-start(bf16[2,32,256]{2,1,0:T(8,128)(2,1)S(1)} %get-tuple-element.34), channel_id=1, source_target_pairs={{32,64},{64,32},{96,128},{128,96},{160,192},{192,160},{224,256},{2... | collective-permute-start | bytes 98312 | tf_op jit(solution)/shard_map/ppermute | solution.py:324
  96.0 8.5 %collective-permute-start.9 = (bf16[2816,128]{1,0:T(8,128)(2,1)S(1)}, bf16[2816,128]{1,0:T(8,128)(2,1)S(1)}, u32[]{:S(2)}, u32[]{:S(2)}) collective-permute-start(bf16[2816,128]{1,0:T(8,128)(2,1)S(1)} %bitcast.13), channel_id=1, source_target_pairs={{0,1},{1,0},{2,3},{3,2},{4,5},{5,4},{6,7},{7,6},{8,9},{9,8},{10,11... | collective-permute-start | bytes 2162696 | tf_op jit(solution)/shard_map/ppermute | solution.py:324

commit v8 on v6

--- a/solution.py
+++ b/solution.py
@@ -180,27 +180,29 @@
         middle_ref[r] = line[WIDE : WIDE + cols]
 
 
-def rims_kernel(side_ref, middle_ref, near_ref, far_ref, to_far_ref, to_near_ref, core_ref):
-    rows, cols = core_ref.shape[:2]
-    lines = []
-    for r in range(rows + 2 * RAD):
-        left, right = by_side(side_ref[1] != 0, near_ref[r], far_ref[r])
-        line = middle_ref[r]
-        head, tail = line[:WIDE] + left, line[cols - WIDE :] + right
-        lines.append(jnp.concatenate([head, line[WIDE : cols - WIDE], tail], axis=0))
+def with_rims(side_ref, middle_ref, near_ref, far_ref, r):
+    left, right = by_side(side_ref[1] != 0, near_ref[r], far_ref[r])
+    line, cols = middle_ref[r], middle_ref.shape[1]
+    head, tail = line[:WIDE] + left, line[cols - WIDE :] + right
+    return jnp.concatenate([head, line[WIDE : cols - WIDE], tail], axis=0)
+
+
+def rims_kernel(side_ref, middle_ref, near_ref, far_ref, to_far_ref, to_near_ref):
+    rows = middle_ref.shape[0] - 2 * RAD
     for r in range(RAD):
-        above, below = lines[r], lines[rows + RAD + r]
+        above = with_rims(side_ref, middle_ref, near_ref, far_ref, r)
+        below = with_rims(side_ref, middle_ref, near_ref, far_ref, rows + RAD + r)
         to_near_ref[r], to_far_ref[r] = by_partner(side_ref[0] != 0, above, below)
-    for r in range(rows):
-        core_ref[r] = lines[RAD + r]
 
 
 def final_kernel(
-    side_ref, hidden_ref, out_ref, state_ref, cot_ref, core_ref, near_ref, far_ref, block_ref, field_ref
+    side_ref, hidden_ref, out_ref, state_ref, cot_ref, middle_ref, near_rim_ref, far_rim_ref,
+    near_ref, far_ref, block_ref, field_ref,
 ):
-    rows, cols = core_ref.shape[:2]
+    rows, cols = state_ref.shape[:2]
     branch = dot(hidden_ref[...], out_ref[...])
-    lines = [core_ref[r] for r in range(rows)]
+    rims = (side_ref, middle_ref, near_rim_ref, far_rim_ref)
+    lines = [with_rims(*rims, RAD + r) for r in range(rows)]
     for r in range(RAD):
         above, below = by_side(side_ref[0] != 0, near_ref[r], far_ref[r])
         lines[r] = lines[r] + above
@@ -421,11 +423,11 @@
     near_rim, far_rim = swap_both(to_near, to_far, LON, True)
     planes = sum_and_copy(shares, 1.0, far, near_rim, far_rim)
     planes = lax.all_to_all(planes, FAR, 0, 0)
-    to_far, to_near, inside = kernel_call(
+    to_far, to_near = kernel_call(
         rims_kernel,
         (sides, middle, near_rim, far_rim),
         [SMEM] + [VMEM] * 3,
-        [edge, edge, like(grid, f32)],
+        [edge, edge],
         name="rims",
     )
     near_edge, far_edge = swap_both(to_near, to_far, LAT, False)
@@ -433,8 +435,8 @@
     copies = sum_and_copy(planes, scale, near, near_edge, far_edge)
     block_out, grad_field = kernel_call(
         final_kernel,
-        (sides, hidden, weight_out, state_field, cot_flat, inside, near_edge, far_edge),
-        [SMEM] + [VMEM] * 7,
+        (sides, hidden, weight_out, state_field, cot_flat, middle, near_rim, far_rim, near_edge, far_edge),
+        [SMEM] + [VMEM] * 9,
         [like(grid, bf16), like(grid, bf16)],
         flops=2 * cells * channels * units,
         name="final",

time: 107 us -> 107 us (level)
  no operation moved by 1% of the time
where the time goes in v8:
time: 107 us; the launch traced here: 106 us
  starting transfers between devices  62 us (58%)
  blocking collectives  16.4 us (15%)
  waiting for transfers between devices  12.6 us (12%)
  Pallas kernels  11.3 us (11%)
  local copies, waits for them, and re-layouts  2 us (2%)
    ppermute x10, starting transfers between devices, swap(): return lax.ppermute(cells, axes, pairs)  41.6 us
    all_to_all x1, blocking collectives, local(): mine = lax.all_to_all(copies, NEAR, 0, 0).reshape(-1, LANES)  16.4 us
    pallas_call x11, Pallas kernels, kernel_call(): pl.pallas_call(body, out_shape=tuple(outs), in_specs=specs, out_specs=tup...  11.3 us
    all_to_all x1, starting transfers between devices, local(): planes = lax.all_to_all(planes, FAR, 0, 0)  11.2 us
    all_to_all x1, starting transfers between devices, local(): shares = lax.all_to_all(chip.reshape(near, -1, LANES), NEAR, 0, 0)  9.23 us
    all_to_all x1, waiting for transfers between devices, local(): planes = lax.all_to_all(planes, FAR, 0, 0)  8.74 us
    ppermute x10, waiting for transfers between devices, swap(): return lax.ppermute(cells, axes, pairs)  3.8 us
  transfers between devices with their start and end apart: 12, of which 8 were waited for; matrix products, arithmetic and copies ran while one was open for 1% of the time, Pallas kernels for 4%

profile of v8, /device:TPU:1, one launch (start us, length us, event | category | flops | bytes accessed | tf_op | source)
XLA Modules:
  0.0 106.3 jit_solution(4504946958166813223)
XLA Ops:
  0.7 0.8 constant_dynamic-slice_fusion
  2.1 6.4 %collective-permute-start = (bf16[2,32,256]{2,1,0:T(8,128)(2,1)S(1)}, bf16[2,32,256]{2,1,0:T(8,128)(2,1)S(1)}, u32[]{:S(2)}, u32[]{:S(2)}) collective-permute-start(bf16[2,32,256]{2,1,0:T(8,128)(2,1)S(1)} %get-tuple-element.40), channel_id=1, source_target_pairs={{0,32},{32,0},{64,96},{96,64},{128,160},{160,128},{192,224},{224,1... | collective-permute-start | bytes 98312 | tf_op jit(solution)/shard_map/ppermute | solution.py:326
  8.6 0.8 bitcast_convert_fusion
  9.7 0.9 copy-done.2
  11.7 4.3 %collective-permute-start.2 = (bf16[12,8,256]{2,1,0:T(8,128)(2,1)S(1)}, bf16[12,8,256]{2,1,0:T(8,128)(2,1)S(1)}, u32[]{:S(2)}, u32[]{:S(2)}) collective-permute-start(bf16[12,8,256]{2,1,0:T(8,128)(2,1)S(1)} %get-tuple-element.24), channel_id=1, source_target_pairs={{1,2},{2,1},{3,4},{4,3},{5,6},{6,5},{7,8},{8,7},{9,10},{10,9},{11,... | collective-permute-start | bytes 147464 | tf_op jit(solution)/shard_map/ppermute | solution.py:326
  16.1 6.8 %collective-permute-start.3 = (bf16[12,8,256]{2,1,0:T(8,128)(2,1)S(1)}, bf16[12,8,256]{2,1,0:T(8,128)(2,1)S(1)}, u32[]{:S(2)}, u32[]{:S(2)}) collective-permute-start(bf16[12,8,256]{2,1,0:T(8,128)(2,1)S(1)} %get-tuple-element.25), channel_id=1, source_target_pairs={{0,1},{1,0},{2,3},{3,2},{4,5},{5,4},{6,7},{7,6},{8,9},{9,8},{10,11... | collective-permute-start | bytes 147464 | tf_op jit(solution)/shard_map/ppermute | solution.py:326
  23.8 2.6 %main.1 = (bf16[2,2816,128]{2,1,0:T(8,128)(2,1)S(1)}, bf16[256,1024]{1,0:T(8,128)(2,1)S(1)}, bf16[256,256]{1,0:T(8,128)(2,1)S(1)}) custom-call(s32[2]{0:T(128)S(1)} %pad_add_fusion.side_ref, bf16[8,192,256]{2,1,0:T(8,128)(2,1)S(1)} %bands.1.bands_ref, bf16[2,32,256]{2,1,0:T(8,128)(2,1)S(1)} %collective-permute-done.lat_near_ref, ...), custom_call_target="tpu_custom_call" | custom-call | flops 671088640 | bytes 4751368 | tf_op jit(solution)/shard_map/main/pallas_call | solution.py:39
  26.5 2.8 %collective-permute-start.8 = (bf16[2816,128]{1,0:T(8,128)(2,1)S(1)}, bf16[2816,128]{1,0:T(8,128)(2,1)S(1)}, u32[]{:S(2)}, u32[]{:S(2)}) collective-permute-start(bf16[2816,128]{1,0:T(8,128)(2,1)S(1)} %slice_bitcast_fusion), channel_id=1, source_target_pairs={{0,1},{1,0},{2,3},{3,2},{4,5},{5,4},{6,7},{7,6},{8,9},{9,8},{10,11... | collective-permute-start | bytes 2162696 | tf_op jit(solution)/shard_map/ppermute | solution.py:326
  29.3 1.4 %adjoint.1 = (bf16[12,8,256]{2,1,0:T(8,128)(2,1)S(1)}, bf16[12,8,256]{2,1,0:T(8,128)(2,1)S(1)}, f32[12,32,256]{2,1,0:T(8,128)S(1)}) custom-call(s32[2]{0:T(128)S(1)} %pad_add_fusion.side_ref, bf16[256,256]{1,0:T(8,128)(2,1)S(1)} %get-tuple-element.27.grad_ref, bf16[3,256,256]{2,1,0:T(8,128)(2,1)S(1)} %copy-done.4, bf16[8,192,256]{2,1,0:T(8,128)(2,1)S(1)} %bands.1.bands_ref), custom_call_target="tpu_custom_call" | custom-call | flops 268435456 | bytes 1802248 | tf_op jit(solution)/shard_map/adjoint/pallas_call | solution.py:39
  31.1 0.9 add.36
  32.0 9.2 %all-to-all-start = ((bf16[32,88,128]{2,1,0:T(8,128)(2,1)}), bf16[32,88,128]{2,1,0:T(8,128)(2,1)S(1)}, u32[]{:S(2)}, u32[]{:S(2)}) async-start(bf16[32,88,128]{2,1,0:T(8,128)(2,1)} %bitcast.6), calls=%async_computation | async-start | bytes 1441792 | tf_op jit(solution)/shard_map/all_to_all | solution.py:421
  41.3 3.9 %collective-permute-start.5 = (bf16[12,8,256]{2,1,0:T(8,128)(2,1)S(1)}, bf16[12,8,256]{2,1,0:T(8,128)(2,1)S(1)}, u32[]{:S(2)}, u32[]{:S(2)}) collective-permute-start(bf16[12,8,256]{2,1,0:T(8,128)(2,1)S(1)} %get-tuple-element.30), channel_id=1, source_target_pairs={{1,2},{2,1},{3,4},{4,3},{5,6},{6,5},{7,8},{8,7},{9,10},{10,9},{11,... | collective-permute-start | bytes 147464 | tf_op jit(solution)/shard_map/ppermute | solution.py:326
  45.2 7.4 %collective-permute-start.4 = (bf16[12,8,256]{2,1,0:T(8,128)(2,1)S(1)}, bf16[12,8,256]{2,1,0:T(8,128)(2,1)S(1)}, u32[]{:S(2)}, u32[]{:S(2)}) collective-permute-start(bf16[12,8,256]{2,1,0:T(8,128)(2,1)S(1)} %get-tuple-element.29.later_than_ref), channel_id=1, source_target_pairs={{0,1},{1,0},{2,3},{3,2},{4,5},{5,4},{6,7},{7,6},{8,9},{9,8},{10,11... | collective-permute-start | bytes 147464 | tf_op jit(solution)/shard_map/ppermute | solution.py:326
  52.7 0.7 collective-permute-done.4.near_ref.near_rim_ref.refs_0_
  53.5 0.8 sum_and_copy.2
  54.3 11.2 %all-to-all-start.1 = ((bf16[8,88,128]{2,1,0:T(8,128)(2,1)}), bf16[8,88,128]{2,1,0:T(8,128)(2,1)S(1)}, u32[]{:S(2)}, u32[]{:S(2)}) async-start(bf16[8,88,128]{2,1,0:T(8,128)(2,1)} %sum_and_copy.2), calls=%async_computation.1 | async-start | bytes 360448 | tf_op jit(solution)/shard_map/all_to_all | solution.py:425
  66.1 1.9 %collective-permute-start.6 = (bf16[2,32,256]{2,1,0:T(8,128)(2,1)S(1)}, bf16[2,32,256]{2,1,0:T(8,128)(2,1)S(1)}, u32[]{:S(2)}, u32[]{:S(2)}) collective-permute-start(bf16[2,32,256]{2,1,0:T(8,128)(2,1)S(1)} %get-tuple-element.31), channel_id=1, source_target_pairs={{0,32},{32,0},{64,96},{96,64},{128,160},{160,128},{192,224},{224,1... | collective-permute-start | bytes 98312 | tf_op jit(solution)/shard_map/ppermute | solution.py:326
  68.0 0.7 collective-permute-start.7
  68.7 2.1 %collective-permute-done.6.near_ref.refs_0_ = bf16[2,32,256]{2,1,0:T(8,128)(2,1)S(1)} collective-permute-done((bf16[2,32,256]{2,1,0:T(8,128)(2,1)S(1)}, bf16[2,32,256]{2,1,0:T(8,128)(2,1)S(1)}, u32[]{:S(2)}, u32[]{:S(2)}) %collective-permute-start.6) | collective-permute-done | bytes 32800 | tf_op jit(solution)/shard_map/ppermute | solution.py:326
  70.8 8.7 %all-to-all-done.1.parts_ref = bf16[8,88,128]{2,1,0:T(8,128)(2,1)S(1)} async-done(((bf16[8,88,128]{2,1,0:T(8,128)(2,1)}), bf16[8,88,128]{2,1,0:T(8,128)(2,1)S(1)}, u32[]{:S(2)}, u32[]{:S(2)}) %all-to-all-start.1) | async-done | bytes 180256 | tf_op jit(solution)/shard_map/all_to_all | solution.py:425
  79.6 16.4 %all_to_all.15 = bf16[32,88,128]{2,1,0:T(8,128)(2,1)S(1)} all-to-all(bf16[32,88,128]{2,1,0:T(8,128)(2,1)S(1)} %sum_and_copy.3), channel_id=1, replica_groups=mesh['z_hi'=4,'x'=4,'z_mid'=2,'z_low'=2,'y'=4,'core'=2] {'x','z_low','y'}, dimensions={0} | all-to-all | bytes 1441792 | tf_op jit(solution)/shard_map/all_to_all | solution.py:444
  96.0 6.7 %collective-permute-start.9 = (bf16[2816,128]{1,0:T(8,128)(2,1)S(1)}, bf16[2816,128]{1,0:T(8,128)(2,1)S(1)}, u32[]{:S(2)}, u32[]{:S(2)}) collective-permute-start(bf16[2816,128]{1,0:T(8,128)(2,1)S(1)} %bitcast.13), channel_id=1, source_target_pairs={{0,1},{1,0},{2,3},{3,2},{4,5},{5,4},{6,7},{7,6},{8,9},{9,8},{10,11... | collective-permute-start | bytes 2162696 | tf_op jit(solution)/shard_map/ppermute | solution.py:326
  102.7 1.6 %final.1 = (bf16[8,32,256]{2,1,0:T(8,128)(2,1)}, bf16[8,32,256]{2,1,0:T(8,128)(2,1)}) custom-call(s32[2]{0:T(128)S(1)} %pad_add_fusion.side_ref, bf16[256,1024]{1,0:T(8,128)(2,1)S(1)} %get-tuple-element.26.hidden_ref, bf16[1024,256]{1,0:T(8,128)(2,1)S(1)} %copy-done.1, bf16[8,32,256]{2,1,0:T(8,128)(2,1)S(1)} %copy-done.3, bf16[256,256]{1,0:T(8,128)(2,1)S(1)} %bitcast.16, ...), custom_call_target="tpu_custom_call" | custom-call | flops 134217728 | bytes 2129928 | tf_op jit(solution)/shard_map/final/pallas_call | solution.py:39
  104.5 1.8 %place.1 = (bf16[1024,256]{1,0:T(8,128)(2,1)}, bf16[256,1024]{1,0:T(8,128)(2,1)}, bf16[768,256]{1,0:T(8,128)(2,1)}) custom-call(s32[2]{0:T(128)S(1)} %pad_add_fusion.side_ref, bf16[2816,128]{1,0:T(8,128)(2,1)S(1)} %bitcast.14, bf16[2816,128]{1,0:T(8,128)(2,1)S(1)} %collective-permute-done.9.other_ref), custom_call_target="tpu_custom_call" | custom-call | bytes 2883592 | tf_op jit(solution)/shard_map/place/pallas_call | solution.py:39
  (33 shorter events, 4.4 us)
Async XLA Ops:
  0.6 7.9 %copy-start = (s32[128,5,8]{0,2,1:T(8,128)S(1)}, s32[128,5,8]{0,2,1:T(8,128)}, u32[]{:S(2)}) copy-start(s32[128,5,8]{0,2,1:T(8,128)} %param.8) | copy-start | bytes 61444
  1.5 9.7 %collective-permute-start.1 = (bf16[2,32,256]{2,1,0:T(8,128)(2,1)S(1)}, bf16[2,32,256]{2,1,0:T(8,128)(2,1)S(1)}, u32[]{:S(2)}, u32[]{:S(2)}) collective-permute-start(bf16[2,32,256]{2,1,0:T(8,128)(2,1)S(1)} %get-tuple-element.39), channel_id=1, source_target_pairs={{32,64},{64,32},{96,128},{128,96},{160,192},{192,160},{224,256},{2... | collective-permute-start | bytes 98312 | tf_op jit(solution)/shard_map/ppermute | solution.py:326
  2.1 9.1 %collective-permute-start = (bf16[2,32,256]{2,1,0:T(8,128)(2,1)S(1)}, bf16[2,32,256]{2,1,0:T(8,128)(2,1)S(1)}, u32[]{:S(2)}, u32[]{:S(2)}) collective-permute-start(bf16[2,32,256]{2,1,0:T(8,128)(2,1)S(1)} %get-tuple-element.40), channel_id=1, source_target_pairs={{0,32},{32,0},{64,96},{96,64},{128,160},{160,128},{192,224},{224,1... | collective-permute-start | bytes 98312 | tf_op jit(solution)/shard_map/ppermute | solution.py:326
  9.7 0.9 copy-start.2
  11.7 11.8 %collective-permute-start.2 = (bf16[12,8,256]{2,1,0:T(8,128)(2,1)S(1)}, bf16[12,8,256]{2,1,0:T(8,128)(2,1)S(1)}, u32[]{:S(2)}, u32[]{:S(2)}) collective-permute-start(bf16[12,8,256]{2,1,0:T(8,128)(2,1)S(1)} %get-tuple-element.24), channel_id=1, source_target_pairs={{1,2},{2,1},{3,4},{4,3},{5,6},{6,5},{7,8},{8,7},{9,10},{10,9},{11,... | collective-permute-start | bytes 147464 | tf_op jit(solution)/shard_map/ppermute | solution.py:326
  16.1 7.7 %copy-start.1 = (bf16[1024,256]{1,0:T(8,128)(2,1)S(1)}, bf16[1024,256]{1,0:T(8,128)(2,1)}, u32[]{:S(2)}) copy-start(bf16[1024,256]{1,0:T(8,128)(2,1)} %out_ref.3) | copy-start | bytes 1572868
  16.1 7.7 %copy-start.3 = (bf16[8,32,256]{2,1,0:T(8,128)(2,1)S(1)}, bf16[8,32,256]{2,1,0:T(8,128)(2,1)}, u32[]{:S(2)}) copy-start(bf16[8,32,256]{2,1,0:T(8,128)(2,1)} %state_ref.5) | copy-start | bytes 393220
  16.1 7.7 %copy-start.4 = (bf16[3,256,256]{2,1,0:T(8,128)(2,1)S(1)}, bf16[3,256,256]{2,1,0:T(8,128)(2,1)}, u32[]{:S(2)}) copy-start(bf16[3,256,256]{2,1,0:T(8,128)(2,1)} %mix_ref.3) | copy-start | bytes 1179652
  16.1 7.7 %copy-start.5 = (bf16[8,32,256]{2,1,0:T(8,128)(2,1)S(1)}, bf16[8,32,256]{2,1,0:T(8,128)(2,1)}, u32[]{:S(2)}) copy-start(bf16[8,32,256]{2,1,0:T(8,128)(2,1)} %param.13) | copy-start | bytes 393220
  16.1 7.7 %copy-start.6 = (bf16[256,1024]{1,0:T(8,128)(2,1)S(1)}, bf16[256,1024]{1,0:T(8,128)(2,1)}, u32[]{:S(2)}) copy-start(bf16[256,1024]{1,0:T(8,128)(2,1)} %in_ref.1) | copy-start | bytes 1572868
  16.1 7.7 %collective-permute-start.3 = (bf16[12,8,256]{2,1,0:T(8,128)(2,1)S(1)}, bf16[12,8,256]{2,1,0:T(8,128)(2,1)S(1)}, u32[]{:S(2)}, u32[]{:S(2)}) collective-permute-start(bf16[12,8,256]{2,1,0:T(8,128)(2,1)S(1)} %get-tuple-element.25), channel_id=1, source_target_pairs={{0,1},{1,0},{2,3},{3,2},{4,5},{5,4},{6,7},{7,6},{8,9},{9,8},{10,11... | collective-permute-start | bytes 147464 | tf_op jit(solution)/shard_map/ppermute | solution.py:326
  26.5 4.6 %collective-permute-start.8 = (bf16[2816,128]{1,0:T(8,128)(2,1)S(1)}, bf16[2816,128]{1,0:T(8,128)(2,1)S(1)}, u32[]{:S(2)}, u32[]{:S(2)}) collective-permute-start(bf16[2816,128]{1,0:T(8,128)(2,1)S(1)} %slice_bitcast_fusion), channel_id=1, source_target_pairs={{0,1},{1,0},{2,3},{3,2},{4,5},{5,4},{6,7},{7,6},{8,9},{9,8},{10,11... | collective-permute-start | bytes 2162696 | tf_op jit(solution)/shard_map/ppermute | solution.py:326
  32.0 21.5 %all-to-all-start = ((bf16[32,88,128]{2,1,0:T(8,128)(2,1)}), bf16[32,88,128]{2,1,0:T(8,128)(2,1)S(1)}, u32[]{:S(2)}, u32[]{:S(2)}) async-start(bf16[32,88,128]{2,1,0:T(8,128)(2,1)} %bitcast.6), calls=%async_computation | async-start | bytes 1441792 | tf_op jit(solution)/shard_map/all_to_all | solution.py:421
  41.3 11.5 %collective-permute-start.5 = (bf16[12,8,256]{2,1,0:T(8,128)(2,1)S(1)}, bf16[12,8,256]{2,1,0:T(8,128)(2,1)S(1)}, u32[]{:S(2)}, u32[]{:S(2)}) collective-permute-start(bf16[12,8,256]{2,1,0:T(8,128)(2,1)S(1)} %get-tuple-element.30), channel_id=1, source_target_pairs={{1,2},{2,1},{3,4},{4,3},{5,6},{6,5},{7,8},{8,7},{9,10},{10,9},{11,... | collective-permute-start | bytes 147464 | tf_op jit(solution)/shard_map/ppermute | solution.py:326
  45.2 8.3 %collective-permute-start.4 = (bf16[12,8,256]{2,1,0:T(8,128)(2,1)S(1)}, bf16[12,8,256]{2,1,0:T(8,128)(2,1)S(1)}, u32[]{:S(2)}, u32[]{:S(2)}) collective-permute-start(bf16[12,8,256]{2,1,0:T(8,128)(2,1)S(1)} %get-tuple-element.29.later_than_ref), channel_id=1, source_target_pairs={{0,1},{1,0},{2,3},{3,2},{4,5},{5,4},{6,7},{7,6},{8,9},{9,8},{10,11... | collective-permute-start | bytes 147464 | tf_op jit(solution)/shard_map/ppermute | solution.py:326
  54.3 25.2 %all-to-all-start.1 = ((bf16[8,88,128]{2,1,0:T(8,128)(2,1)}), bf16[8,88,128]{2,1,0:T(8,128)(2,1)S(1)}, u32[]{:S(2)}, u32[]{:S(2)}) async-start(bf16[8,88,128]{2,1,0:T(8,128)(2,1)} %sum_and_copy.2), calls=%async_computation.1 | async-start | bytes 360448 | tf_op jit(solution)/shard_map/all_to_all | solution.py:425
  66.1 4.7 %collective-permute-start.6 = (bf16[2,32,256]{2,1,0:T(8,128)(2,1)S(1)}, bf16[2,32,256]{2,1,0:T(8,128)(2,1)S(1)}, u32[]{:S(2)}, u32[]{:S(2)}) collective-permute-start(bf16[2,32,256]{2,1,0:T(8,128)(2,1)S(1)} %get-tuple-element.31), channel_id=1, source_target_pairs={{0,32},{32,0},{64,96},{96,64},{128,160},{160,128},{192,224},{224,1... | collective-permute-start | bytes 98312 | tf_op jit(solution)/shard_map/ppermute | solution.py:326
  68.0 2.7 %collective-permute-start.7 = (bf16[2,32,256]{2,1,0:T(8,128)(2,1)S(1)}, bf16[2,32,256]{2,1,0:T(8,128)(2,1)S(1)}, u32[]{:S(2)}, u32[]{:S(2)}) collective-permute-start(bf16[2,32,256]{2,1,0:T(8,128)(2,1)S(1)} %get-tuple-element.32), channel_id=1, source_target_pairs={{32,64},{64,32},{96,128},{128,96},{160,192},{192,160},{224,256},{2... | collective-permute-start | bytes 98312 | tf_op jit(solution)/shard_map/ppermute | solution.py:326
  96.0 8.5 %collective-permute-start.9 = (bf16[2816,128]{1,0:T(8,128)(2,1)S(1)}, bf16[2816,128]{1,0:T(8,128)(2,1)S(1)}, u32[]{:S(2)}, u32[]{:S(2)}) collective-permute-start(bf16[2816,128]{1,0:T(8,128)(2,1)S(1)} %bitcast.13), channel_id=1, source_target_pairs={{0,1},{1,0},{2,3},{3,2},{4,5},{5,4},{6,7},{7,6},{8,9},{9,8},{10,11... | collective-permute-start | bytes 2162696 | tf_op jit(solution)/shard_map/ppermute | solution.py:326
